TPU v7x, 32 devices: a whole 2x2x4 slice. The times are simulated.
32 devices in a mesh: batch: 8 (over y, x, core), ctx: 4 (over z).
Axes of the slice: x: 2, y: 2, z: 4, core: 2. Of those that a mesh axis runs over, the one named last changes fastest.
Arguments:
- tokens: bfloat16 [16, 1024, 1600], P('batch', 'ctx'), may hold values from -8 to 8
- teacher: bfloat16 [16, 1024, 1600], P('batch', 'ctx'), may hold values from -6 to 6
- cotangent: bfloat16 [16, 1024, 1600], P('batch', 'ctx'), may hold values from -6 to 6
- valid: int32 [16, 1024], P('batch', 'ctx'), may hold values from 0 to 1, as said below
- w_query: bfloat16 [1600, 1600], P('batch', 'ctx'), may hold values from -0.15625 to 0.15625
- w_key: bfloat16 [1600, 320], P('batch', 'ctx'), may hold values from -0.15625 to 0.15625
- w_value: bfloat16 [1600, 640], P('batch', 'ctx'), may hold values from -0.15625 to 0.15625
- w_mixer: bfloat16 [1600, 6400], P('batch', 'ctx'), may hold values from -0.15625 to 0.15625
- w_output: bfloat16 [3200, 1600], P('batch', 'ctx'), may hold values from -0.109375 to 0.109375
- w_gate: bfloat16 [1600, 5504], P('batch', 'ctx'), may hold values from -0.15625 to 0.15625
- w_up: bfloat16 [1600, 5504], P('batch', 'ctx'), may hold values from -0.15625 to 0.15625
- w_down: bfloat16 [5504, 1600], P('batch', 'ctx'), may hold values from -0.15625 to 0.15625
- w_select: bfloat16 [3200, 132], P('batch'), may hold values from -0.109375 to 0.109375
- w_step: bfloat16 [100, 3200], P(None, 'batch'), may hold values from -0.625 to 0.625
- log_decay: bfloat16 [16, 3200], P(None, 'batch'), may hold values from -6 to 1
- conv_taps: bfloat16 [4, 3200], P(None, 'batch'), may hold values from -3 to 3
- conv_bias: bfloat16 [3200], P('batch'), may hold values from -2 to 2
- step_bias: bfloat16 [3200], P('batch'), may hold values from -6 to -1
- skip_gain: bfloat16 [3200], P('batch'), may hold values from 0.29882812 to 1.1953125
- beta_attn: bfloat16 [3200], P('batch'), may hold values from 0.5 to 2
- beta_ssm: bfloat16 [3200], P('batch'), may hold values from 0.5 to 2
- gain_first: bfloat16 [1600], P('batch'), may hold values from 0.5 to 1.5
- gain_second: bfloat16 [1600], P('batch'), may hold values from 0.5 to 1.5
Outputs:
- output: bfloat16 [16, 1024, 1600], P('batch', 'ctx')
- distill_loss: float32 [], replicated
- tokens_grad: bfloat16 [16, 1024, 1600], P('batch', 'ctx')
- query_grad: float32 [1600, 1600], P('batch', 'ctx')
- key_grad: float32 [1600, 320], P('batch', 'ctx')
- value_grad: float32 [1600, 640], P('batch', 'ctx')
- mixer_grad: float32 [1600, 6400], P('batch', 'ctx')
- output_grad: float32 [3200, 1600], P('batch', 'ctx')
- gate_grad: float32 [1600, 5504], P('batch', 'ctx')
- up_grad: float32 [1600, 5504], P('batch', 'ctx')
- down_grad: float32 [5504, 1600], P('batch', 'ctx')
- select_grad: float32 [3200, 132], P('batch')
- step_grad: float32 [100, 3200], P(None, 'batch')
- decay_grad: float32 [16, 3200], P(None, 'batch')
- taps_grad: float32 [4, 3200], P(None, 'batch')
- conv_bias_grad: float32 [3200], P('batch')
- step_bias_grad: float32 [3200], P('batch')
- skip_grad: float32 [3200], P('batch')
- beta_attn_grad: float32 [3200], P('batch')
- beta_ssm_grad: float32 [3200], P('batch')
- gain_first_grad: float32 [1600], P('batch')
- gain_second_grad: float32 [1600], P('batch')
Inputs may be any that keep to these rules, and one draw needn't show every extreme that they name: `valid`: every sequence's first position is 1.
All inputs are finite; a program needn't handle non-finite values.
Results may differ from a plain program's by a relative error of at most 0.017.
Values may be sent and summed in bfloat16 or wider, within the bound.
A program may use at most 576 MiB of HBM per device.

v0:
```python
import math

import jax
import jax.numpy as jnp
from jax import lax
from jax.sharding import PartitionSpec as P

D = 1600
HEADS = 25
KV = 5
HD = 64
INNER = 3200
STATE = 16
CONV = 4
RANK = 100
WINDOW = 1024
MICRO = 2


EPS = 1e-05
F32 = jnp.float32
BF16 = jnp.bfloat16


def shifted(value, axis, steps):
    count = lax.axis_size(axis)
    initial, last = (max(0, -steps), min(count, count - steps))
    return lax.ppermute(value, axis, [(source, source + steps) for source in range(initial, last)])


def prefix(x, axis, combine, identity, reverse):
    size, mine = (lax.axis_size(axis), lax.axis_index(axis))
    everything = jax.tree.map(
        lambda part, kind: lax.all_gather(part.astype(kind), axis), x, (jnp.bfloat16, jnp.bfloat16)
    )
    start = jax.tree.map(
        lambda part, zero: jnp.broadcast_to(jnp.asarray(zero, part.dtype), part.shape), x, identity
    )

    def hop(k, before):
        at = size - 1 - k if reverse else k
        reached = at > mine if reverse else at < mine
        new = combine(
            before, jax.tree.map(lambda part, own: part[at].astype(own.dtype), everything, x)
        )
        return jax.tree.map(lambda a, b: jnp.where(reached, a, b), new, before)

    return lax.fori_loop(0, size, hop, start)


def as_sent(x):
    return jax.tree.map(lambda a: a.astype(jnp.bfloat16) if a.dtype == jnp.float32 else a, x)


def rms_scale(value):
    return lax.rsqrt(jnp.mean(value * value, axis=-1, keepdims=True) + EPS)


def norm_back(value, scale, upstream):
    return scale * upstream - value * scale**3 * jnp.mean(upstream * value, axis=-1, keepdims=True)


def silu_pair(value):
    sigma = jax.nn.sigmoid(value)
    return (value * sigma, sigma * (1.0 + value * (1.0 - sigma)))


def matmul(left, right):
    return jnp.dot(left, right, preferred_element_type=F32)


def matmul_back(left, right):
    return lax.dot_general(left, right, (((1,), (1,)), ((), ())), preferred_element_type=F32)


def outer_sum(left, right):
    return lax.dot_general(left, right, (((0,), (0,)), ((), ())), preferred_element_type=F32)


def chain(earlier, later):
    return (earlier[0] * later[0], later[0] * earlier[1] + later[1])


def cut_blocks(value, block):
    seqs, length, last = value.shape
    return jnp.moveaxis(value.reshape(seqs, length // block, block, last), 1, 0)


def join_blocks(value):
    turns, seqs, block, last = value.shape
    return jnp.moveaxis(value, 0, 1).reshape(seqs, turns * block, last)


def ssm_forward(start, steps, drive, b_coef, c_coef, decay, with_out):
    block = math.gcd(steps.shape[1], 16)

    def advance(state, item):
        step_blk, drive_blk, b_blk, c_blk = item
        first = state
        outs = []
        for place in range(block):
            factor = jnp.exp(step_blk[:, place, None, :] * decay)
            state = (
                factor * state
                + (step_blk[:, place] * drive_blk[:, place])[:, None, :] * b_blk[:, place, :, None]
            )
            if with_out:
                outs.append(jnp.sum(c_blk[:, place, :, None] * state, axis=1))
        if with_out:
            return (state, (jnp.stack(outs, axis=1), first))
        return (state, None)

    items = (
        cut_blocks(steps, block),
        cut_blocks(drive, block),
        cut_blocks(b_coef, block),
        cut_blocks(c_coef, block),
    )
    final, kept = lax.scan(advance, start, items)
    if with_out:
        return (final, join_blocks(kept[0]), kept[1])
    return (final, None, None)


def ssm_backward(arrive, starts, steps, drive, b_coef, c_coef, grad_out, decay, full):
    block = math.gcd(steps.shape[1], 16)

    def retreat(carry, item):
        adjoint, grad_decay = carry
        step_blk, drive_blk, b_blk, c_blk, out_blk = item[:5]
        factors = [jnp.exp(step_blk[:, place, None, :] * decay) for place in range(block)]
        states = []
        if full:
            states = [item[5]]
            for place in range(block):
                states.append(
                    factors[place] * states[-1]
                    + (step_blk[:, place] * drive_blk[:, place])[:, None, :]
                    * b_blk[:, place, :, None]
                )
        drive_grads = [None] * block
        step_grads = [None] * block
        b_grads = [None] * block
        c_grads = [None] * block
        for place in reversed(range(block)):
            current = c_blk[:, place, :, None] * out_blk[:, place, None, :] + adjoint
            if full:
                along = current * states[place] * factors[place]
                weighted = jnp.sum(current * b_blk[:, place, :, None], axis=1)
                step_grads[place] = jnp.sum(along * decay, axis=1) + weighted * drive_blk[:, place]
                drive_grads[place] = weighted * step_blk[:, place]
                b_grads[place] = jnp.sum(
                    current * (step_blk[:, place] * drive_blk[:, place])[:, None, :], axis=2
                )
                c_grads[place] = jnp.sum(out_blk[:, place, None, :] * states[place + 1], axis=2)
                grad_decay = grad_decay + jnp.sum(along * step_blk[:, place, None, :], axis=0)
            adjoint = factors[place] * current
        if full:
            return (
                (adjoint, grad_decay),
                (
                    jnp.stack(drive_grads, axis=1),
                    jnp.stack(step_grads, axis=1),
                    jnp.stack(b_grads, axis=1),
                    jnp.stack(c_grads, axis=1),
                ),
            )
        return ((adjoint, grad_decay), None)

    items = (
        cut_blocks(steps, block),
        cut_blocks(drive, block),
        cut_blocks(b_coef, block),
        cut_blocks(c_coef, block),
        cut_blocks(grad_out, block),
    )
    if full:
        items = items + (starts,)
    (adjoint, grad_decay), kept = lax.scan(
        retreat, (arrive, jnp.zeros(decay.shape, F32)), items, reverse=True
    )
    if full:
        return (adjoint, grad_decay, tuple((join_blocks(part) for part in kept)))
    return (adjoint, grad_decay, None)


def per_device(
    tokens,
    teacher,
    cotangent,
    valid,
    w_query,
    w_key,
    w_value,
    w_mixer,
    w_output,
    w_gate,
    w_up,
    w_down,
    w_select,
    w_step,
    log_decay,
    conv_taps,
    conv_bias,
    step_bias,
    skip_gain,
    beta_attn,
    beta_ssm,
    gain_first,
    gain_second,
):
    seq_grp, span, width = tokens.shape
    length = span * lax.axis_size("ctx")
    per_micro = seq_grp // MICRO
    rows = per_micro * span
    group = HEADS // KV
    vhead = INNER // HEADS
    scale = 1.0 / math.sqrt(HD)
    all_tokens = seq_grp * lax.axis_size("batch") * length
    q_places = lax.axis_index("ctx") * span + jnp.arange(span)
    k_places = jnp.arange(length)
    allowed = (k_places[None, :] <= q_places[:, None]) & (
        k_places[None, :] > q_places[:, None] - WINDOW
    )

    def scores_of(q_heads, k_heads):
        raw = jnp.einsum("scgqd,slgd->sgqcl", q_heads, k_heads, preferred_element_type=F32) * scale
        return jnp.where(allowed, raw, -1e30)

    def fetch():
        c_query, c_key, c_value, c_mixer, c_output, c_gate, c_up, c_down = (
            lax.all_gather(w_query, "ctx", axis=1, tiled=True),
            lax.all_gather(w_key, "ctx", axis=1, tiled=True),
            lax.all_gather(w_value, "ctx", axis=1, tiled=True),
            lax.all_gather(w_mixer, "ctx", axis=1, tiled=True),
            lax.all_gather(w_output, "ctx", axis=1, tiled=True),
            lax.all_gather(w_gate, "ctx", axis=1, tiled=True),
            lax.all_gather(w_up, "ctx", axis=1, tiled=True),
            lax.all_gather(w_down, "ctx", axis=1, tiled=True),
        )
        return (
            lax.all_gather(c_query, "batch", axis=0, tiled=True),
            lax.all_gather(c_key, "batch", axis=0, tiled=True),
            lax.all_gather(c_value, "batch", axis=0, tiled=True),
            lax.all_gather(c_mixer, "batch", axis=0, tiled=True),
            lax.all_gather(c_output, "batch", axis=0, tiled=True),
            lax.all_gather(c_gate, "batch", axis=0, tiled=True),
            lax.all_gather(c_up, "batch", axis=0, tiled=True),
            lax.all_gather(c_down, "batch", axis=0, tiled=True),
            lax.all_gather(w_select, "batch", axis=0, tiled=True),
            lax.all_gather(w_step, "batch", axis=1, tiled=True),
            lax.all_gather(log_decay, "batch", axis=1, tiled=True),
            lax.all_gather(conv_taps, "batch", axis=1, tiled=True),
            lax.all_gather(conv_bias, "batch", axis=0, tiled=True),
            lax.all_gather(step_bias, "batch", axis=0, tiled=True),
            lax.all_gather(skip_gain, "batch", axis=0, tiled=True),
            lax.all_gather(beta_attn, "batch", axis=0, tiled=True),
            lax.all_gather(beta_ssm, "batch", axis=0, tiled=True),
            lax.all_gather(gain_first, "batch", axis=0, tiled=True),
            lax.all_gather(gain_second, "batch", axis=0, tiled=True),
        )

    count = lax.psum(jnp.sum(valid.astype(F32)), ("batch", "ctx"))
    factor = all_tokens / count
    outputs = []
    input_grads = []
    loss_local = jnp.zeros((), F32)
    result = None
    for micro in range(MICRO):
        first_row = micro * per_micro
        last_row = first_row + per_micro
        full = fetch()
        (
            f_query,
            f_key,
            f_value,
            f_mixer,
            f_output,
            f_gate,
            f_up,
            f_down,
            f_select,
            f_step,
            f_decay,
            f_taps,
            f_conv_bias,
            f_step_bias,
            f_skip,
            f_beta_attn,
            f_beta_ssm,
            f_gain_first,
            f_gain_second,
        ) = full
        decay = -jnp.exp(f_decay.astype(F32))
        taps = f_taps.astype(F32)
        skip = f_skip.astype(F32)
        beta_a = f_beta_attn.astype(F32)
        beta_s = f_beta_ssm.astype(F32)
        gain_one = f_gain_first.astype(F32)
        gain_two = f_gain_second.astype(F32)
        x_flat = tokens[first_row:last_row].reshape(rows, D).astype(F32)
        scale1 = rms_scale(x_flat)
        normed1 = (x_flat * scale1 * gain_one).astype(BF16)
        queries = matmul(normed1, f_query).astype(BF16)
        keys_own = matmul(normed1, f_key).astype(BF16)
        values_own = matmul(normed1, f_value).astype(BF16)
        mixer = matmul(normed1, f_mixer)
        conv_in = mixer[:, :INNER].astype(BF16).reshape(per_micro, span, INNER)
        gate_z = mixer[:, INNER:].reshape(per_micro, span, INNER)
        keys_all, values_all = (
            lax.all_gather(keys_own.reshape(per_micro, span, KV * HD), "ctx", axis=1, tiled=True),
            lax.all_gather(
                values_own.reshape(per_micro, span, KV * vhead), "ctx", axis=1, tiled=True
            ),
        )
        q_heads = queries.reshape(per_micro, span, KV, group, HD)
        k_heads = keys_all.reshape(per_micro, length, KV, HD)
        v_heads = values_all.reshape(per_micro, length, KV, vhead)
        scores = scores_of(q_heads, k_heads)
        peak = jnp.max(scores, axis=-1, keepdims=True)
        expo = jnp.exp(scores - peak)
        total = jnp.sum(expo, axis=-1, keepdims=True)
        log_total = peak + jnp.log(total)
        attn = jnp.einsum(
            "sgqcl,slgv->scgqv", (expo / total).astype(BF16), v_heads, preferred_element_type=F32
        ).reshape(rows, INNER)
        rim = shifted(conv_in[:, span - (CONV - 1) :], "ctx", 1)
        extended = jnp.concatenate([rim, conv_in], axis=1).astype(F32)
        pre_conv = f_conv_bias.astype(F32) + sum(
            (taps[tap] * extended[:, tap : tap + span] for tap in range(CONV))
        )
        conv_out, conv_slope = silu_pair(pre_conv)
        conv_low = conv_out.reshape(rows, INNER).astype(BF16)
        projected = matmul(conv_low, f_select)
        rank_low = projected[:, :RANK].astype(BF16)
        b_coef = projected[:, RANK : RANK + STATE].reshape(per_micro, span, STATE)
        c_coef = projected[:, RANK + STATE :].reshape(per_micro, span, STATE)
        step_pre = matmul(rank_low, f_step) + f_step_bias.astype(F32)
        steps = jax.nn.softplus(step_pre).reshape(per_micro, span, INNER)
        zeros_state = jnp.zeros((per_micro, STATE, INNER), F32)
        final_local, _, _ = ssm_forward(zeros_state, steps, conv_out, b_coef, c_coef, decay, False)
        through = jnp.exp(decay * jnp.sum(steps, axis=1)[:, None, :])
        _, entry = prefix(
            (through, final_local),
            "ctx",
            chain,
            (jnp.ones_like(through), jnp.zeros_like(final_local)),
            False,
        )
        _, scan_out, starts = ssm_forward(entry, steps, conv_out, b_coef, c_coef, decay, True)
        gate_act, gate_slope = silu_pair(gate_z)
        pre_gate = scan_out + skip * conv_out
        ssm_flat = (pre_gate * gate_act).reshape(rows, INNER)
        attn_scale = rms_scale(attn)
        attn_norm = attn * attn_scale
        ssm_scale = rms_scale(ssm_flat)
        ssm_norm = ssm_flat * ssm_scale
        merged = (0.5 * (attn_norm * beta_a + ssm_norm * beta_s)).astype(BF16)
        hidden1 = x_flat + matmul(merged, f_output)
        scale2 = rms_scale(hidden1)
        normed2 = (hidden1 * scale2 * gain_two).astype(BF16)
        gate_pre = matmul(normed2, f_gate)
        up_pre = matmul(normed2, f_up)
        gate_act2, gate_slope2 = silu_pair(gate_pre)
        inner_ff = (gate_act2 * up_pre).astype(BF16)
        hidden2 = hidden1 + matmul(inner_ff, f_down)
        outputs.append(hidden2.astype(BF16).reshape(per_micro, span, D))
        target = teacher[first_row:last_row].reshape(rows, D).astype(F32)
        weight_rows = valid[first_row:last_row].reshape(rows, 1).astype(F32)
        diff = hidden2 - target
        loss_local = loss_local + jnp.sum(weight_rows * diff * diff)
        full = fetch()
        (
            f_query,
            f_key,
            f_value,
            f_mixer,
            f_output,
            f_gate,
            f_up,
            f_down,
            f_select,
            f_step,
            f_decay,
            f_taps,
            f_conv_bias,
            f_step_bias,
            f_skip,
            f_beta_attn,
            f_beta_ssm,
            f_gain_first,
            f_gain_second,
        ) = full
        seed = (
            cotangent[first_row:last_row].reshape(rows, D).astype(F32) + factor * weight_rows * diff
        )
        seed_low = seed.astype(BF16)
        g_down = outer_sum(inner_ff, seed_low)
        d_inner = matmul_back(seed_low, f_down)
        d_gate = (d_inner * up_pre * gate_slope2).astype(BF16)
        d_up = (d_inner * gate_act2).astype(BF16)
        g_gate = outer_sum(normed2, d_gate)
        g_up = outer_sum(normed2, d_up)
        d_norm2 = matmul_back(d_gate, f_gate) + matmul_back(d_up, f_up)
        g_gain_second = jnp.sum(d_norm2 * hidden1 * scale2, axis=0)
        d_hidden1 = seed + norm_back(hidden1, scale2, d_norm2 * gain_two)
        d_branch = d_hidden1.astype(BF16)
        g_output = outer_sum(merged, d_branch)
        d_merged = matmul_back(d_branch, f_output)
        g_beta_attn = jnp.sum(0.5 * d_merged * attn_norm, axis=0)
        g_beta_ssm = jnp.sum(0.5 * d_merged * ssm_norm, axis=0)
        d_attn = norm_back(attn, attn_scale, 0.5 * d_merged * beta_a).astype(BF16)
        d_ssm = norm_back(ssm_flat, ssm_scale, 0.5 * d_merged * beta_s).reshape(
            per_micro, span, INNER
        )
        d_heads = d_attn.reshape(per_micro, span, KV, group, vhead)
        probs = jnp.exp(scores_of(q_heads, k_heads) - log_total)
        d_values = jnp.einsum(
            "sgqcl,scgqv->slgv", probs.astype(BF16), d_heads, preferred_element_type=F32
        )
        d_probs = jnp.einsum("scgqv,slgv->sgqcl", d_heads, v_heads, preferred_element_type=F32)
        d_scores = (probs * (d_probs - jnp.sum(probs * d_probs, axis=-1, keepdims=True))).astype(
            BF16
        )
        d_queries = (
            (jnp.einsum("sgqcl,slgd->scgqd", d_scores, k_heads, preferred_element_type=F32) * scale)
            .reshape(rows, HEADS * HD)
            .astype(BF16)
        )
        d_keys = (
            jnp.einsum("sgqcl,scgqd->slgd", d_scores, q_heads, preferred_element_type=F32) * scale
        )
        own_keys, own_values = (
            lax.psum_scatter(
                d_keys.reshape(per_micro, length, KV * HD).astype(jnp.bfloat16),
                "ctx",
                scatter_dimension=1,
                tiled=True,
            ).astype(jnp.float32),
            lax.psum_scatter(
                d_values.reshape(per_micro, length, KV * vhead).astype(jnp.bfloat16),
                "ctx",
                scatter_dimension=1,
                tiled=True,
            ).astype(jnp.float32),
        )
        d_keys_low = own_keys.reshape(rows, KV * HD).astype(BF16)
        d_values_low = own_values.reshape(rows, KV * vhead).astype(BF16)
        d_pre_gate = d_ssm * gate_act
        d_gate_z = d_ssm * pre_gate * gate_slope
        g_skip = jnp.sum(d_pre_gate * conv_out, axis=(0, 1))
        start_local, _, _ = ssm_backward(
            zeros_state, None, steps, conv_out, b_coef, c_coef, d_pre_gate, decay, False
        )
        _, arrive = prefix(
            (through, start_local),
            "ctx",
            chain,
            (jnp.ones_like(through), jnp.zeros_like(start_local)),
            True,
        )
        _, grad_decay, scan_grads = ssm_backward(
            arrive, starts, steps, conv_out, b_coef, c_coef, d_pre_gate, decay, True
        )
        g_drive, g_steps, g_b, g_c = scan_grads
        d_step_pre = g_steps.reshape(rows, INNER) * jax.nn.sigmoid(step_pre)
        g_step_bias = jnp.sum(d_step_pre, axis=0)
        d_step_low = d_step_pre.astype(BF16)
        g_step = outer_sum(rank_low, d_step_low)
        d_rank = matmul_back(d_step_low, f_step)
        d_projected = jnp.concatenate(
            [d_rank, g_b.reshape(rows, STATE), g_c.reshape(rows, STATE)], axis=1
        ).astype(BF16)
        g_select = outer_sum(conv_low, d_projected)
        d_conv = (
            g_drive
            + d_pre_gate * skip
            + matmul_back(d_projected, f_select).reshape(per_micro, span, INNER)
        )
        d_pre_conv = d_conv * conv_slope
        g_conv_bias = jnp.sum(d_pre_conv, axis=(0, 1))
        g_taps = jnp.stack(
            [
                jnp.sum(d_pre_conv * extended[:, tap : tap + span], axis=(0, 1))
                for tap in range(CONV)
            ]
        )
        d_extended = sum(
            (
                jnp.pad(taps[tap] * d_pre_conv, ((0, 0), (tap, CONV - 1 - tap), (0, 0)))
                for tap in range(CONV)
            )
        )
        back_rim = shifted(as_sent(d_extended[:, : CONV - 1]), "ctx", -1)
        d_conv_in = d_extended[:, CONV - 1 :].at[:, span - (CONV - 1) :].add(back_rim)
        d_mixer = jnp.concatenate(
            [d_conv_in.reshape(rows, INNER), d_gate_z.reshape(rows, INNER)], axis=1
        ).astype(BF16)
        g_mixer = outer_sum(normed1, d_mixer)
        g_query = outer_sum(normed1, d_queries)
        g_key = outer_sum(normed1, d_keys_low)
        g_value = outer_sum(normed1, d_values_low)
        d_norm1 = (
            matmul_back(d_queries, f_query)
            + matmul_back(d_keys_low, f_key)
            + matmul_back(d_values_low, f_value)
            + matmul_back(d_mixer, f_mixer)
        )
        g_gain_first = jnp.sum(d_norm1 * x_flat * scale1, axis=0)
        d_tokens = d_hidden1 + norm_back(x_flat, scale1, d_norm1 * gain_one)
        input_grads.append(d_tokens.astype(BF16).reshape(per_micro, span, D))
        small_terms = (
            g_select,
            g_step,
            grad_decay * decay,
            g_taps,
            g_conv_bias,
            g_step_bias,
            g_skip,
            g_beta_attn,
            g_beta_ssm,
            g_gain_first,
            g_gain_second,
        )
        (
            t_query,
            t_key,
            t_value,
            t_mixer,
            t_output,
            t_gate,
            t_up,
            t_down,
            t_select,
            t_step,
            t_decay,
            t_taps,
            t_conv_bias,
            t_step_bias,
            t_skip,
            t_beta_attn,
            t_beta_ssm,
            t_gain_first,
            t_gain_second,
        ) = (g_query, g_key, g_value, g_mixer, g_output, g_gate, g_up, g_down) + small_terms
        larger = (
            lax.psum_scatter(
                lax.psum_scatter(
                    t_query.astype(jnp.bfloat16), "batch", scatter_dimension=0, tiled=True
                ),
                "ctx",
                scatter_dimension=1,
                tiled=True,
            ).astype(jnp.float32),
            lax.psum_scatter(
                lax.psum_scatter(
                    t_key.astype(jnp.bfloat16), "batch", scatter_dimension=0, tiled=True
                ),
                "ctx",
                scatter_dimension=1,
                tiled=True,
            ).astype(jnp.float32),
            lax.psum_scatter(
                lax.psum_scatter(
                    t_value.astype(jnp.bfloat16), "batch", scatter_dimension=0, tiled=True
                ),
                "ctx",
                scatter_dimension=1,
                tiled=True,
            ).astype(jnp.float32),
            lax.psum_scatter(
                lax.psum_scatter(
                    t_mixer.astype(jnp.bfloat16), "batch", scatter_dimension=0, tiled=True
                ),
                "ctx",
                scatter_dimension=1,
                tiled=True,
            ).astype(jnp.float32),
            lax.psum_scatter(
                lax.psum_scatter(
                    t_output.astype(jnp.bfloat16), "batch", scatter_dimension=0, tiled=True
                ),
                "ctx",
                scatter_dimension=1,
                tiled=True,
            ).astype(jnp.float32),
            lax.psum_scatter(
                lax.psum_scatter(
                    t_gate.astype(jnp.bfloat16), "batch", scatter_dimension=0, tiled=True
                ),
                "ctx",
                scatter_dimension=1,
                tiled=True,
            ).astype(jnp.float32),
            lax.psum_scatter(
                lax.psum_scatter(
                    t_up.astype(jnp.bfloat16), "batch", scatter_dimension=0, tiled=True
                ),
                "ctx",
                scatter_dimension=1,
                tiled=True,
            ).astype(jnp.float32),
            lax.psum_scatter(
                lax.psum_scatter(
                    t_down.astype(jnp.bfloat16), "batch", scatter_dimension=0, tiled=True
                ),
                "ctx",
                scatter_dimension=1,
                tiled=True,
            ).astype(jnp.float32),
        )
        smaller = (
            lax.psum(
                lax.psum_scatter(
                    t_select.astype(jnp.bfloat16), "batch", scatter_dimension=0, tiled=True
                ),
                "ctx",
            ).astype(jnp.float32),
            lax.psum(
                lax.psum_scatter(
                    t_step.astype(jnp.bfloat16), "batch", scatter_dimension=1, tiled=True
                ),
                "ctx",
            ).astype(jnp.float32),
            lax.psum(
                lax.psum_scatter(
                    t_decay.astype(jnp.bfloat16), "batch", scatter_dimension=1, tiled=True
                ),
                "ctx",
            ).astype(jnp.float32),
            lax.psum(
                lax.psum_scatter(
                    t_taps.astype(jnp.bfloat16), "batch", scatter_dimension=1, tiled=True
                ),
                "ctx",
            ).astype(jnp.float32),
            lax.psum(
                lax.psum_scatter(
                    t_conv_bias.astype(jnp.bfloat16), "batch", scatter_dimension=0, tiled=True
                ),
                "ctx",
            ).astype(jnp.float32),
            lax.psum(
                lax.psum_scatter(
                    t_step_bias.astype(jnp.bfloat16), "batch", scatter_dimension=0, tiled=True
                ),
                "ctx",
            ).astype(jnp.float32),
            lax.psum(
                lax.psum_scatter(
                    t_skip.astype(jnp.bfloat16), "batch", scatter_dimension=0, tiled=True
                ),
                "ctx",
            ).astype(jnp.float32),
            lax.psum(
                lax.psum_scatter(
                    t_beta_attn.astype(jnp.bfloat16), "batch", scatter_dimension=0, tiled=True
                ),
                "ctx",
            ).astype(jnp.float32),
            lax.psum(
                lax.psum_scatter(
                    t_beta_ssm.astype(jnp.bfloat16), "batch", scatter_dimension=0, tiled=True
                ),
                "ctx",
            ).astype(jnp.float32),
            lax.psum(
                lax.psum_scatter(
                    t_gain_first.astype(jnp.bfloat16), "batch", scatter_dimension=0, tiled=True
                ),
                "ctx",
            ).astype(jnp.float32),
            lax.psum(
                lax.psum_scatter(
                    t_gain_second.astype(jnp.bfloat16), "batch", scatter_dimension=0, tiled=True
                ),
                "ctx",
            ).astype(jnp.float32),
        )
        shares = tuple(larger) + tuple(smaller)
        result = (
            shares
            if result is None
            else tuple((left + right for left, right in zip(result, shares)))
        )
    loss_sum = lax.psum(loss_local, ("batch", "ctx"))
    (
        r_query,
        r_key,
        r_value,
        r_mixer,
        r_output,
        r_gate,
        r_up,
        r_down,
        r_select,
        r_step,
        r_decay,
        r_taps,
        r_conv_bias,
        r_step_bias,
        r_skip,
        r_beta_attn,
        r_beta_ssm,
        r_gain_first,
        r_gain_second,
    ) = result
    return (
        jnp.concatenate(outputs, axis=0),
        loss_sum / (count * D),
        jnp.concatenate(input_grads, axis=0),
        r_query,
        r_key,
        r_value,
        r_mixer,
        r_output,
        r_gate,
        r_up,
        r_down,
        r_select,
        r_step,
        r_decay,
        r_taps,
        r_conv_bias,
        r_step_bias,
        r_skip,
        r_beta_attn,
        r_beta_ssm,
        r_gain_first,
        r_gain_second,
    )


def solution(mesh):
    return jax.shard_map(
        per_device,
        mesh=mesh,
        in_specs=(
            P("batch", "ctx", None),
            P("batch", "ctx", None),
            P("batch", "ctx", None),
            P("batch", "ctx"),
            P("batch", "ctx"),
            P("batch", "ctx"),
            P("batch", "ctx"),
            P("batch", "ctx"),
            P("batch", "ctx"),
            P("batch", "ctx"),
            P("batch", "ctx"),
            P("batch", "ctx"),
            P("batch", None),
            P(None, "batch"),
            P(None, "batch"),
            P(None, "batch"),
            P("batch"),
            P("batch"),
            P("batch"),
            P("batch"),
            P("batch"),
            P("batch"),
            P("batch"),
        ),
        out_specs=(
            P("batch", "ctx", None),
            P(),
            P("batch", "ctx", None),
            P("batch", "ctx"),
            P("batch", "ctx"),
            P("batch", "ctx"),
            P("batch", "ctx"),
            P("batch", "ctx"),
            P("batch", "ctx"),
            P("batch", "ctx"),
            P("batch", "ctx"),
            P("batch", None),
            P(None, "batch"),
            P(None, "batch"),
            P(None, "batch"),
            P("batch"),
            P("batch"),
            P("batch"),
            P("batch"),
            P("batch"),
            P("batch"),
            P("batch"),
        ),
        check_vma=False,
    )
```

profile of v0, /device:TPU:8, one launch (start us, length us, event | category | flops | bytes accessed | tf_op | source)
XLA Modules:
  0.0 7369.5 jit_solution(8106097139174215927)
XLA Ops:
  616.0 123.9 %while.194 = (s32[]{:T(128)}, f32[1,16,3200]{2,1,0:T(8,128)}, f32[16,1,16,3200]{3,2,1,0:T(8,128)}, f32[16,3200]{1,0:T(8,128)S(1)}, f32[16,1,16,3200]{3,2,1,0:T(8...) while((s32[]{:T(128)}, f32[1,16,3200]{2,1,0:T(8,128)}, ...), condition=%wide.region_6.7_spmd.clone, body=%wide.region_5.6_spmd.clone.sunk | while | flops 3379203 | bytes 2859631 | solution.py:119
  767.8 358.6 %while.192 = (s32[]{:T(128)}, f32[1,16,3200]{2,1,0:T(8,128)}, f32[16,1,16,3200]{3,2,1,0:T(8,128)}, f32[16,1,16,3200]{3,2,1,0:T(8,128)}, f32[16,1,16,3200]{3,2,1,...) while((s32[]{:T(128)}, f32[1,16,3200]{2,1,0:T(8,128)}, ...), condition=%wide.region_26.27_spmd, body=%wide.region_9.26_spmd.sunk | while | flops 7372802 | bytes 7678337 | solution.py:119
  1143.8 125.8 %while.196 = (s32[]{:T(128)}, f32[1,16,3200]{2,1,0:T(8,128)}, f32[16,1,16,3200]{3,2,1,0:T(8,128)}, f32[16,3200]{1,0:T(8,128)S(1)}, f32[16,1,16,3200]{3,2,1,0:T(8...) while((s32[]{:T(128)}, f32[1,16,3200]{2,1,0:T(8,128)}, ...), condition=%wide.region_35.36_spmd.clone, body=%wide.region_34.35_spmd.clone.sunk | while | flops 3379203 | bytes 2859631 | solution.py:119
  1297.5 372.9 %while.193 = (s32[]{:T(128)}, f32[1,16,3200]{2,1,0:T(8,128)}, f32[16,1,16,3200]{3,2,1,0:T(8,128)}, f32[16,1,16,3200]{3,2,1,0:T(8,128)}, f32[16,1,16,3200]{3,2,1,...) while((s32[]{:T(128)}, f32[1,16,3200]{2,1,0:T(8,128)}, ...), condition=%wide.region_55.56_spmd, body=%wide.region_38.55_spmd.sunk | while | flops 7372802 | bytes 7678337 | solution.py:119
  1958.1 114.9 %while.198 = (s32[]{:T(128)}, f32[1,16,3200]{2,1,0:T(8,128)}, f32[16,1,16,3200]{3,2,1,0:T(8,128)}, f32[16,3200]{1,0:T(8,128)S(1)}, f32[16,1,16,16]{3,2,1,0:T(8,1...) while((s32[]{:T(128)}, f32[1,16,3200]{2,1,0:T(8,128)}, ...), condition=%wide.region_70.71_spmd.clone, body=%wide.region_69.70_spmd.clone.sunk | while | flops 3328004 | bytes 2667651 | solution.py:179
  2100.3 927.4 %while.200 = (s32[]{:T(128)}, f32[1,16,3200]{2,1,0:T(8,128)}, f32[16,3200]{1,0:T(8,128)}, f32[16,1,16,3200]{3,2,1,0:T(8,128)}, f32[16,1,16,3200]{3,2,1,0:T(8,128...) while((s32[]{:T(128)}, f32[1,16,3200]{2,1,0:T(8,128)}, ...), condition=%wide.region_138.139_spmd.clone, body=%wide.region_73.138_spmd.clone.sunk | while | flops 35378692 | bytes 45611928 | solution.py:179
  3037.3 113.9 %while.201 = (s32[]{:T(128)}, f32[1,16,3200]{2,1,0:T(8,128)}, f32[16,1,16,3200]{3,2,1,0:T(8,128)}, f32[16,3200]{1,0:T(8,128)S(1)}, f32[16,1,16,16]{3,2,1,0:T(8,1...) while((s32[]{:T(128)}, f32[1,16,3200]{2,1,0:T(8,128)}, ...), condition=%wide.region_147.148_spmd.clone, body=%wide.region_146.147_spmd.clone.sunk | while | flops 3328004 | bytes 2667651 | solution.py:179
  3308.7 927.8 %while.203 = (s32[]{:T(128)}, f32[1,16,3200]{2,1,0:T(8,128)}, f32[16,3200]{1,0:T(8,128)}, f32[16,1,16,3200]{3,2,1,0:T(8,128)}, f32[16,1,16,3200]{3,2,1,0:T(8,128...) while((s32[]{:T(128)}, f32[1,16,3200]{2,1,0:T(8,128)}, ...), condition=%wide.region_215.216_spmd.clone, body=%wide.region_150.215_spmd.clone.sunk | while | flops 35378692 | bytes 45611928 | solution.py:179
  4586.0 66.2 reduce-scatter.183.cloned.1.call-done
  4654.5 66.3 reduce-scatter.181.cloned.1.call-done
  4723.1 88.3 %reduce-scatter.127.cloned.1.call-done = bf16[400,1600]{1,0:T(8,128)(2,1)} async-done(((bf16[3200,1600]{1,0:T(8,128)(2,1)}), bf16[400,1600]{1,0:T(8,128)(2,1)}) %reduce-scatter.127.cloned.1.call-update) | async-done | bytes 1280016 | tf_op jit(solution)/shard_map/reduce_scatter | solution.py:580
  4814.9 86.9 %reduce-scatter.125.cloned.1.call-done = bf16[400,1600]{1,0:T(8,128)(2,1)} async-done(((bf16[3200,1600]{1,0:T(8,128)(2,1)}), bf16[400,1600]{1,0:T(8,128)(2,1)}) %reduce-scatter.125.cloned.1.call-update) | async-done | bytes 1280016 | tf_op jit(solution)/shard_map/reduce_scatter | solution.py:580
  4905.3 158.6 %reduce-scatter.131.cloned.1.call-done = bf16[688,1600]{1,0:T(8,128)(2,1)} async-done(((bf16[5504,1600]{1,0:T(8,128)(2,1)}), bf16[688,1600]{1,0:T(8,128)(2,1)}) %reduce-scatter.131.cloned.1.call-update) | async-done | bytes 2201616 | tf_op jit(solution)/shard_map/reduce_scatter | solution.py:604
  5068.4 157.5 %reduce-scatter.129.cloned.1.call-done = bf16[688,1600]{1,0:T(8,128)(2,1)} async-done(((bf16[5504,1600]{1,0:T(8,128)(2,1)}), bf16[688,1600]{1,0:T(8,128)(2,1)}) %reduce-scatter.129.cloned.1.call-update) | async-done | bytes 2201616 | tf_op jit(solution)/shard_map/reduce_scatter | solution.py:604
  5230.4 170.8 %reduce-scatter.195.cloned.1.call-done = bf16[200,6400]{1,0:T(8,128)(2,1)} async-done(((bf16[1600,6400]{1,0:T(8,128)(2,1)}), bf16[200,6400]{1,0:T(8,128)(2,1)}) %reduce-scatter.195.cloned.1.call-update) | async-done | bytes 2560016
  5406.1 171.0 %reduce-scatter.193.cloned.1.call-done = bf16[200,6400]{1,0:T(8,128)(2,1)} async-done(((bf16[1600,6400]{1,0:T(8,128)(2,1)}), bf16[200,6400]{1,0:T(8,128)(2,1)}) %reduce-scatter.193.cloned.1.call-update) | async-done | bytes 2560016
  5581.8 195.5 %reduce-scatter.199.cloned.1.call-done = bf16[200,5504]{1,0:T(8,128)(2,1)} async-done(((bf16[1600,5504]{1,0:T(8,128)(2,1)}), bf16[200,5504]{1,0:T(8,128)(2,1)}) %reduce-scatter.199.cloned.1.call-update) | async-done | bytes 2201616
  5781.7 208.3 %reduce-scatter.197.cloned.1.call-done = bf16[200,5504]{1,0:T(8,128)(2,1)} async-done(((bf16[1600,5504]{1,0:T(8,128)(2,1)}), bf16[200,5504]{1,0:T(8,128)(2,1)}) %reduce-scatter.197.cloned.1.call-update) | async-done | bytes 2201616
  5994.5 209.1 %reduce-scatter.203.cloned.1.call-done = bf16[200,5504]{1,0:T(8,128)(2,1)} async-done(((bf16[1600,5504]{1,0:T(8,128)(2,1)}), bf16[200,5504]{1,0:T(8,128)(2,1)}) %reduce-scatter.203.cloned.1.call-update) | async-done | bytes 2201616
  6413.7 195.0 %reduce-scatter.201.cloned.1.call-done = bf16[200,5504]{1,0:T(8,128)(2,1)} async-done(((bf16[1600,5504]{1,0:T(8,128)(2,1)}), bf16[200,5504]{1,0:T(8,128)(2,1)}) %reduce-scatter.201.cloned.1.call-update) | async-done | bytes 2201616
  6617.9 68.5 all-reduce.49.cloned.1.call-done
  7001.8 61.8 reduce-scatter.151.cloned.1.call-done
  7065.1 63.3 reduce-scatter.149.cloned.1.call-done
  7301.6 56.1 reduce-scatter.161.cloned.1.call-done
  (8159 shorter events, 5314.7 us)
Async XLA Ops:
  130.6 1553.3 %all-gather.39.cloned.1.call-start = ((), (), s32[]{:S(2)}) async-start(), calls=%async_computation.48 | async-start | bytes 11980800 | tf_op jit(solution)/shard_map/all_gather | solution.py:246
  396.0 3869.5 %reduce-scatter.121.cloned.1.call-start = ((), (), s32[]{:S(2)}) async-start(), calls=%async_computation.55 | async-start | bytes 819200 | tf_op jit(solution)/shard_map/reduce_scatter | solution.py:434
  4431.2 1558.7 %reduce-scatter.197.cloned.1.call-start = ((), (), s32[]{:S(2)}) async-start(), calls=%async_computation.98 | async-start | bytes 19814400
  4442.8 1760.8 %reduce-scatter.203.cloned.1.call-start = ((), (), s32[]{:S(2)}) async-start(), calls=%async_computation.101 | async-start | bytes 19814400
  4453.4 1801.3 %reduce-scatter.179.cloned.1.call-start = ((), (), s32[]{:S(2)}) async-start(), calls=%async_computation.89 | async-start | bytes 921600
  4455.6 1837.2 %reduce-scatter.177.cloned.1.call-start = ((), (), s32[]{:S(2)}) async-start(), calls=%async_computation.88 | async-start | bytes 921600
  4457.0 1873.6 %reduce-scatter.175.cloned.1.call-start = ((), (), s32[]{:S(2)}) async-start(), calls=%async_computation.87 | async-start | bytes 921600
  4458.4 1910.5 %reduce-scatter.173.cloned.1.call-start = ((), (), s32[]{:S(2)}) async-start(), calls=%async_computation.86 | async-start | bytes 921600
  4459.6 1950.7 %all-reduce.51.cloned.1.call-start = ((), (), s32[]{:S(2)}) async-start(), calls=%async_computation.103 | async-start | bytes 966656 | tf_op jit(solution)/shard_map/psum | solution.py:613
  4463.2 2145.6 %reduce-scatter.201.cloned.1.call-start = ((), (), s32[]{:S(2)}) async-start(), calls=%async_computation.100 | async-start | bytes 19814400
  4473.7 2212.7 %all-reduce.49.cloned.1.call-start = ((), (), s32[]{:S(2)}) async-start(), calls=%async_computation.102 | async-start | bytes 196608
  4517.2 2201.1 %reduce-scatter.143.cloned.1.call-start = ((), (), s32[]{:S(2)}) async-start(), calls=%async_computation.71 | async-start | bytes 204800
  4519.0 2207.7 %reduce-scatter.141.cloned.1.call-start = ((), (), s32[]{:S(2)}) async-start(), calls=%async_computation.70 | async-start | bytes 204800
  4520.8 2226.7 %reduce-scatter.147.cloned.1.call-start = ((), (), s32[]{:S(2)}) async-start(), calls=%async_computation.73 | async-start | bytes 409600
  4539.1 2229.4 %reduce-scatter.145.cloned.1.call-start = ((), (), s32[]{:S(2)}) async-start(), calls=%async_computation.72 | async-start | bytes 409600
  4585.9 2208.3 %reduce-scatter.139.cloned.1.call-start = ((), (), s32[]{:S(2)}) async-start(), calls=%async_computation.69 | async-start | bytes 1024000
  4654.4 2165.7 %reduce-scatter.137.cloned.1.call-start = ((), (), s32[]{:S(2)}) async-start(), calls=%async_computation.68 | async-start | bytes 1024000
  4723.0 2135.7 %reduce-scatter.155.cloned.1.call-start = ((), (), s32[]{:S(2)}) async-start(), calls=%async_computation.77 | async-start | bytes 2048000
  4814.9 2081.7 %reduce-scatter.153.cloned.1.call-start = ((), (), s32[]{:S(2)}) async-start(), calls=%async_computation.76 | async-start | bytes 2048000
  4905.3 2042.0 %reduce-scatter.167.cloned.1.call-start = ((), (), s32[]{:S(2)}) async-start(), calls=%async_computation.83 | async-start | bytes 3072000
  5068.3 1930.5 %reduce-scatter.165.cloned.1.call-start = ((), (), s32[]{:S(2)}) async-start(), calls=%async_computation.82 | async-start | bytes 3072000
  5230.4 1833.2 %reduce-scatter.151.cloned.1.call-start = ((), (), s32[]{:S(2)}) async-start(), calls=%async_computation.75 | async-start | bytes 4096000
  5405.9 1722.5 %reduce-scatter.149.cloned.1.call-start = ((), (), s32[]{:S(2)}) async-start(), calls=%async_computation.74 | async-start | bytes 4096000
  5581.7 1603.9 %reduce-scatter.159.cloned.1.call-start = ((), (), s32[]{:S(2)}) async-start(), calls=%async_computation.79 | async-start | bytes 3522560
  (2467 other events, 63063.6 us)
Sparse Core Ops, SparseCore 0:
  54.6 66.0 all-gather.52
  438.5 105.5 all-gather.34
  546.5 63.9 all-gather.38
  612.2 93.3 all-gather.40
  707.6 93.3 all-gather.42
  802.7 96.3 all-gather.46
  4587.3 64.7 reduce-scatter.182
  4655.9 64.7 reduce-scatter.180
  4724.3 87.0 reduce-scatter.126
  4814.8 86.9 reduce-scatter.124
  4905.4 158.4 reduce-scatter.130
  5067.5 158.4 reduce-scatter.128
  5229.3 171.8 reduce-scatter.194
  5405.2 171.8 reduce-scatter.192
  5579.5 197.7 reduce-scatter.198
  5779.5 210.4 reduce-scatter.196
  5992.2 211.3 reduce-scatter.202
  6412.6 196.0 reduce-scatter.200
  6615.4 70.9 all-reduce.48
  7001.1 62.4 reduce-scatter.150
  7065.9 62.3 reduce-scatter.148
  7187.9 54.9 reduce-scatter.156
  7245.1 54.9 reduce-scatter.162
  7302.6 54.9 reduce-scatter.160
  (36 shorter events, 1273.0 us)
where the time goes:
time: 7460 us; the launch traced here: 7370 us
  waiting for transfers between devices  2910 us (39%)
  other arithmetic  1870 us (25%)
  local copies, waits for them, and re-layouts  1600 us (21%)
  matrix products  595 us (8%)
  blocking collectives  326 us (4%)
    unnamed x95, waiting for transfers between devices  2180 us
    another operation x544, local copies, waits for them, and re-layouts, advance(): return (state, (jnp.stack(outs, axis=1), first))  335 us
    reduce_sum x192, other arithmetic, retreat(): jnp.sum(along * decay, axis=1) + weighted * drive_blk[:, place]  329 us
    reduce_scatter x2, waiting for transfers between devices, per_device(): lax.psum_scatter(t_down.astype(jnp.bfloat16), 'batch', scatter_dimension=...  316 us
    squeeze x416, local copies, waits for them, and re-layouts, ssm_forward(): final, kept = lax.scan(advance, start, items)  311 us
    reduce_sum x160, other arithmetic, retreat(): jnp.sum(current * (step_blk[:, place] * drive_blk[:, place])[:, None, :],...  304 us
    reduce_scatter x2, waiting for transfers between devices, per_device(): lax.psum_scatter(t_output.astype(jnp.bfloat16), 'batch', scatter_dimensio...  175 us
    dot_general x20, matrix products, matmul_back(): lax.dot_general(left, right, (((1,), (1,)), ((), ())), preferred_element_...  160 us

commit v1 on v0

v1 whole, which is shorter than its diff:
```python
import functools
import math

import jax
import jax.numpy as jnp
from jax import lax
from jax.experimental import pallas as pl
from jax.experimental.pallas import tpu as pltpu
from jax.sharding import PartitionSpec as P

D = 1600
HEADS = 25
KV = 5
HD = 64
INNER = 3200
STATE = 16
CONV = 4
RANK = 100
WINDOW = 1024
GROUP = HEADS // KV
VHEAD = INNER // HEADS
LANE = 128

EPS = 1e-05
F32 = jnp.float32
BF16 = jnp.bfloat16
LOG2E = math.log2(math.e)
LN2 = math.log(2.0)
MESH = pl.DeviceIdType.MESH


def permute_bit(value, axis, bit):
    count = lax.axis_size(axis)
    return lax.ppermute(value, axis, [(i, i ^ bit) for i in range(count)])


def shift(value, axis, steps, wrap):
    count = lax.axis_size(axis)
    pairs = [(i, (i + steps) % count) for i in range(count) if wrap or 0 <= i + steps < count]
    return lax.ppermute(value, axis, pairs)


def bits_of(axis):
    count = lax.axis_size(axis)
    return [1 << k for k in range(count.bit_length() - 1)]


def total_over(value, axes):
    for axis in axes:
        for bit in bits_of(axis):
            value = value + permute_bit(value, axis, bit)
    return value


def from_ctx(blocks):
    count, mine = lax.axis_size("ctx"), lax.axis_index("ctx")
    out = []
    for at in range(count):
        block = blocks[0]
        for r in range(1, count):
            block = jnp.where(mine ^ r == at, blocks[r], block)
        out.append(block)
    return out


def gather_columns(shard):
    return lax.all_gather(shard, "ctx", axis=0)


def gather_rows(block):
    return lax.all_gather(block, "batch", axis=0, tiled=True)


def copy_rows(rows, copy):
    whole = rows // 16 * 16

    def body(i, _):
        copy(pl.multiple_of(i * 16, 16), 16)
        return 0

    lax.fori_loop(0, whole // 16, body, 0)
    if whole < rows:
        copy(whole, rows - whole)


def pieces_of(part, n, places, at=0, group=0, wide=0):
    out = []
    for i, place in enumerate(places):
        lo = 0
        while lo < n:
            col = i * n + lo
            hi, target = n, at + col
            if group:
                hi = min(n, (col // group + 1) * group - i * n)
                target = at + col // group * wide + col % group
            out.append((part, place, lo, hi, target))
            lo = hi
    return tuple(out)


def gather_kernel(n_parts, items, program, *refs):
    plain = [i for i, (pieces, _) in enumerate(items) if not pieces]
    shards, refs = refs[:n_parts], refs[n_parts:]
    direct, refs = dict(zip(plain, refs)), refs[len(plain) :]
    wholes, refs = refs[: len(items)], refs[len(items) :]
    parts, refs = refs[:n_parts], refs[n_parts:]
    blocks, sems = refs[: len(items)], refs[len(items) :]
    z_own, z_send, z_recv, b_send, b_recv, b_own = sems
    b, c = lax.axis_index("batch"), lax.axis_index("ctx")
    bits = bits_of("ctx")[::-1]

    barrier = pltpu.get_barrier_semaphore()
    peers = [{"ctx": c ^ bit} for bit in bits] + [{"batch": b ^ bit} for bit in (1, 2, 4)]
    for device in peers:
        pl.semaphore_signal(barrier, inc=1, device_id=device, device_id_type=MESH)
    pl.semaphore_wait(barrier, len(peers))

    started, stores = [], []

    def remote(source, target, send_sem, recv_sem, device):
        copy = pltpu.make_async_remote_copy(
            src_ref=source,
            dst_ref=target,
            send_sem=send_sem,
            recv_sem=recv_sem,
            device_id=device,
            device_id_type=MESH,
        )
        copy.start()
        started.append(copy)
        return copy

    come, reached = {}, {}

    def columns(part):
        shard, slot = shards[part], parts[part]
        stage = reached.get(part, 0)
        bit = bits[stage]
        if stage == 0:
            own = pltpu.make_async_copy(shard, slot.at[c], z_own.at[part])
            own.start()
            come[part] = {0: own.wait}
        for r in sorted(come[part]):
            if r:
                come[part][r]()
                come[part][r] = lambda: None
            copy = remote(
                slot.at[c ^ r] if r else shard,
                slot.at[c ^ r],
                z_send.at[part, r ^ bit],
                z_recv.at[part, r ^ bit],
                {"ctx": c ^ bit},
            )
            come[part][r ^ bit] = copy.wait_recv
        reached[part] = stage + 1

    flights = {}

    def send(item, slot, source, target, bit):
        return remote(
            source, target, b_send.at[item, slot], b_recv.at[item, slot], {"batch": b ^ bit}
        )

    def keep(item, slot, r):
        there = wholes[item].at[b ^ r]
        store = pltpu.make_async_copy(blocks[item].at[slot], there, b_own.at[item, slot])
        store.start()
        stores.append(store)
        return send(item, 4 + slot, blocks[item].at[slot], there, 1)

    def launch(item):
        pieces, rows = items[item]
        block = blocks[item]
        if pieces:
            for part in sorted({piece[0] for piece in pieces}):
                for r in come[part]:
                    come[part][r]()
                    come[part][r] = lambda: None
            ends = sorted((at, at + hi - lo) for _, _, lo, hi, at in pieces)
            ends.append((block.shape[2], 0))
            gaps = [(end, ends[i + 1][0]) for i, (_, end) in enumerate(ends[:-1])]

            def relay(start, count):
                for part, place, lo, hi, at in pieces:
                    block[0, pl.ds(start, count), at : at + hi - lo] = parts[part][
                        place, pl.ds(start, count), lo:hi
                    ]
                for lo, hi in gaps:
                    if lo < hi:
                        block[0, pl.ds(start, count), lo:hi] = jnp.zeros((count, hi - lo), block.dtype)

            copy_rows(block.shape[1], relay)
        else:
            own = pltpu.make_async_copy(direct[item], block.at[0], b_own.at[item, 4])
            own.start()
            own.wait()
        if rows:
            flights[item] = [
                send(item, 1, block.at[0], block.at[1], 2),
                send(item, 2, block.at[0], block.at[2], 4),
            ]
            flights[item].append(keep(item, 0, 0))
        else:
            store = pltpu.make_async_copy(block.at[0], wholes[item], b_own.at[item, 0])
            store.start()
            stores.append(store)

    def forward(item):
        block, flight = blocks[item], flights[item]
        n = block.shape[2]
        half = n // 2 // LANE * LANE
        flight[0].wait_recv()
        left, right = (slice(None), slice(0, half)), (slice(None), slice(half, n))
        flight.append(send(item, 3, block.at[1, *left], block.at[3, *left], 4))
        flight.append(keep(item, 1, 2))
        flight[1].wait_recv()
        flight.append(send(item, 0, block.at[2, *right], block.at[3, *right], 2))
        flight.append(keep(item, 2, 4))

    def last(item):
        flight = flights[item]
        flight[3].wait_recv()
        flight[5].wait_recv()
        flight.append(keep(item, 3, 6))

    acts = {"columns": columns, "launch": launch, "forward": forward, "last": last}
    for act, which in program:
        acts[act](which)
    for flight in flights.values():
        for key in (2, 4, 6, 7):
            flight[key].wait_recv()
    for copy in stores:
        copy.wait()
    for copy in started:
        copy.wait_send()


def gather_all(shards, items, program, collective_id):
    count, nbatch = lax.axis_size("ctx"), lax.axis_size("batch")
    if nbatch != 8:
        found, out = [gather_columns(shard) for shard in shards], []
        for item in items:
            if not isinstance(item, tuple):
                out.append(gather_rows(item).reshape(nbatch, *item.shape))
                continue
            pieces, n, rows = item
            block = jnp.zeros((found[pieces[0][0]].shape[1], n), shards[pieces[0][0]].dtype)
            for part, place, lo, hi, at in pieces:
                block = block.at[:, at : at + hi - lo].set(found[part][place, :, lo:hi])
            out.append(gather_rows(block).reshape(nbatch, *block.shape) if rows else block)
        return out
    flat, kinds, shapes, blocks = list(shards), [], [], []
    for item in items:
        if isinstance(item, tuple):
            pieces, n, rows = item
            k, dtype = shards[pieces[0][0]].shape[0], shards[pieces[0][0]].dtype
        else:
            (k, n), pieces, rows, dtype = item.shape, (), True, item.dtype
            flat.append(item)
        kinds.append((pieces, rows))
        blocks.append(pltpu.VMEM((4 if rows else 1, k, n), dtype))
        shapes.append(jax.ShapeDtypeStruct((nbatch, k, n) if rows else (k, n), dtype))
    dma = pltpu.SemaphoreType.DMA
    hbm = pl.BlockSpec(memory_space=pl.ANY)
    return pl.pallas_call(
        functools.partial(gather_kernel, len(shards), tuple(kinds), program),
        in_specs=[hbm] * len(flat),
        out_specs=[hbm] * len(shapes),
        out_shape=shapes,
        scratch_shapes=[pltpu.VMEM((count,) + w.shape, w.dtype) for w in shards]
        + blocks
        + [dma((len(shards),)), dma((len(shards), count)), dma((len(shards), count))]
        + [dma((len(shapes), 8)), dma((len(shapes), 8)), dma((len(shapes), 5))],
        compiler_params=pltpu.CompilerParams(
            collective_id=collective_id, has_side_effects=True, vmem_limit_bytes=56 << 20
        ),
        name="gather_weights",
    )(*flat)


class Staged:
    def __init__(self, live):
        self.live = live
        self.fresh = list(live)
        self.stage = 0

    def fly(self, key, value):
        self.live[key] = value
        self.fresh.append(key)


def hold(staged, *values):
    flying = [[item.live[key] for key in item.fresh] for item in staged]
    flying, values = lax.optimization_barrier((flying, values))
    for item, arrived in zip(staged, flying):
        item.live.update(zip(item.fresh, arrived))
        item.fresh = []
    return values[0] if len(values) == 1 else values


class FromCtx(Staged):
    def __init__(self, value):
        super().__init__({0: value[None]})
        self.orders = [[0]]

    def step(self):
        bits = bits_of("ctx")[::-1]
        if self.stage < len(bits):
            bit = bits[self.stage]
            sent = list(self.live.values())
            sent = jnp.concatenate(sent, axis=0) if len(sent) > 1 else sent[0]
            self.orders.append([r ^ bit for order in self.orders for r in order])
            self.fly(self.stage + 1, permute_bit(sent, "ctx", bit))
        self.stage += 1

    def finish(self):
        while self.stage < len(bits_of("ctx")):
            self.step()
        return {
            r: self.live[i][j] for i, order in enumerate(self.orders) for j, r in enumerate(order)
        }


class ToCtx(Staged):
    def __init__(self, blocks):
        super().__init__({(r, 0): block for r, block in blocks.items()})

    def total(self, r):
        terms = [v.astype(F32) for key, v in self.live.items() if key[0] == r]
        return functools.reduce(jnp.add, terms)

    def step(self):
        bits = bits_of("ctx")
        if self.stage < len(bits):
            bit = bits[self.stage]
            which = sorted({key[0] for key in self.live if key[0] & bit})
            sent = jnp.stack([self.total(r).astype(BF16) for r in which])
            got = permute_bit(sent, "ctx", bit)
            self.live = {key: v for key, v in self.live.items() if not key[0] & bit}
            self.fresh = [key for key in self.fresh if key in self.live]
            for i, r in enumerate(which):
                self.fly((r ^ bit, self.stage + 1), got[i])
        self.stage += 1

    def result(self):
        while self.stage < len(bits_of("ctx")):
            self.step()
        return self.total(0)


def assemble_kernel(names, cuts, *refs):
    parts, wholes = refs[: len(names)], refs[len(names) : len(names) + len(cuts)]
    held, sems_in, sems_out, send_sems, recv_sems = refs[-5:]
    b = lax.axis_index("batch")
    other = {"batch": b ^ 1}
    ins = {}
    for i, (part, (r, lo)) in enumerate(zip(parts, names)):
        n = part.shape[1]
        slot = held.at[r // 2] if n == held.shape[2] else held.at[r // 2, :, lo : lo + n]
        ins.setdefault(r, []).append(pltpu.make_async_copy(part, slot, sems_in.at[i]))
        ins[r][-1].start()
    barrier = pltpu.get_barrier_semaphore()
    pl.semaphore_signal(barrier, inc=1, device_id=other, device_id_type=MESH)
    pl.semaphore_wait(barrier, 1)
    waits = []
    for r, copies in ins.items():
        for copy in copies:
            copy.wait()
        for i, (whole, (lo, hi)) in enumerate(zip(wholes, cuts)):
            slot = held.at[r // 2] if len(cuts) == 1 else held.at[r // 2, :, lo:hi]
            goes = pltpu.make_async_remote_copy(
                src_ref=slot,
                dst_ref=whole.at[b ^ r],
                send_sem=send_sems.at[i, r // 2],
                recv_sem=recv_sems.at[i, r // 2],
                device_id=other,
                device_id_type=MESH,
            )
            stays = pltpu.make_async_copy(slot, whole.at[b ^ r], sems_out.at[i, r // 2])
            goes.start()
            stays.start()
            waits += [goes, stays]
    for copy in waits:
        copy.wait()


def assemble(parts, widths, collective_id):
    names = tuple(parts)
    k, n = parts[(0, 0)].shape
    cuts = tuple((sum(widths[:i]), sum(widths[: i + 1])) for i in range(len(widths)))
    hbm = pl.BlockSpec(memory_space=pl.ANY)
    dma = pltpu.SemaphoreType.DMA
    wholes = pl.pallas_call(
        functools.partial(assemble_kernel, names, cuts),
        in_specs=[hbm] * len(names),
        out_specs=[hbm] * len(cuts),
        out_shape=[jax.ShapeDtypeStruct((8, k, width), BF16) for width in widths],
        scratch_shapes=[pltpu.VMEM((4, k, n), BF16), dma((len(names),)), dma((len(cuts), 4))]
        + [dma((len(cuts), 4)), dma((len(cuts), 4))],
        compiler_params=pltpu.CompilerParams(
            collective_id=collective_id, has_side_effects=True, vmem_limit_bytes=40 << 20
        ),
        cost_estimate=pl.CostEstimate(flops=0, bytes_accessed=32 * k * n, transcendentals=0),
        name="assemble",
    )(*[parts[name] for name in names])
    return [whole.reshape(8 * k, -1) for whole in wholes]


class Gather(Staged):
    def __init__(self, block, shard=None):
        self.block, self.shard = block, shard
        self.columns = None if shard is None else FromCtx(shard)
        super().__init__({(0, 0): block} if shard is None else self.columns.live)

    def step(self):
        if lax.axis_size("batch") != 8:
            return
        if self.columns:
            if self.columns.stage < len(bits_of("ctx")):
                self.columns.live, self.columns.fresh = self.live, []
                self.columns.step()
                self.live, self.fresh = self.columns.live, self.columns.fresh
                return
            self.columns.live = self.live
            self.live = {(0, 0): jnp.concatenate(from_ctx(self.columns.finish()), axis=1)}
            self.columns, self.fresh = None, []
        live, block = self.live, self.live[(0, 0)]
        if self.stage == 0:
            for bit in (2, 4):
                self.fly((bit, 0), permute_bit(block, "batch", bit))
        elif self.stage == 1:
            n = block.shape[1]
            half = n // 2 // LANE * LANE
            self.fly((6, 0), permute_bit(live[(2, 0)][:, :half], "batch", 4))
            self.fly((6, half), permute_bit(live[(4, 0)][:, half:], "batch", 2))
        self.stage += 1

    def whole(self, collective_id, *widths):
        if lax.axis_size("batch") == 8:
            return assemble(self.live, widths, collective_id)
        block = self.block
        if self.shard is not None:
            block = jnp.concatenate(list(gather_columns(self.shard)), axis=1)
        whole = gather_rows(block)
        return jnp.split(whole, [sum(widths[:i]) for i in range(1, len(widths))], axis=1)


def ctx_terms(own, columns):
    nctx, mine = lax.axis_size("ctx"), lax.axis_index("ctx")
    at, cuts = 0, []
    for n in columns:
        cuts.append([own[:, at + c * n : at + (c + 1) * n] for c in range(nctx)])
        at += nctx * n
    parts = [jnp.concatenate(cut, axis=1) if len(cut) > 1 else cut[0] for cut in zip(*cuts)]
    blocks = {}
    for r in range(nctx):
        blocks[r] = parts[0]
        for c in range(1, nctx):
            blocks[r] = jnp.where(mine ^ r == c, parts[c], blocks[r])
    return ToCtx(blocks)


class Scatter(Staged):
    def __init__(self, left, right, *columns, trim=None):
        count = lax.axis_size("batch")
        super().__init__({})
        self.columns, self.trim = columns, trim
        self.tall, self.right = left.T.reshape(count, -1, left.shape[0]), right
        self.arrived = {}
        self.spread = None

    def rows_of(self, which):
        mine = lax.axis_index("batch")
        return jnp.concatenate(
            [lax.dynamic_index_in_dim(self.tall, mine ^ r, 0, keepdims=False) for r in which], axis=0
        )

    def part(self, which, lo, hi):
        k = self.tall.shape[1]
        own = matmul(self.rows_of(which), self.right[:, lo:hi])
        for key, order in self.arrived.items():
            if key[0] in (lo, -1):
                off = lo if key[0] == -1 else 0
                pieces = [
                    self.live[key][
                        order.index(r) * k : (order.index(r) + 1) * k, off : off + hi - lo
                    ]
                    for r in which
                ]
                own = own + jnp.concatenate(pieces, axis=0).astype(F32)
        return own

    def step(self):
        stage = self.stage
        self.stage += 1
        count, bits = lax.axis_size("batch"), bits_of("batch")
        n = self.right.shape[1]
        cut = n // 2 // LANE * LANE
        halves = ((0, cut, bits[1:]), (cut, n, bits[:0:-1]))
        if self.stage > len(bits) + 1 and not self.spread:
            return
        if count != 8 and stage <= len(bits):
            self.stage = len(bits) + 1
            whole = matmul(self.tall.reshape(-1, self.tall.shape[2]), self.right).astype(BF16)
            own = lax.psum_scatter(whole, "batch", scatter_dimension=0, tiled=True)
            self.live = {"own": self.trim(own) if self.trim else own}
            if self.columns:
                self.to_ctx(self.live["own"])
        elif stage == 0:
            odd = [r for r in range(count) if r & 1]
            sent = matmul(self.rows_of(odd), self.right).astype(BF16)
            self.fly((-1, 0), permute_bit(sent, "batch", 1))
            self.arrived[(-1, 0)] = [r ^ 1 for r in odd]
        elif stage < len(bits):
            fresh = {}
            for lo, hi, order in halves:
                gone, bit = sum(order[: stage - 1]), order[stage - 1]
                which = [r for r in range(count) if not r & (gone | 1) and r & bit]
                fresh[(lo, stage)] = permute_bit(self.part(which, lo, hi).astype(BF16), "batch", bit)
                self.arrived[(lo, stage)] = [r ^ bit for r in which]
            for key, value in fresh.items():
                self.fly(key, value)
        elif stage == len(bits):
            own = jnp.concatenate([self.part([0], lo, hi) for lo, hi, _ in halves], axis=1)
            own = own.astype(BF16)
            self.live, self.fresh = {"own": self.trim(own) if self.trim else own}, []
            if self.columns:
                self.to_ctx(self.live["own"])
                self.step()
        elif self.spread:
            self.spread.live, self.spread.fresh = self.live, []
            self.spread.step()
            self.live, self.fresh = self.spread.live, self.spread.fresh

    def to_ctx(self, own):
        self.spread = ctx_terms(own, self.columns)
        self.live, self.fresh = self.spread.live, []

    def finished(self):
        while self.stage <= len(bits_of("batch")):
            self.step()
        return self.live["own"]

    def result(self):
        while self.stage <= len(bits_of("batch")) or not self.spread:
            self.step()
        self.spread.live = self.live
        total, out = self.spread.result(), []
        for n in self.columns:
            at = sum(v.shape[1] for v in out)
            out.append(total[:, at : at + n])
        return out


def reduce_kernel(n_parts, items, program, *refs):
    n = len(items)
    plain = [i for i, pieces in enumerate(items) if not pieces]
    terms, refs = refs[:n], refs[n:]
    outs, refs = refs[: n_parts + len(plain)], refs[n_parts + len(plain) :]
    accs, refs = refs[:n], refs[n:]
    firsts, refs = refs[:n], refs[n:]
    seconds, refs = refs[:n], refs[n:]
    thirds, refs = refs[:n], refs[n:]
    parts, refs = refs[:n_parts], refs[n_parts:]
    lands, sems = refs[: n_parts + len(plain)], refs[n_parts + len(plain) :]
    load, b_send, b_recv, z_send, z_recv = sems
    nctx = lax.axis_size("ctx")
    b, c = lax.axis_index("batch"), lax.axis_index("ctx")

    barrier = pltpu.get_barrier_semaphore()
    peers = [{"ctx": c ^ r} for r in range(1, nctx)] + [{"batch": b ^ bit} for bit in (1, 2, 4)]
    for device in peers:
        pl.semaphore_signal(barrier, inc=1, device_id=device, device_id_type=MESH)
    pl.semaphore_wait(barrier, len(peers))

    started = []

    def remote(source, target, send_sem, recv_sem, device):
        copy = pltpu.make_async_remote_copy(
            src_ref=source,
            dst_ref=target,
            send_sem=send_sem,
            recv_sem=recv_sem,
            device_id=device,
            device_id_type=MESH,
        )
        copy.start()
        started.append(copy)
        return copy

    def send(item, slot, source, target, bit):
        return remote(
            source, target, b_send.at[item, slot], b_recv.at[item, slot], {"batch": b ^ bit}
        )

    def halves(item):
        width = accs[item].shape[2]
        cut = width // 2 // LANE * LANE
        return (0, cut), (cut, width)

    def add(to, j, other, i, lo, hi):
        def rows(start, count):
            at = pl.ds(start, count)
            total = to[j, at, lo:hi].astype(F32) + other[i, at, lo:hi].astype(F32)
            to[j, at, lo:hi] = total.astype(BF16)

        copy_rows(to.shape[1], rows)

    flights, z_flights = {}, {}

    def begin(item):
        copies = []
        for j in range(4):
            own = pltpu.make_async_copy(terms[item].at[b ^ (2 * j)], accs[item].at[j], load.at[item, j])
            own.start()
            copies.append(own)
        for j in range(4):
            copies.append(send(item, j, terms[item].at[b ^ (2 * j + 1)], firsts[item].at[j], 1))
        flights[item] = copies

    def sub(ref, j, span):
        return ref.at[j, :, span[0] : span[1]]

    def first(item):
        acc, flight = accs[item], flights[item]
        left, right = halves(item)
        for j in (3, 1, 2, 0):
            flight[j].wait()
            flight[4 + j].wait_recv()
            add(acc, j, firsts[item], j, 0, acc.shape[2])
            if j == 1:
                after = [
                    send(item, 4, sub(acc, 1, left), sub(seconds[item], 0, left), 2),
                    send(item, 5, sub(acc, 3, left), sub(seconds[item], 1, left), 2),
                ]
            if j == 2:
                after += [
                    send(item, 6, sub(acc, 2, right), sub(seconds[item], 0, right), 4),
                    send(item, 7, sub(acc, 3, right), sub(seconds[item], 1, right), 4),
                ]
        flights[item] = after

    def second(item):
        acc, flight = accs[item], flights[item]
        left, right = halves(item)
        flight[1].wait_recv()
        add(acc, 2, seconds[item], 1, *left)
        after = [send(item, 8, sub(acc, 2, left), sub(thirds[item], 0, left), 4)]
        flight[3].wait_recv()
        add(acc, 1, seconds[item], 1, *right)
        after.append(send(item, 9, sub(acc, 1, right), sub(thirds[item], 0, right), 2))
        flight[0].wait_recv()
        flight[2].wait_recv()
        add(acc, 0, seconds[item], 0, 0, acc.shape[2])
        flights[item] = after

    def third(item):
        acc = accs[item]
        for copy in flights[item]:
            copy.wait_recv()
        add(acc, 0, thirds[item], 0, 0, acc.shape[2])
        if items[item]:

            def relay(start, count):
                at = pl.ds(start, count)
                for part, place, lo, hi, col in items[item]:
                    parts[part][place, at, lo:hi] = acc[0, at, col : col + hi - lo]

            copy_rows(acc.shape[1], relay)
        else:
            slot = n_parts + plain.index(item)
            land = lands[slot]

            def keep(start, count):
                land[c, pl.ds(start, count), :] = acc[0, pl.ds(start, count), :]

            copy_rows(acc.shape[1], keep)
            z_flights[slot] = [
                remote(
                    acc.at[0], land.at[c], z_send.at[slot, r], z_recv.at[slot, r], {"ctx": c ^ r}
                )
                for r in range(1, nctx)
            ]

    def spread(part):
        z_flights[part] = [
            remote(
                parts[part].at[c ^ r],
                lands[part].at[r],
                z_send.at[part, r],
                z_recv.at[part, r],
                {"ctx": c ^ r},
            )
            for r in range(1, nctx)
        ]

    def finish(slot):
        land, out = lands[slot], outs[slot]
        for copy in z_flights[slot]:
            copy.wait_recv()

        def rows(start, count):
            at = pl.ds(start, count)
            first = parts[slot][c, at, :] if slot < n_parts else land[0, at, :]
            total = first.astype(F32)
            for r in range(1, nctx):
                total = total + land[r, at, :].astype(F32)
            out[at, :] = total

        copy_rows(out.shape[0], rows)

    acts = {"b": begin, "f": first, "s": second, "t": third, "p": spread, "e": finish}
    for act, which in program:
        acts[act](which)
    for copy in started:
        copy.wait_send()


def reduce_all(terms, items, widths, program, collective_id):
    nctx, nbatch = lax.axis_size("ctx"), lax.axis_size("batch")
    plain = [i for i, pieces in enumerate(items) if not pieces]
    rows = {piece[0]: terms[i].shape[0] // nbatch for i, ps in enumerate(items) for piece in ps}
    if nbatch != 8:
        sums = [lax.psum_scatter(t, "batch", scatter_dimension=0, tiled=True) for t in terms]
        out = []
        for part, n in enumerate(widths):
            whole = jnp.zeros((rows[part], nctx, n), BF16)
            for i, pieces in enumerate(items):
                for at_part, place, lo, hi, col in pieces:
                    if at_part == part:
                        whole = whole.at[:, place, lo:hi].set(sums[i][:, col : col + hi - lo])
            out.append(lax.psum_scatter(whole, "ctx", scatter_dimension=1).astype(F32))
        return out + [lax.psum(sums[i], "ctx").astype(F32) for i in plain]
    terms = [t.reshape(nbatch, -1, t.shape[1]) for t in terms]
    sizes = [t.shape[1:] for t in terms]
    shapes = [(rows[part], n) for part, n in enumerate(widths)] + [sizes[i] for i in plain]
    dma = pltpu.SemaphoreType.DMA
    return pl.pallas_call(
        functools.partial(reduce_kernel, len(widths), tuple(items), program),
        in_specs=[pl.BlockSpec(memory_space=pl.ANY)] * len(terms),
        out_specs=[pl.BlockSpec(memory_space=pltpu.VMEM)] * len(shapes),
        out_shape=[jax.ShapeDtypeStruct(shape, F32) for shape in shapes],
        scratch_shapes=[pltpu.VMEM((count,) + size, BF16) for count in (4, 4, 2, 1) for size in sizes]
        + [pltpu.VMEM((nctx,) + shape, BF16) for shape in shapes[: len(widths)]]
        + [pltpu.VMEM((nctx,) + shape, BF16) for shape in shapes]
        + [dma((len(terms), 4)), dma((len(terms), 10)), dma((len(terms), 10))]
        + [dma((len(shapes), nctx)), dma((len(shapes), nctx))],
        compiler_params=pltpu.CompilerParams(
            collective_id=collective_id, has_side_effects=True, vmem_limit_bytes=62 << 20
        ),
        name="reduce_gradients",
    )(*terms)


def wide(tile, width):
    return jnp.concatenate([tile] * (width // LANE), axis=1)


def fold(value):
    parts = [value[:, at : at + LANE] for at in range(0, value.shape[1], LANE)]
    return functools.reduce(jnp.add, parts)


SCAN_WIDTH = 640
SCAN_PART = 384
UNROLL = 8


def scan_parts(width):
    return [(lo, min(width, lo + SCAN_PART)) for lo in range(0, width, SCAN_PART)]


def scan_specs(seqs, span, chan):
    pos = pl.BlockSpec((1, span, SCAN_WIDTH), lambda s, e: (s, 0, e))
    coef = pl.BlockSpec((1, span, STATE, LANE), lambda s, e: (s, 0, 0, 0))
    dec = pl.BlockSpec((STATE, SCAN_WIDTH), lambda s, e: (0, e))
    state = pl.BlockSpec((1, STATE, SCAN_WIDTH), lambda s, e: (s, 0, e))
    return pos, coef, dec, state


def scan_params():
    return pltpu.CompilerParams(vmem_limit_bytes=56 << 20)


def scan_cost(seqs, span, chan, ops):
    cells = seqs * span * chan * STATE
    return pl.CostEstimate(flops=cells * ops, bytes_accessed=seqs * span * chan * 16, transcendentals=cells)


def final_kernel(step_ref, xc_ref, b_ref, dec_ref, fin_ref, drive):
    span, width = step_ref.shape[1:]
    drive[...] = step_ref[0] * xc_ref[0]
    for lo, hi in scan_parts(width):
        dec = dec_ref[:, lo:hi]

        def body(i, h):
            for j in range(UNROLL):
                t = i * UNROLL + j
                f = jnp.exp2(step_ref[0, pl.ds(t, 1), lo:hi] * dec)
                h = f * h + drive[pl.ds(t, 1), lo:hi] * wide(b_ref[0, t], hi - lo)
            return h

        fin_ref[0, :, lo:hi] = lax.fori_loop(
            0, span // UNROLL, body, jnp.zeros((STATE, hi - lo), F32)
        )


def scan_final(steps, xc, bb, dec):
    seqs, span, chan = steps.shape
    pos, coef, decs, state = scan_specs(seqs, span, chan)
    return pl.pallas_call(
        final_kernel,
        grid=(seqs, chan // SCAN_WIDTH),
        in_specs=[pos, pos, coef, decs],
        out_specs=state,
        out_shape=jax.ShapeDtypeStruct((seqs, STATE, chan), F32),
        scratch_shapes=[pltpu.VMEM((span, SCAN_WIDTH), F32)],
        compiler_params=scan_params(),
        cost_estimate=scan_cost(seqs, span, chan, 6),
        name="scan_final",
    )(steps, xc, bb, dec)


def out_kernel(step_ref, xc_ref, b_ref, c_ref, dec_ref, entry_ref, y_ref, drive):
    span, width = step_ref.shape[1:]
    drive[...] = step_ref[0] * xc_ref[0]
    for lo, hi in scan_parts(width):
        dec = dec_ref[:, lo:hi]

        def body(i, h):
            rows = []
            for j in range(UNROLL):
                t = i * UNROLL + j
                f = jnp.exp2(step_ref[0, pl.ds(t, 1), lo:hi] * dec)
                h = f * h + drive[pl.ds(t, 1), lo:hi] * wide(b_ref[0, t], hi - lo)
                rows.append(jnp.sum(h * wide(c_ref[0, t], hi - lo), axis=0, keepdims=True))
            at = pl.multiple_of(i * UNROLL, UNROLL)
            y_ref[0, pl.ds(at, UNROLL), lo:hi] = jnp.concatenate(rows, axis=0)
            return h

        lax.fori_loop(0, span // UNROLL, body, entry_ref[0, :, lo:hi])


def scan_out_of(steps, xc, bb, cc, dec, entry):
    seqs, span, chan = steps.shape
    pos, coef, decs, state = scan_specs(seqs, span, chan)
    return pl.pallas_call(
        out_kernel,
        grid=(seqs, chan // SCAN_WIDTH),
        in_specs=[pos, pos, coef, coef, decs, state],
        out_specs=pos,
        out_shape=jax.ShapeDtypeStruct((seqs, span, chan), F32),
        scratch_shapes=[pltpu.VMEM((span, SCAN_WIDTH), F32)],
        compiler_params=scan_params(),
        cost_estimate=scan_cost(seqs, span, chan, 10),
        name="scan_out",
    )(steps, xc, bb, cc, dec, entry)


def adjoint_kernel(step_ref, gy_ref, c_ref, dec_ref, out_ref):
    span, width = step_ref.shape[1:]
    for lo, hi in scan_parts(width):
        dec = dec_ref[:, lo:hi]

        def body(i, g):
            for j in range(UNROLL):
                t = span - 1 - (i * UNROLL + j)
                f = jnp.exp2(step_ref[0, pl.ds(t, 1), lo:hi] * dec)
                g = f * (g + gy_ref[0, pl.ds(t, 1), lo:hi] * wide(c_ref[0, t], hi - lo))
            return g

        out_ref[0, :, lo:hi] = lax.fori_loop(
            0, span // UNROLL, body, jnp.zeros((STATE, hi - lo), F32)
        )


def scan_adjoint(steps, gy, cc, dec):
    seqs, span, chan = steps.shape
    pos, coef, decs, state = scan_specs(seqs, span, chan)
    return pl.pallas_call(
        adjoint_kernel,
        grid=(seqs, chan // SCAN_WIDTH),
        in_specs=[pos, pos, coef, decs],
        out_specs=state,
        out_shape=jax.ShapeDtypeStruct((seqs, STATE, chan), F32),
        compiler_params=scan_params(),
        cost_estimate=scan_cost(seqs, span, chan, 6),
        name="scan_adjoint",
    )(steps, gy, cc, dec)


def back_kernel(
    step_ref, xc_ref, gy_ref, b_ref, c_ref, dec_ref, entry_ref, arrive_ref,
    dxc_ref, dstep_ref, db_ref, dc_ref, ddec_ref, drive, hs, fs,
):
    span, width = step_ref.shape[1:]
    drive[...] = step_ref[0] * xc_ref[0]

    @pl.when(pl.program_id(1) == 0)
    def _():
        db_ref[...] = jnp.zeros_like(db_ref)
        dc_ref[...] = jnp.zeros_like(dc_ref)

    for lo, hi in scan_parts(width):
        n = hi - lo
        dec = dec_ref[:, lo:hi]

        def ahead(i, h):
            for j in range(UNROLL):
                t = i * UNROLL + j
                f = jnp.exp2(step_ref[0, pl.ds(t, 1), lo:hi] * dec)
                hs[t, :, :n] = h
                fs[t, :, :n] = f
                h = f * h + drive[pl.ds(t, 1), lo:hi] * wide(b_ref[0, t], n)
            return h

        last = lax.fori_loop(0, span // UNROLL, ahead, entry_ref[0, :, lo:hi])

        def back(i, carry):
            g, h, ddec = carry
            weighted, along = [], []
            for j in range(UNROLL):
                t = span - 1 - (i * UNROLL + j)
                gy = gy_ref[0, pl.ds(t, 1), lo:hi]
                g = g + gy * wide(c_ref[0, t], n)
                dc_ref[0, t] += fold(gy * h)
                db_ref[0, t] += fold(g * drive[pl.ds(t, 1), lo:hi])
                weighted.append(jnp.sum(g * wide(b_ref[0, t], n), axis=0, keepdims=True))
                g = g * fs[t, :, :n]
                h = hs[t, :, :n]
                m = g * h
                along.append(jnp.sum(m * dec, axis=0, keepdims=True))
                ddec = ddec + m * step_ref[0, pl.ds(t, 1), lo:hi]
            at = pl.multiple_of(span - (i + 1) * UNROLL, UNROLL)
            w8 = jnp.concatenate(weighted[::-1], axis=0)
            m8 = jnp.concatenate(along[::-1], axis=0)
            dxc_ref[0, pl.ds(at, UNROLL), lo:hi] = w8 * step_ref[0, pl.ds(at, UNROLL), lo:hi]
            dstep_ref[0, pl.ds(at, UNROLL), lo:hi] = (
                m8 * LN2 + w8 * xc_ref[0, pl.ds(at, UNROLL), lo:hi]
            )
            return g, h, ddec

        start = (arrive_ref[0, :, lo:hi], last, jnp.zeros((STATE, n), F32))
        ddec_ref[0, :, lo:hi] = lax.fori_loop(0, span // UNROLL, back, start)[2]


def scan_back(steps, xc, gy, bb, cc, dec, entry, arrive):
    seqs, span, chan = steps.shape
    pos, coef, decs, state = scan_specs(seqs, span, chan)
    by_pos = jax.ShapeDtypeStruct((seqs, span, chan), F32)
    by_coef = jax.ShapeDtypeStruct((seqs, span, STATE, LANE), F32)
    return pl.pallas_call(
        back_kernel,
        grid=(seqs, chan // SCAN_WIDTH),
        in_specs=[pos, pos, pos, coef, coef, decs, state, state],
        out_specs=[pos, pos, coef, coef, state],
        out_shape=[by_pos, by_pos, by_coef, by_coef, jax.ShapeDtypeStruct((seqs, STATE, chan), F32)],
        scratch_shapes=[pltpu.VMEM((span, SCAN_WIDTH), F32)]
        + [pltpu.VMEM((span, STATE, SCAN_PART), F32)] * 2,
        compiler_params=scan_params(),
        cost_estimate=scan_cost(seqs, span, chan, 24),
        name="scan_back",
    )(steps, xc, gy, bb, cc, dec, entry, arrive)


def attend_mask(place_ref, mask):
    span = mask.shape[0]
    row = lax.broadcasted_iota(jnp.int32, (span, span), 0) + place_ref[0]
    col = lax.broadcasted_iota(jnp.int32, (span, span), 1)
    for at in range(mask.shape[1] // span):
        apart = row - (col + place_ref[at])
        allowed = (apart >= 0) & (apart < WINDOW)
        mask[:, at * span : (at + 1) * span] = jnp.where(allowed, 0.0, -1e30)


def first_step():
    return (pl.program_id(0) == 0) & (pl.program_id(1) == 0)


def scores_of(q, k):
    return lax.dot_general(q, k, (((1,), (1,)), ((), ())), preferred_element_type=F32)


QWIDE = -(-GROUP * HD // LANE) * LANE
KWIDE = -(-KV * HD // LANE) * LANE


def heads_in(k_refs, v_refs, k_all, v_all):
    span, at = v_refs[0].shape[2], 0
    for k_ref, v_ref in zip(k_refs, v_refs):
        for i in range(v_ref.shape[0]):
            v_all[at : at + span, :] = v_ref[i, 0]
            for h in range(KV):

                @pl.when(pl.program_id(1) == h)
                def _(k_ref=k_ref, i=i, at=at, h=h):
                    k_all[at : at + span, :] = k_ref[i, 0, :, h * HD : (h + 1) * HD]

            at += span


def attend_kernel(n, place_ref, q_ref, *refs):
    k_refs, v_refs, (out_ref, mask, k_all, v_all) = refs[:n], refs[n : 2 * n], refs[2 * n :]
    pl.when(first_step())(lambda: attend_mask(place_ref, mask))
    heads_in(k_refs, v_refs, k_all, v_all)
    for g in range(GROUP):
        s = scores_of(q_ref[0, :, g * HD : (g + 1) * HD], k_all[...]) + mask[...]
        e = jnp.exp(s - jnp.max(s, axis=-1, keepdims=True))
        total = jnp.sum(e, axis=-1, keepdims=True)
        mixed = jnp.dot(e.astype(BF16), v_all[...], preferred_element_type=F32)
        out_ref[0, :, g * VHEAD : (g + 1) * VHEAD] = mixed / total


def attend_specs(span, kvs):
    q = pl.BlockSpec((1, span, QWIDE), lambda s, h: (s, 0, h))
    ks = [pl.BlockSpec((kv.shape[0], 1, span, KWIDE), lambda s, h: (0, s, 0, 0)) for kv in kvs]
    vs = [
        pl.BlockSpec((kv.shape[0], 1, span, VHEAD), lambda s, h: (0, s, 0, KWIDE // VHEAD + h))
        for kv in kvs
    ]
    out = pl.BlockSpec((1, span, GROUP * VHEAD), lambda s, h: (s, 0, h))
    length = span * sum(kv.shape[0] for kv in kvs)
    held = [
        pltpu.VMEM((span, length), F32),
        pltpu.VMEM((length, HD), BF16),
        pltpu.VMEM((length, VHEAD), BF16),
    ]
    return [pl.BlockSpec(memory_space=pltpu.SMEM), q] + ks + vs, q, out, length, held


def attend(place_of, q, kvs):
    seqs, span, _ = q.shape
    ins, _, out, length, held = attend_specs(span, kvs)
    cells = seqs * HEADS * span * length
    return pl.pallas_call(
        functools.partial(attend_kernel, len(kvs)),
        grid=(seqs, KV),
        in_specs=ins,
        out_specs=out,
        out_shape=jax.ShapeDtypeStruct((seqs, span, INNER), F32),
        scratch_shapes=held,
        compiler_params=pltpu.CompilerParams(vmem_limit_bytes=50 << 20),
        cost_estimate=pl.CostEstimate(
            flops=cells * 2 * (HD + VHEAD), bytes_accessed=cells, transcendentals=cells
        ),
        name="attend",
    )(place_of, q, *kvs, *kvs)


def attend_back_kernel(n, place_ref, q_ref, *refs):
    k_refs, v_refs, refs = refs[:n], refs[n : 2 * n], refs[2 * n :]
    o_ref, do_ref, dq_ref, dk_ref, dv_ref, mask, k_all, v_all, dk_sum, dv_sum = refs
    pl.when(first_step())(lambda: attend_mask(place_ref, mask))
    heads_in(k_refs, v_refs, k_all, v_all)
    k, v = k_all[...], v_all[...]
    for g in range(GROUP):
        q = q_ref[0, :, g * HD : (g + 1) * HD]
        do = do_ref[0, :, g * VHEAD : (g + 1) * VHEAD]
        o = o_ref[0, :, g * VHEAD : (g + 1) * VHEAD]
        s = scores_of(q, k) + mask[...]
        e = jnp.exp(s - jnp.max(s, axis=-1, keepdims=True))
        p = e * (1.0 / jnp.sum(e, axis=-1, keepdims=True))
        dp = scores_of(do, v)
        ds = (p * (dp - jnp.sum(do.astype(F32) * o, axis=-1, keepdims=True))).astype(BF16)
        dq = jnp.dot(ds, k, preferred_element_type=F32).astype(BF16)
        dq_ref[0, :, g * HD : (g + 1) * HD] = dq * jnp.asarray(HD**-0.5, BF16)
        dv = lax.dot_general(do, p.astype(BF16), (((0,), (0,)), ((), ())), preferred_element_type=F32)
        dk = lax.dot_general(q, ds, (((0,), (0,)), ((), ())), preferred_element_type=F32)
        if g == 0:
            dk_sum[...] = dk
            dv_sum[...] = dv
        else:
            dk_sum[...] += dk
            dv_sum[...] += dv
    if QWIDE > GROUP * HD:
        dq_ref[0, :, GROUP * HD :] = jnp.zeros((dq_ref.shape[1], QWIDE - GROUP * HD), BF16)
    dv_ref[0] = dv_sum[...].T.astype(BF16)
    dk = dk_sum[...].T.astype(BF16)

    @pl.when(pl.program_id(1) == 0)
    def _():
        dk_ref[...] = jnp.zeros_like(dk_ref)

    for h in range(KV):

        @pl.when(pl.program_id(1) == h)
        def _(h=h):
            dk_ref[0, :, h * HD : (h + 1) * HD] = dk


def attend_back(place_of, q, kvs, o, do):
    seqs, span, _ = q.shape
    ins, qs, out, length, held = attend_specs(span, kvs)
    cells = seqs * HEADS * span * length
    return pl.pallas_call(
        functools.partial(attend_back_kernel, len(kvs)),
        grid=(seqs, KV),
        in_specs=ins + [out, out],
        out_specs=[
            qs,
            pl.BlockSpec((1, length, KWIDE), lambda s, h: (s, 0, 0)),
            pl.BlockSpec((1, length, VHEAD), lambda s, h: (s, 0, h)),
        ],
        out_shape=[
            jax.ShapeDtypeStruct(q.shape, BF16),
            jax.ShapeDtypeStruct((seqs, length, KWIDE), BF16),
            jax.ShapeDtypeStruct((seqs, length, KV * VHEAD), BF16),
        ],
        scratch_shapes=held + [pltpu.VMEM((HD, length), F32), pltpu.VMEM((VHEAD, length), F32)],
        compiler_params=pltpu.CompilerParams(vmem_limit_bytes=50 << 20),
        cost_estimate=pl.CostEstimate(
            flops=cells * 2 * (3 * HD + 2 * VHEAD), bytes_accessed=cells, transcendentals=cells
        ),
        name="attend_back",
    )(place_of, q, *kvs, *kvs, o, do)


def rms_scale(value):
    return lax.rsqrt(jnp.mean(value * value, axis=-1, keepdims=True) + EPS)


def norm_back(value, scale, upstream):
    return scale * upstream - value * scale**3 * jnp.mean(upstream * value, axis=-1, keepdims=True)


def silu_pair(value):
    sigma = jax.nn.sigmoid(value)
    return (value * sigma, sigma * (1.0 + value * (1.0 - sigma)))


def matmul(left, right):
    return jnp.dot(left, right, preferred_element_type=F32)


def matmul_back(left, right):
    return lax.dot_general(left, right, (((1,), (1,)), ((), ())), preferred_element_type=F32)


def outer_sum(left, right):
    return lax.dot_general(left, right, (((0,), (0,)), ((), ())), preferred_element_type=F32)


def carried(states, sums, dec, later):
    mine = lax.axis_index("ctx")
    total = jnp.zeros(states[0].shape, F32)
    for r in range(1, lax.axis_size("ctx")):
        far = mine ^ r
        passed = jnp.zeros(sums[0].shape, F32)
        for q in range(1, lax.axis_size("ctx")):
            at = mine ^ q
            between = (at > mine) & (at < far) if later else (at < mine) & (at > far)
            passed = passed + jnp.where(between, sums[q], 0.0)
        reaches = far > mine if later else far < mine
        total = total + jnp.where(reaches, jnp.exp2(dec * passed) * states[r].astype(F32), 0.0)
    return total


def per_device(
    tokens,
    teacher,
    cotangent,
    valid,
    w_query,
    w_key,
    w_value,
    w_mixer,
    w_output,
    w_gate,
    w_up,
    w_down,
    w_select,
    w_step,
    log_decay,
    conv_taps,
    conv_bias,
    step_bias,
    skip_gain,
    beta_attn,
    beta_ssm,
    gain_first,
    gain_second,
):
    seqs, span, width = tokens.shape
    nctx, nbatch = lax.axis_size("ctx"), lax.axis_size("batch")
    rows = seqs * span
    scale = 1.0 / math.sqrt(HD)
    all_tokens = rows * nbatch * nctx
    order = [0]
    for bit in bits_of("ctx")[::-1]:
        order += [r ^ bit for r in order]
    place_of = jnp.stack([(lax.axis_index("ctx") ^ r) * span for r in order]).astype(jnp.int32)

    lines = jnp.concatenate(
        [w_step, log_decay, conv_taps]
        + [v[None] for v in (conv_bias, step_bias, skip_gain, beta_attn, beta_ssm)]
        + [w_select.T],
        axis=0,
    )
    n_lines, chan = lines.shape
    gains = jnp.stack([gain_first, gain_second])
    packed = jnp.concatenate(
        [lines, jnp.pad(gains, ((0, 0), (0, chan - gains.shape[1])))], axis=0
    )
    packed = jnp.pad(packed, ((0, -packed.shape[0] % 16), (0, -chan % (2 * LANE))))
    n_q, n_k, n_v, n_mixer = [w.shape[1] for w in (w_query, w_key, w_value, w_mixer)]
    ff = nctx * w_gate.shape[1]
    every, half = range(nctx), nctx // 2
    here = jnp.full((8, LANE), jnp.sum(valid.astype(F32)))
    shards = [w_query, w_key, w_value, w_mixer, w_output, w_gate, w_up, here]
    in_kv = pieces_of(1, n_k, every) + pieces_of(2, n_v, every, KWIDE)
    items = [
        packed,
        (in_kv, KWIDE + KV * VHEAD, True),
        (pieces_of(0, n_q, every, 0, GROUP * HD, QWIDE), KV * QWIDE, True),
        (pieces_of(3, n_mixer, range(half)), INNER, True),
        (pieces_of(3, n_mixer, range(half, nctx)), INNER, True),
        (pieces_of(4, w_output.shape[1], every), D, False),
        (
            pieces_of(5, w_gate.shape[1], every) + pieces_of(6, w_up.shape[1], every, ff),
            2 * ff,
            False,
        ),
        (pieces_of(7, LANE, every), nctx * LANE, True),
    ]
    program = (
        "c1 c2 c0 c7 l0 c1 c2 l1 c0 c7 c3 l2 l7 c5 c3 f0 c6 l3 l4 f1 f2 f7 e0 c5 c4 f3 c6 e1 e2 "
        "e7 c4 l6 f4 l5 e3 e4"
    )
    acts = {"c": "columns", "l": "launch", "f": "forward", "e": "last"}
    program = tuple((acts[word[0]], int(word[1:])) for word in program.split())
    f_packed, f_kv, f_q, f_conv, f_z, row_output, row_gate_up, counts = gather_all(
        shards, items, program, 0
    )
    f_kv, f_q, f_conv, f_z = [v.reshape(-1, v.shape[2]) for v in (f_kv, f_q, f_conv, f_z)]
    count = jnp.sum(counts[:, 0, ::LANE])
    get_output, get_gate_up = Gather(row_output), Gather(row_gate_up)
    get_down = Gather(None, w_down)
    f_conv = hold([get_down], f_conv)
    f_vectors = f_packed[:, :n_lines, :chan].transpose(1, 0, 2).reshape(n_lines, nbatch * chan)
    f_select = f_vectors[RANK + STATE + CONV + 5 :].T
    f_gains = f_packed[:, n_lines : n_lines + 2, : gains.shape[1]]
    f_gains = f_gains.transpose(1, 0, 2).reshape(2, -1)

    f_step = f_vectors[:RANK]
    f_decay = f_vectors[RANK : RANK + STATE].astype(F32)
    taps = f_vectors[RANK + STATE : RANK + STATE + CONV].astype(F32)
    f_conv_bias, f_step_bias, skip, beta_a, beta_s = [
        f_vectors[RANK + STATE + CONV + i].astype(F32) for i in range(5)
    ]
    gain_one, gain_two = f_gains[0].astype(F32), f_gains[1].astype(F32)
    decay = -jnp.exp(f_decay)
    dec = decay * LOG2E

    get_gate_up.step()
    x_flat = tokens.reshape(rows, D).astype(F32)
    scale1 = rms_scale(x_flat)
    normed1 = (x_flat * scale1 * gain_one).astype(BF16)
    conv_in = matmul(normed1, f_conv).astype(BF16).reshape(seqs, span, INNER)
    rim = shift(conv_in[:, span - (CONV - 1) :], "ctx", 1, False)
    conv_in, then1 = hold([], conv_in, normed1)
    kv_own = matmul(then1, f_kv).astype(BF16).reshape(seqs, span, KWIDE + KV * VHEAD)
    get_kv = FromCtx(kv_own)
    get_kv.step()
    q_heads = (matmul(then1, f_q) * scale).astype(BF16).reshape(seqs, span, KV * QWIDE)
    gate_z = matmul(then1, f_z).reshape(seqs, span, INNER)
    extended = jnp.concatenate([rim, conv_in], axis=1).astype(F32)
    pre_conv = f_conv_bias + sum((taps[tap] * extended[:, tap : tap + span] for tap in range(CONV)))
    conv_out, conv_slope = silu_pair(pre_conv)
    conv_out = hold([get_gate_up, get_kv], conv_out)

    get_kv.step()
    get_gate_up.step()
    get_output.step()
    get_down.step()
    conv_low = conv_out.reshape(rows, INNER).astype(BF16)
    projected = matmul(conv_low, f_select)
    rank_low = projected[:, :RANK].astype(BF16)
    coefs = projected[:, RANK:].reshape(seqs, span, 2, STATE, 1)
    bb = jnp.broadcast_to(coefs[:, :, 0], (seqs, span, STATE, LANE))
    cc = jnp.broadcast_to(coefs[:, :, 1], (seqs, span, STATE, LANE))
    step_pre = matmul(rank_low, f_step) + f_step_bias
    steps = jax.nn.softplus(step_pre).reshape(seqs, span, INNER)
    step_sums = jnp.sum(steps, axis=1, keepdims=True)
    final = scan_final(steps, conv_out, bb, dec)
    final = hold([get_output, get_kv, get_gate_up, get_down], final)

    sums_high = step_sums.astype(BF16)
    sums_low = (step_sums - sums_high.astype(F32)).astype(BF16)
    get_state = FromCtx(jnp.concatenate([final.astype(BF16), sums_high, sums_low], axis=1))
    get_state.step()
    get_output.step()
    get_down.step()
    get_kv.finish()
    kvs = list(get_kv.live.values())
    attn = attend(place_of, q_heads, kvs).reshape(rows, INNER)
    attn = hold([get_state, get_output, get_down], attn)
    get_state.step()
    get_down.step()
    f_gate, f_up = hold([get_state], *get_gate_up.whole(2, ff, ff))

    states = get_state.finish()
    all_sums = {
        r: v[:, STATE : STATE + 1].astype(F32) + v[:, STATE + 1 :].astype(F32)
        for r, v in states.items()
    }
    entry = carried({r: v[:, :STATE] for r, v in states.items()}, all_sums, dec, False)
    scan_out = scan_out_of(steps, conv_out, bb, cc, dec, entry)
    (f_output,) = get_output.whole(1, D)
    scan_out, f_output = hold([get_down], scan_out, f_output)
    get_down.step()

    gate_act, gate_slope = silu_pair(gate_z)
    pre_gate = scan_out + skip * conv_out
    ssm_flat = (pre_gate * gate_act).reshape(rows, INNER)
    attn_scale = rms_scale(attn)
    attn_norm = attn * attn_scale
    ssm_scale = rms_scale(ssm_flat)
    ssm_norm = ssm_flat * ssm_scale
    merged = (0.5 * (attn_norm * beta_a + ssm_norm * beta_s)).astype(BF16)
    hidden1 = x_flat + matmul(merged, f_output)

    scale2 = rms_scale(hidden1)
    normed2 = (hidden1 * scale2 * gain_two).astype(BF16)
    gate_pre = matmul(normed2, f_gate)
    up_pre = matmul(normed2, f_up)
    gate_act2, gate_slope2 = silu_pair(gate_pre)
    inner_ff = (gate_act2 * up_pre).astype(BF16)
    (f_down,) = get_down.whole(3, D)
    hidden2 = hidden1 + matmul(inner_ff, f_down)
    output = hidden2.astype(BF16).reshape(seqs, span, D)
    weight_rows = valid.reshape(rows, 1).astype(F32)
    diff = hidden2 - teacher.reshape(rows, D).astype(F32)
    loss_local = jnp.sum(weight_rows * diff * diff)
    loss_sum = total_over(jnp.full((8, LANE), loss_local), ("batch", "ctx"))[0, 0]

    seed = cotangent.reshape(rows, D).astype(F32) + all_tokens / count * weight_rows * diff
    seed_low = seed.astype(BF16)
    put_down = Scatter(inner_ff, seed_low, w_down.shape[1])
    put_down.step()
    d_inner = matmul_back(seed_low, f_down)
    d_gate = (d_inner * up_pre * gate_slope2).astype(BF16)
    d_up = (d_inner * gate_act2).astype(BF16)
    d_gate, d_up = hold([put_down], d_gate, d_up)

    put_down.step()
    put_gate = Scatter(normed2, d_gate, w_gate.shape[1])
    put_gate.step()
    put_up = Scatter(normed2, d_up, w_up.shape[1])
    put_up.step()
    d_norm2 = matmul_back(d_gate, f_gate) + matmul_back(d_up, f_up)
    g_gain_second = jnp.sum(d_norm2 * hidden1 * scale2, axis=0, keepdims=True)
    d_hidden1 = seed + norm_back(hidden1, scale2, d_norm2 * gain_two)
    d_hidden1 = hold([put_down, put_gate, put_up], d_hidden1)

    put_down.step()
    put_gate.step()
    d_branch = d_hidden1.astype(BF16)
    put_output = Scatter(merged, d_branch, w_output.shape[1])
    put_output.step()
    d_merged = matmul_back(d_branch, f_output)
    g_beta_attn = jnp.sum(0.5 * d_merged * attn_norm, axis=0, keepdims=True)
    g_beta_ssm = jnp.sum(0.5 * d_merged * ssm_norm, axis=0, keepdims=True)
    d_attn = norm_back(attn, attn_scale, 0.5 * d_merged * beta_a).astype(BF16)
    d_ssm = norm_back(ssm_flat, ssm_scale, 0.5 * d_merged * beta_s).reshape(seqs, span, INNER)
    d_pre_gate = d_ssm * gate_act
    d_gate_z = (d_ssm * pre_gate * gate_slope).reshape(rows, INNER).astype(BF16)
    g_skip = jnp.sum(d_pre_gate * conv_out, axis=(0, 1))[None]
    adjoint = scan_adjoint(steps, d_pre_gate, cc, dec)
    d_attn, d_pre_gate, d_gate_z, adjoint = hold(
        [put_down, put_gate, put_output], d_attn, d_pre_gate, d_gate_z, adjoint
    )

    put_down.step()
    put_gate.step()
    put_up.step()
    get_adjoint = FromCtx(adjoint.astype(BF16))
    get_adjoint.step()
    dq, dk, dv = attend_back(
        place_of, q_heads, kvs, attn.reshape(seqs, span, INNER), d_attn.reshape(seqs, span, INNER)
    )
    dq, dk, dv = hold([put_down, put_gate, put_up, get_adjoint], dq, dk, dv)
    get_adjoint.step()
    put_down.step()
    put_gate.step()
    put_up.step()
    put_output.step()
    dq = dq.reshape(rows, KV * QWIDE)
    g_q = outer_sum(normed1, dq).astype(BF16)
    g_z = outer_sum(normed1, d_gate_z).astype(BF16)
    d_norm1 = matmul_back(dq, f_q) + matmul_back(d_gate_z, f_z)
    d_norm1, g_q, g_z = hold(
        [get_adjoint, put_down, put_gate, put_up, put_output], d_norm1, g_q, g_z
    )

    d_kv = jnp.concatenate([dk, dv], axis=-1).reshape(seqs, nctx, span, KWIDE + KV * VHEAD)
    put_kv = ToCtx({r: d_kv[:, i] for i, r in enumerate(order)})
    put_kv.step()
    put_gate.step()
    put_up.step()
    put_output.step()
    arrive = carried(get_adjoint.finish(), all_sums, dec, True)
    g_drive, g_steps, g_b, g_c, grad_decay = scan_back(
        steps, conv_out, d_pre_gate, bb, cc, dec, entry, arrive
    )
    g_drive, g_steps, g_b, g_c = hold(
        [put_gate, put_up, put_output, put_kv], g_drive, g_steps, g_b, g_c
    )

    put_kv.step()
    put_up.step()
    put_output.step()
    d_step_pre = g_steps.reshape(rows, INNER) * jax.nn.sigmoid(step_pre)
    g_step_bias = jnp.sum(d_step_pre, axis=0, keepdims=True)
    d_step_low = d_step_pre.astype(BF16)
    d_rank = matmul_back(d_step_low, f_step)
    d_projected = jnp.concatenate(
        [d_rank] + [jnp.sum(g, axis=-1).reshape(rows, STATE) for g in (g_b, g_c)], axis=1
    ).astype(BF16)
    d_conv = (
        g_drive
        + d_pre_gate * skip
        + matmul_back(d_projected, f_select).reshape(seqs, span, INNER)
    )
    d_pre_conv = hold([put_kv], d_conv * conv_slope)
    g_conv_bias = jnp.sum(d_pre_conv, axis=(0, 1))[None]
    g_taps = [
        jnp.sum(d_pre_conv * extended[:, tap : tap + span], axis=(0, 1))[None]
        for tap in range(CONV)
    ]
    d_extended = sum(
        (
            jnp.pad(taps[tap] * d_pre_conv, ((0, 0), (tap, CONV - 1 - tap), (0, 0)))
            for tap in range(CONV)
        )
    )
    back_rim = shift(d_extended[:, : CONV - 1].astype(BF16), "ctx", -1, False)
    d_conv_in = d_extended[:, CONV - 1 :].at[:, span - (CONV - 1) :].add(back_rim.astype(F32))
    d_conv_in = d_conv_in.reshape(rows, INNER).astype(BF16)
    d_conv_in = hold([put_output, put_up], d_conv_in)

    put_output.step()
    d_kv_own = put_kv.result().astype(BF16).reshape(rows, KWIDE + KV * VHEAD)
    d_norm1 = d_norm1 + matmul_back(d_kv_own, f_kv) + matmul_back(d_conv_in, f_conv)
    g_gain_first = jnp.sum(d_norm1 * x_flat * scale1, axis=0, keepdims=True)
    d_tokens = d_hidden1 + norm_back(x_flat, scale1, d_norm1 * gain_one)
    tokens_grad = d_tokens.astype(BF16).reshape(seqs, span, D)
    g_conv = outer_sum(normed1, d_conv_in).astype(BF16)
    g_kv = outer_sum(normed1, d_kv_own).astype(BF16)

    pad_rank, pad_sel = -RANK % 8, -(RANK + 2 * STATE) % 8
    g_step = outer_sum(jnp.pad(rank_low, ((0, 0), (0, pad_rank))), d_step_low)
    g_select = outer_sum(jnp.pad(d_projected, ((0, 0), (0, pad_sel))), conv_low)
    own_gain = D // nbatch
    gains_wide = [
        jnp.pad(g.reshape(nbatch, own_gain), ((0, 0), (0, chan - own_gain))).reshape(1, INNER)
        for g in (g_gain_first, g_gain_second)
    ]
    few = g_taps + [g_conv_bias, g_step_bias, g_skip, g_beta_attn, g_beta_ssm] + gains_wide
    few.append(jnp.zeros((-len(few) % 8, INNER), F32))
    at_sel = RANK + pad_rank
    at_dec = at_sel + RANK + 2 * STATE + pad_sel
    at_few = at_dec + STATE

    small = jnp.concatenate(
        [g_step, g_select, jnp.sum(grad_decay, axis=0) * decay] + few, axis=0
    ).astype(BF16)
    small = small.reshape(small.shape[0], nbatch, chan).transpose(1, 0, 2)
    small = jnp.pad(small, ((0, 0), (0, -small.shape[1] % 16), (0, -chan % (2 * LANE))))
    small = small.reshape(-1, small.shape[2])
    small = hold([put_output], small)
    terms = [g_conv, g_z, g_q, g_kv, small]
    items = [items[3][0], items[4][0], items[2][0], items[1][0], ()]
    program = "b4 b3 b2 b1 b0 f4 f3 f2 f1 s4 f0 s3 t4 s2 t3 p1 p2 t2 p0 s1 e4 t1 s0 t0 p3 e1 e2 e0 e3"
    program = tuple((word[0], int(word[1:])) for word in program.split())
    (r_down,), (r_gate,), (r_up,), (r_output,) = [
        put.result() for put in (put_down, put_gate, put_up, put_output)
    ]
    r_query, r_key, r_value, r_mixer, small = reduce_all(
        terms, items, (n_q, n_k, n_v, n_mixer), program, 4
    )
    small = small[:, :chan]
    return (
        output,
        loss_sum / (count * D),
        tokens_grad,
        r_query,
        r_key,
        r_value,
        r_mixer,
        r_output,
        r_gate,
        r_up,
        r_down,
        small[at_sel : at_sel + RANK + 2 * STATE].T,
        small[:RANK],
        small[at_dec:at_few],
        small[at_few : at_few + CONV],
        *[small[at_few + CONV + i] for i in range(5)],
        *[small[at_few + CONV + 5 + i, :own_gain] for i in range(2)],
    )


def solution(mesh):
    by_pos = P("batch", "ctx", None)
    by_both = P("batch", "ctx")
    by_row, by_col, by_one = P("batch", None), P(None, "batch"), P("batch")
    weights = (by_both,) * 8 + (by_row,) + (by_col,) * 3 + (by_one,) * 7
    return jax.shard_map(
        per_device,
        mesh=mesh,
        in_specs=(by_pos, by_pos, by_pos, by_both) + weights,
        out_specs=(by_pos, P(), by_pos) + weights,
        check_vma=False,
    )
```

time: 7460 us -> 1770 us (0.24)
  waiting for transfers between devices: 2910 us -> 97.8 us
  other arithmetic: 1870 us -> 182 us
  local copies, waits for them, and re-layouts: 1600 us -> 225 us
  Pallas kernels: 0 us -> 749 us
  blocking collectives: 326 us -> 0 us
  matrix products: 595 us -> 408 us
    unnamed x95 -> x0, waiting for transfers between devices: 2180 us -> none
    reduce_sum x679 -> x9, other arithmetic: 1020 us -> 50.5 us  [the longest x1 20 us: per_device(): jnp.sum(d_pre_conv * extended[:, tap:tap + span], axis=(0, 1))[None]]
    pallas_call x0 -> x11, Pallas kernels: none -> 749 us  [the longest x1 213 us: reduce_all(): pl.pallas_call(functools.partial(reduce_kernel, len(widths), tuple(items)...]
    another operation x696 -> x7, local copies, waits for them, and re-layouts: 659 us -> 7.13 us  [the longest x3 5.61 us: step(): sent = jnp.stack([self.total(r).astype(BF16) for r in which])]
    reduce_scatter x10 -> x0, waiting for transfers between devices: 491 us -> none  [the longest x2 316 us: per_device(): lax.psum_scatter(t_down.astype(jnp.bfloat16), 'batch', scatter_dimension=...]
    mul x323 -> x3, other arithmetic: 363 us -> 7.79 us  [the longest x1 6.44 us: per_device(): d_pre_conv = hold([put_kv], d_conv * conv_slope)]
    add x216 -> x15, other arithmetic: 363 us -> 19.7 us  [the longest x4 12.3 us: total(): return functools.reduce(jnp.add, terms)]
    squeeze x416 -> x8, local copies, waits for them, and re-layouts: 311 us -> 17.3 us  [the longest x4 9.83 us: step(): self.fly((r ^ bit, self.stage + 1), got[i])]
where the time goes in v1:
time: 1770 us; the launch traced here: 1750 us
  Pallas kernels  749 us (42%)
  matrix products  408 us (23%)
  local copies, waits for them, and re-layouts  225 us (13%)
  other arithmetic  182 us (10%)
  waiting for transfers between devices  97.8 us (6%)
  starting transfers between devices  85.4 us (5%)
    dot_general x38, matrix products, matmul(): return jnp.dot(left, right, preferred_element_type=F32)  259 us
    pallas_call x1, Pallas kernels, reduce_all(): pl.pallas_call(functools.partial(reduce_kernel, len(widths), tuple(items)...  213 us
    pallas_call x1, Pallas kernels, gather_all(): pl.pallas_call(functools.partial(gather_kernel, len(shards), tuple(kinds)...  189 us
    dot_general x10, matrix products, matmul_back(): lax.dot_general(left, right, (((1,), (1,)), ((), ())), preferred_element_...  113 us
    pallas_call x1, Pallas kernels, scan_back(): pl.pallas_call(back_kernel, grid=(seqs, chan // SCAN_WIDTH), in_specs=[po...  107 us
    ppermute x55, waiting for transfers between devices, permute_bit(): return lax.ppermute(value, axis, [(i, i ^ bit) for i in range(count)])  97.8 us
    ppermute x55, starting transfers between devices, permute_bit(): return lax.ppermute(value, axis, [(i, i ^ bit) for i in range(count)])  70.3 us
    pallas_call x1, Pallas kernels, attend_back(): pl.pallas_call(functools.partial(attend_back_kernel, len(kvs)), grid=(seq...  54.2 us
  transfers between devices with their start and end apart: 57, of which 10 were waited for; matrix products, arithmetic and copies ran while one was open for 34% of the time, Pallas kernels for 19%

profile of v1, /device:TPU:8, one launch (start us, length us, event | category | flops | bytes accessed | tf_op | source)
XLA Modules:
  0.0 1753.9 jit_solution(16905866204120822689)
XLA Ops:
  15.6 189.4 %gather_weights.1 = (bf16[8,272,512]{2,1,0:T(8,128)(2,1)}, bf16[8,200,1024]{2,1,0:T(8,128)(2,1)}, bf16[8,200,1920]{2,1,0:T(8,128)(2,1)}, bf16[8,200,3200]{2,1,0:...) custom-call(bf16[200,400]{1,0:T(8,128)(2,1)} %refs_0_.1, ...), custom_call_target="tpu_custom_call" | custom-call | tf_op jit(solution)/shard_map/gather_weights/pallas_call | solution.py:265
  273.8 29.6 %collective-permute-done.4.refs_1_.refs_4_ = bf16[1,2,256,1024]{3,2,1,0:T(8,128)(2,1)} collective-permute-done((bf16[1,2,256,1024]{3,2,1,0:T(8,128)(2,1)S(1)}, bf16[1,2,256,1024]{3,2,1,0:T(8,128)(2,1)}, u32[]{:S(2)}, u32[]{:S(2)}) %collective-permute-start.4) | collective-permute-done | bytes 1048608 | tf_op jit(solution)/shard_map/ppermute | solution.py:34
  374.1 26.7 %scan_final.1 = f32[2,16,3200]{2,1,0:T(8,128)} custom-call(f32[2,256,3200]{2,1,0:T(8,128)} %bitcast.484, f32[2,256,3200]{2,1,0:T(8,128)} %get-tuple-element.161.xc_ref, f32[2,256,16,128]{3,2,1,0:T(8,128)} %broadcast_in_dim.121.b_ref, f32[16,3200]{1,0:T(8,128)} %mul.594.dec_ref), custom_call_target="tpu_custom_call" | custom-call | flops 157286400 | bytes 26214400 | tf_op jit(solution)/shard_map/scan_final/pallas_call | solution.py:811
  424.2 31.5 %attend.1 = f32[2,256,3200]{2,1,0:T(8,128)} custom-call(s32[4]{0:T(128)S(1)} %pad_add_fusion.1.place_ref, bf16[2,256,1920]{2,1,0:T(8,128)(2,1)S(1)} %bitcast.380, bf16[1,2,256,1024]{3,2,1,0:T(8,128)(2,1)S(1)} %bitcast.375, bf16[1,2,256,1024]{3,2,1,0:T(8,128)(2,1)} %collective-permute-done.4.refs_1_.refs_4_, ...), custom_call_target="tpu_custom_call" | custom-call | flops 5033164800 | bytes 13107200 | tf_op jit(solution)/shard_map/attend/pallas_call | solution.py:1035
  455.8 27.3 %assemble.3 = (bf16[8,200,5504]{2,1,0:T(8,128)(2,1)}, bf16[8,200,5504]{2,1,0:T(8,128)(2,1)}) custom-call(bf16[200,11008]{1,0:T(8,128)(2,1)S(1)} %bitcast.372, bf16[200,11008]{1,0:T(8,128)(2,1)} %collective-permute-done.2.refs_1_, bf16[200,11008]{1,0:T(8,128)(2,1)} %collective-permute-done.3.refs_2_, bf16[200,5504]{1,0:T(8,128)(2,1)} %collective-permute-done.7.refs_3_, ...), custom_call_target="tpu_custom_call" | custom-call | bytes 70451200 | tf_op jit(solution)/shard_map/assemble/pallas_call | solution.py:393
  518.4 47.5 %scan_out.1 = f32[2,256,3200]{2,1,0:T(8,128)} custom-call(f32[2,256,3200]{2,1,0:T(8,128)} %bitcast.485, f32[2,256,3200]{2,1,0:T(8,128)} %get-tuple-element.161.xc_ref, f32[2,256,16,128]{3,2,1,0:T(8,128)} %broadcast_in_dim.121.b_ref, f32[2,256,16,128]{3,2,1,0:T(8,128)} %broadcast_in_dim.124.c_ref, f32[16,3200]{1,0:T(8,128)} %mul.594.dec_ref, ...), custom_call_target="tpu_custom_call" | custom-call | flops 262144000 | bytes 26214400 | tf_op jit(solution)/shard_map/scan_out/pallas_call | solution.py:847
  565.9 18.7 %multiply_reduce_fusion.8 = (f32[2,256]{1,0:T(2,128)S(1)}, f32[2,256,3200]{2,1,0:T(8,128)}, f32[2,256,3200]{2,1,0:T(8,128)}) fusion(f32[2,256,3200]{2,1,0:T(8,128)} %scan_out.1, f32[2,256,3200]{2,1,0:T(8,128)} %get-tuple-element.161.xc_ref, f32[3200]{0:T(1024)S(1)} %reshape.571, bf16[1600,3200,1]{1,0,2:T(8,128)(2,1)} %bitcast.478, ...), kind=kOutput, calls=%fused_computation.42 | convolution fusion | flops 5257625088 | bytes 38107648 | tf_op jit(solution)/shard_map/dot_general | solution.py:1132
  592.0 14.9 multiply_reduce_fusion.14
  613.2 17.0 fusion.227
  630.2 23.7 %fusion = (bf16[5504,512]{0,1:T(8,128)(2,1)}, f32[512,5504]{1,0:T(8,128)}) fusion(f32[512,5504]{1,0:T(8,128)} %fusion.227, bf16[512,1600]{0,1:T(8,128)(2,1)} %copy-done.64, bf16[1600,5504]{1,0:T(8,128)(2,1)} %bitcast.474), kind=kOutput, calls=%fused_computation.6 | convolution fusion | flops 9034661888 | bytes 47431680 | tf_op jit(solution)/shard_map/dot_general | solution.py:1132
  667.2 15.9 assemble.5
  683.1 24.5 %fusion.216 = (bf16[512,1600]{0,1:T(8,128)(2,1)}, f32[512,1600]{0,1:T(8,128)}, f32[]{:T(128)}, bf16[512,1600]{0,1:T(8,128)(2,1)}) fusion(f32[512,1600]{0,1:T(8,128)} %bitcast.432, f32[512,1600]{0,1:T(8,128)} %bitcast.431, f32[512]{0:T(512)S(1)} %copy-done.171, f32[512]{0:T(512)S(1)} %bitcast.464, f32[512,1600]{0,1:T(8,128)} %get-tuple-element.462, ...), kind=kOutput, calls=%fused_computation.446 | convolution fusion | flops 9042034688 | bytes 56545284 | tf_op jit(solution)/shard_map/dot_general | solution.py:1132
  741.9 27.6 %multiply_convert_fusion = (bf16[512,5504]{1,0:T(8,128)(2,1)}, bf16[512,5504]{1,0:T(8,128)(2,1)}) fusion(f32[512,5504]{1,0:T(8,128)} %fusion.227, f32[512,5504]{1,0:T(8,128)} %get-tuple-element.465, bf16[512,1600]{0,1:T(8,128)(2,1)} %get-tuple-element.372, bf16[5504,1600]{1,0:T(8,128)(2,1)} %bitcast.403), kind=kOutput, calls=%fused_computation.12 | convolution fusion | flops 9054388224 | bytes 53067776 | tf_op jit(solution)/shard_map/dot_general | solution.py:1136
  837.0 16.7 multiply_reduce_fusion.10
  858.2 13.0 collective-permute-done.25
  871.7 18.1 %multiply_reduce_fusion = (bf16[3200]{0:T(1024)(128)(2,1)S(1)}, f32[512]{0:T(512)S(1)}, f32[512]{0:T(512)S(1)}, bf16[3200]{0:T(1024)(128)(2,1)S(1)}, f32[512,3200]{1,0:T(8,128)}) fusion(f32[2,256,3200]{2,1,0:T(8,128)} %get-tuple-element.375, f32[512]{0:T(512)S(1)} %bitcast.461, f32[3200]{0:T(1024)S(1)} %get-tuple-element.470, f32[512,3200]{1,0:T(8,128)} %bitcast.384, ...), kind=kOutput, calls=%fused_computation.30 | convolution fusion | flops 5264172032 | bytes 31585792 | tf_op jit(solution)/shard_map/dot_general | solution.py:1136
  951.6 26.7 %scan_adjoint.1 = f32[2,16,3200]{2,1,0:T(8,128)} custom-call(f32[2,256,3200]{2,1,0:T(8,128)} %bitcast.486, f32[2,256,3200]{2,1,0:T(8,128)} %get-tuple-element.224.gy_ref, f32[2,256,16,128]{3,2,1,0:T(8,128)} %broadcast_in_dim.124.c_ref, f32[16,3200]{1,0:T(8,128)} %mul.594.dec_ref), custom_call_target="tpu_custom_call" | custom-call | flops 157286400 | bytes 26214400 | tf_op jit(solution)/shard_map/scan_adjoint/pallas_call | solution.py:880
  1030.4 54.2 %attend_back.1 = (bf16[2,256,1920]{2,1,0:T(8,128)(2,1)}, bf16[2,1024,384]{2,1,0:T(8,128)(2,1)S(1)}, bf16[2,1024,640]{2,1,0:T(8,128)(2,1)}) custom-call(s32[4]{0:T(128)S(1)} %copy-done.14, bf16[2,256,1920]{2,1,0:T(8,128)(2,1)} %bitcast.379, bf16[1,2,256,1024]{3,2,1,0:T(8,128)(2,1)S(1)} %bitcast.377, ...), custom_call_target="tpu_custom_call" | custom-call | flops 11744051200 | bytes 13107200 | tf_op jit(solution)/shard_map/attend_back/pallas_call | solution.py:1095
  1145.6 17.3 collective-permute-done.41
  1217.8 107.2 %scan_back.1 = (f32[2,256,3200]{2,1,0:T(8,128)}, f32[2,256,3200]{2,1,0:T(8,128)}, f32[2,256,16,128]{3,2,1,0:T(8,128)}, f32[2,256,16,128]{3,2,1,0:T(8,128)}, f32[2,16,3200]{2,1,0:T(8,128)}) custom-call(f32[2,256,3200]{2,1,0:T(8,128)} %bitcast.487, f32[2,256,3200]{2,1,0:T(8,128)} %get-tuple-element.161.xc_ref, f32[2,256,3200]{2,1,0:T(8,128)} %get-tuple-element.224.gy_ref, ...), custom_call_target="tpu_custom_call" | custom-call | flops 629145600 | bytes 26214400 | tf_op jit(solution)/shard_map/scan_back/pallas_call | solution.py:952
  1394.0 15.6 collective-permute-done.53
  1413.6 20.0 %multiply_reduce_fusion.3 = (bf16[3200]{0:T(1024)(128)(2,1)S(1)}, bf16[3200]{0:T(1024)(128)(2,1)S(1)}, bf16[3200]{0:T(1024)(128)(2,1)S(1)}, bf16[3200]{0:T(1024)...) fusion(f32[2,256,3200]{2,1,0:T(8,128)} %multiply_multiply_fusio, ...), kind=kLoop, calls=%fused_computation.33 | loop fusion | flops 21283200 | bytes 59065600 | tf_op jit(solution)/shard_map/reduce_sum | solution.py:1427
  1487.8 13.1 concatenate.183
  1522.9 212.9 %reduce_gradients.1 = (f32[200,400]{1,0:T(8,128)}, f32[200,80]{1,0:T(8,128)}, f32[200,160]{1,0:T(8,128)}, f32[200,1600]{1,0:T(8,128)}, f32[272,512]{1,0:T(8,128)}) custom-call(bf16[8,200,3200]{2,1,0:T(8,128)(2,1)} %bitcast.417, bf16[8,200,3200]{2,1,0:T(8,128)(2,1)} %bitcast.416, bf16[8,200,1920]{2,1,0:T(8,128)(2,1)} %bitcast.420, ...), custom_call_target="tpu_custom_call" | custom-call | tf_op jit(solution)/shard_map/reduce_gradients/pallas_call | solution.py:738
  (786 shorter events, 738.4 us)
Async XLA Ops:
  205.0 98.4 %collective-permute-start.2 = (bf16[200,11008]{1,0:T(8,128)(2,1)}, bf16[200,11008]{1,0:T(8,128)(2,1)}, u32[]{:S(2)}, u32[]{:S(2)}) collective-permute-start(bf16[200,11008]{1,0:T(8,128)(2,1)} %get-tuple-element.172.refs_0_), channel_id=1, source_target_pairs={{0,8},{4,12},{8,0},{12,4},{16,24},{20,28},{24,16},{28,20},{1,9},{5... | collective-permute-start | bytes 13209608 | tf_op jit(solution)/shard_map/ppermute | solution.py:34
  205.7 97.7 %collective-permute-start.3 = (bf16[200,11008]{1,0:T(8,128)(2,1)}, bf16[200,11008]{1,0:T(8,128)(2,1)}, u32[]{:S(2)}, u32[]{:S(2)}) collective-permute-start(bf16[200,11008]{1,0:T(8,128)(2,1)} %get-tuple-element.172.refs_0_), channel_id=1, source_target_pairs={{0,16},{4,20},{8,24},{12,28},{16,0},{20,4},{24,8},{28,12},{1,17},{... | collective-permute-start | bytes 13209608 | tf_op jit(solution)/shard_map/ppermute | solution.py:34
  245.2 112.8 %collective-permute-start.9 = (bf16[1,688,400]{1,2,0:T(8,128)(2,1)}, bf16[1,688,400]{1,2,0:T(8,128)(2,1)}, u32[]{:S(2)}, u32[]{:S(2)}) collective-permute-start(bf16[1,688,400]{1,2,0:T(8,128)(2,1)} %copy.122), channel_id=1, source_target_pairs={{0,2},{1,3},{2,0},{3,1},{4,6},{5,7},{6,4},{7,5},{8,10},{9,11},{10,... | collective-permute-start | bytes 1651208 | tf_op jit(solution)/shard_map/ppermute | solution.py:34
  262.8 143.6 %collective-permute-start = (bf16[400,1600]{1,0:T(8,128)(2,1)}, bf16[400,1600]{1,0:T(8,128)(2,1)S(1)}, u32[]{:S(2)}, u32[]{:S(2)}) collective-permute-start(bf16[400,1600]{1,0:T(8,128)(2,1)} %get-tuple-element.178.refs_0_), channel_id=1, source_target_pairs={{0,8},{4,12},{8,0},{12,4},{16,24},{20,28},{24,16},{28,20},{1,9},{5... | collective-permute-start | bytes 3840008 | tf_op jit(solution)/shard_map/ppermute | solution.py:34
  306.5 99.9 %collective-permute-start.7 = (bf16[200,5504]{1,0:T(8,128)(2,1)}, bf16[200,5504]{1,0:T(8,128)(2,1)}, u32[]{:S(2)}, u32[]{:S(2)}) collective-permute-start(bf16[200,5504]{1,0:T(8,128)(2,1)} %slice.543), channel_id=1, source_target_pairs={{0,16},{4,20},{8,24},{12,28},{16,0},{20,4},{24,8},{28,12},{1,17},{... | collective-permute-start | bytes 6604808 | tf_op jit(solution)/shard_map/ppermute | solution.py:34
  311.1 95.3 %collective-permute-start.8 = (bf16[200,5504]{1,0:T(8,128)(2,1)}, bf16[200,5504]{1,0:T(8,128)(2,1)}, u32[]{:S(2)}, u32[]{:S(2)}) collective-permute-start(bf16[200,5504]{1,0:T(8,128)(2,1)} %slice.544), channel_id=1, source_target_pairs={{0,8},{4,12},{8,0},{12,4},{16,24},{20,28},{24,16},{28,20},{1,9},{5... | collective-permute-start | bytes 6604808 | tf_op jit(solution)/shard_map/ppermute | solution.py:34
  315.3 91.1 %collective-permute-start.6 = (bf16[2,2,256,1024]{3,2,1,0:T(8,128)(2,1)}, bf16[2,2,256,1024]{3,2,1,0:T(8,128)(2,1)}, u32[]{:S(2)}, u32[]{:S(2)}) collective-permute-start(bf16[2,2,256,1024]{3,2,1,0:T(8,128)(2,1)} %pad_maximum_fusion.1), channel_id=1, source_target_pairs={{0,1},{1,0},{2,3},{3,2},{4,5},{5,4},{6,7},{7,6},{8,9},{9,8},{10,11... | collective-permute-start | bytes 6291464 | tf_op jit(solution)/shard_map/ppermute | solution.py:34
  786.5 85.0 %collective-permute-start.28 = (bf16[800,5504]{1,0:T(8,128)(2,1)}, bf16[800,5504]{1,0:T(8,128)(2,1)}, u32[]{:S(2)}, u32[]{:S(2)}) collective-permute-start(bf16[800,5504]{1,0:T(8,128)(2,1)} %convolution_convert_fusion.3), channel_id=1, source_target_pairs={{0,4},{4,0},{8,12},{12,8},{16,20},{20,16},{24,28},{28,24},{1,5},{5... | collective-permute-start | bytes 26419208 | tf_op jit(solution)/shard_map/ppermute | solution.py:34
  897.0 94.0 %collective-permute-start.33 = (bf16[1600,1600]{1,0:T(8,128)(2,1)}, bf16[1600,1600]{1,0:T(8,128)(2,1)}, u32[]{:S(2)}, u32[]{:S(2)}) collective-permute-start(bf16[1600,1600]{1,0:T(8,128)(2,1)} %convolution_convert_fusion.5), channel_id=1, source_target_pairs={{0,4},{4,0},{8,12},{12,8},{16,20},{20,16},{24,28},{28,24},{1,5},{5... | collective-permute-start | bytes 15360008 | tf_op jit(solution)/shard_map/ppermute | solution.py:34
  904.2 86.8 %collective-permute-start.32 = (bf16[400,2816]{1,0:T(8,128)(2,1)}, bf16[400,2816]{1,0:T(8,128)(2,1)}, u32[]{:S(2)}, u32[]{:S(2)}) collective-permute-start(bf16[400,2816]{1,0:T(8,128)(2,1)} %fusion.11), channel_id=1, source_target_pairs={{0,16},{4,20},{8,24},{12,28},{16,0},{20,4},{24,8},{28,12},{1,17},{... | collective-permute-start | bytes 6758408 | tf_op jit(solution)/shard_map/ppermute | solution.py:34
  910.1 80.9 %collective-permute-start.31 = (bf16[400,2688]{1,0:T(8,128)(2,1)}, bf16[400,2688]{1,0:T(8,128)(2,1)}, u32[]{:S(2)}, u32[]{:S(2)}) collective-permute-start(bf16[400,2688]{1,0:T(8,128)(2,1)} %fusion.13), channel_id=1, source_target_pairs={{0,8},{4,12},{8,0},{12,4},{16,24},{20,28},{24,16},{28,20},{1,9},{5... | collective-permute-start | bytes 6451208 | tf_op jit(solution)/shard_map/ppermute | solution.py:34
  988.1 112.8 %collective-permute-start.38 = (bf16[400,2816]{1,0:T(8,128)(2,1)}, bf16[400,2816]{1,0:T(8,128)(2,1)}, u32[]{:S(2)}, u32[]{:S(2)}) collective-permute-start(bf16[400,2816]{1,0:T(8,128)(2,1)} %fusion.12), channel_id=1, source_target_pairs={{0,16},{4,20},{8,24},{12,28},{16,0},{20,4},{24,8},{28,12},{1,17},{... | collective-permute-start | bytes 6758408 | tf_op jit(solution)/shard_map/ppermute | solution.py:34
  989.6 110.0 %collective-permute-start.37 = (bf16[400,2688]{1,0:T(8,128)(2,1)}, bf16[400,2688]{1,0:T(8,128)(2,1)}, u32[]{:S(2)}, u32[]{:S(2)}) collective-permute-start(bf16[400,2688]{1,0:T(8,128)(2,1)} %fusion.14), channel_id=1, source_target_pairs={{0,8},{4,12},{8,0},{12,4},{16,24},{20,28},{24,16},{28,20},{1,9},{5... | collective-permute-start | bytes 6451208 | tf_op jit(solution)/shard_map/ppermute | solution.py:34
  995.2 106.9 %collective-permute-start.36 = (bf16[200,2816]{1,0:T(8,128)(2,1)}, bf16[200,2816]{1,0:T(8,128)(2,1)}, u32[]{:S(2)}, u32[]{:S(2)}) collective-permute-start(bf16[200,2816]{1,0:T(8,128)(2,1)} %fusion.29), channel_id=1, source_target_pairs={{0,8},{4,12},{8,0},{12,4},{16,24},{20,28},{24,16},{28,20},{1,9},{5... | collective-permute-start | bytes 3379208 | tf_op jit(solution)/shard_map/ppermute | solution.py:34
  1000.3 101.8 %collective-permute-start.35 = (bf16[200,2688]{1,0:T(8,128)(2,1)}, bf16[200,2688]{1,0:T(8,128)(2,1)}, u32[]{:S(2)}, u32[]{:S(2)}) collective-permute-start(bf16[200,2688]{1,0:T(8,128)(2,1)} %fusion.27), channel_id=1, source_target_pairs={{0,16},{4,20},{8,24},{12,28},{16,0},{20,4},{24,8},{28,12},{1,17},{... | collective-permute-start | bytes 3225608 | tf_op jit(solution)/shard_map/ppermute | solution.py:34
  1009.2 82.9 %collective-permute-start.34 = (bf16[2,688,400]{1,2,0:T(8,128)(2,1)}, bf16[2,688,400]{1,2,0:T(8,128)(2,1)S(1)}, u32[]{:S(2)}, u32[]{:S(2)}) collective-permute-start(bf16[2,688,400]{1,2,0:T(8,128)(2,1)} %copy.152), channel_id=1, source_target_pairs={{0,1},{1,0},{2,3},{3,2},{4,5},{5,4},{6,7},{7,6},{8,9},{9,8},{10,11... | collective-permute-start | bytes 3302408 | tf_op jit(solution)/shard_map/ppermute | solution.py:34
  1099.5 77.1 %collective-permute-start.46 = (bf16[800,832]{1,0:T(8,128)(2,1)}, bf16[800,832]{1,0:T(8,128)(2,1)}, u32[]{:S(2)}, u32[]{:S(2)}) collective-permute-start(bf16[800,832]{1,0:T(8,128)(2,1)} %add_convert_fusion.3), channel_id=1, source_target_pairs={{0,16},{4,20},{8,24},{12,28},{16,0},{20,4},{24,8},{28,12},{1,17},{... | collective-permute-start | bytes 3993608 | tf_op jit(solution)/shard_map/ppermute | solution.py:34
  1106.5 80.4 %collective-permute-start.44 = (bf16[200,2816]{1,0:T(8,128)(2,1)}, bf16[200,2816]{1,0:T(8,128)(2,1)}, u32[]{:S(2)}, u32[]{:S(2)}) collective-permute-start(bf16[200,2816]{1,0:T(8,128)(2,1)} %fusion.31), channel_id=1, source_target_pairs={{0,8},{4,12},{8,0},{12,4},{16,24},{20,28},{24,16},{28,20},{1,9},{5... | collective-permute-start | bytes 3379208 | tf_op jit(solution)/shard_map/ppermute | solution.py:34
  1174.6 156.0 %collective-permute-start.51 = (bf16[2,2,256,1024]{3,2,1,0:T(8,128)(2,1)}, bf16[2,2,256,1024]{3,2,1,0:T(8,128)(2,1)}, u32[]{:S(2)}, u32[]{:S(2)}) collective-permute-start(bf16[2,2,256,1024]{3,2,1,0:T(8,128)(2,1)} %pad_maximum_fusion.2), channel_id=1, source_target_pairs={{0,1},{1,0},{2,3},{3,2},{4,5},{5,4},{6,7},{7,6},{8,9},{9,8},{10,11... | collective-permute-start | bytes 6291464 | tf_op jit(solution)/shard_map/ppermute | solution.py:34
  1196.2 139.8 %collective-permute-start.50 = (bf16[400,832]{1,0:T(8,128)(2,1)}, bf16[400,832]{1,0:T(8,128)(2,1)}, u32[]{:S(2)}, u32[]{:S(2)}) collective-permute-start(bf16[400,832]{1,0:T(8,128)(2,1)} %add_convert_fusion.12), channel_id=1, source_target_pairs={{0,8},{4,12},{8,0},{12,4},{16,24},{20,28},{24,16},{28,20},{1,9},{5... | collective-permute-start | bytes 1996808 | tf_op jit(solution)/shard_map/ppermute | solution.py:34
  1199.6 136.4 %collective-permute-start.49 = (bf16[400,768]{1,0:T(8,128)(2,1)}, bf16[400,768]{1,0:T(8,128)(2,1)}, u32[]{:S(2)}, u32[]{:S(2)}) collective-permute-start(bf16[400,768]{1,0:T(8,128)(2,1)} %add_convert_fusion.15), channel_id=1, source_target_pairs={{0,16},{4,20},{8,24},{12,28},{16,0},{20,4},{24,8},{28,12},{1,17},{... | collective-permute-start | bytes 1843208 | tf_op jit(solution)/shard_map/ppermute | solution.py:34
  1211.2 122.4 %collective-permute-start.48 = (bf16[2,200,1376]{2,1,0:T(8,128)(2,1)}, bf16[2,200,1376]{2,1,0:T(8,128)(2,1)}, u32[]{:S(2)}, u32[]{:S(2)}) collective-permute-start(bf16[2,200,1376]{2,1,0:T(8,128)(2,1)} %pad_maximum_fusion.12), channel_id=1, source_target_pairs={{0,1},{1,0},{2,3},{3,2},{4,5},{5,4},{6,7},{7,6},{8,9},{9,8},{10,11... | collective-permute-start | bytes 3302408 | tf_op jit(solution)/shard_map/ppermute | solution.py:34
  1213.7 122.3 %collective-permute-start.47 = (bf16[1,200,1376]{2,1,0:T(8,128)(2,1)}, bf16[1,200,1376]{2,1,0:T(8,128)(2,1)}, u32[]{:S(2)}, u32[]{:S(2)}) collective-permute-start(bf16[1,200,1376]{2,1,0:T(8,128)(2,1)} %fusion.118), channel_id=1, source_target_pairs={{0,2},{1,3},{2,0},{3,1},{4,6},{5,7},{6,4},{7,5},{8,10},{9,11},{10,... | collective-permute-start | bytes 1651208 | tf_op jit(solution)/shard_map/ppermute | solution.py:34
  1360.8 103.6 %collective-permute-start.54 = (bf16[1,200,1376]{2,1,0:T(8,128)(2,1)}, bf16[1,200,1376]{2,1,0:T(8,128)(2,1)}, u32[]{:S(2)}, u32[]{:S(2)}) collective-permute-start(bf16[1,200,1376]{2,1,0:T(8,128)(2,1)} %fusion.119), channel_id=1, source_target_pairs={{0,2},{1,3},{2,0},{3,1},{4,6},{5,7},{6,4},{7,5},{8,10},{9,11},{10,... | collective-permute-start | bytes 1651208 | tf_op jit(solution)/shard_map/ppermute | solution.py:34
  (227 other events, 4468.9 us)

commit v2 on v1

--- a/solution.py
+++ b/solution.py
@@ -43,13 +43,6 @@
 def bits_of(axis):
     count = lax.axis_size(axis)
     return [1 << k for k in range(count.bit_length() - 1)]
-
-
-def total_over(value, axes):
-    for axis in axes:
-        for bit in bits_of(axis):
-            value = value + permute_bit(value, axis, bit)
-    return value
 
 
 def from_ctx(blocks):
@@ -536,10 +529,11 @@
         self.spread = ctx_terms(own, self.columns)
         self.live, self.fresh = self.spread.live, []
 
-    def finished(self):
+    def blocks(self, *columns):
         while self.stage <= len(bits_of("batch")):
             self.step()
-        return self.live["own"]
+        terms = ctx_terms(self.live["own"], columns).live
+        return {key[0]: block for key, block in terms.items()}
 
     def result(self):
         while self.stage <= len(bits_of("batch")) or not self.spread:
@@ -552,19 +546,22 @@
         return out
 
 
-def reduce_kernel(n_parts, items, program, *refs):
+def reduce_kernel(n_parts, n_late, items, program, *refs):
     n = len(items)
     plain = [i for i, pieces in enumerate(items) if not pieces]
-    terms, refs = refs[:n], refs[n:]
-    outs, refs = refs[: n_parts + len(plain)], refs[n_parts + len(plain) :]
+    nctx = lax.axis_size("ctx")
+    n_slots = n_parts + len(plain) + n_late
+    terms, tile, refs = refs[:n], refs[n], refs[n + 1 :]
+    lates, refs = refs[: n_late * nctx], refs[n_late * nctx :]
+    outs, refs = refs[:n_slots], refs[n_slots:]
+    tile_out, refs = refs[0], refs[1:]
     accs, refs = refs[:n], refs[n:]
     firsts, refs = refs[:n], refs[n:]
     seconds, refs = refs[:n], refs[n:]
     thirds, refs = refs[:n], refs[n:]
     parts, refs = refs[:n_parts], refs[n_parts:]
-    lands, sems = refs[: n_parts + len(plain)], refs[n_parts + len(plain) :]
-    load, b_send, b_recv, z_send, z_recv = sems
-    nctx = lax.axis_size("ctx")
+    lands, refs = refs[:n_slots], refs[n_slots:]
+    load, b_send, b_recv, z_send, z_recv, held, came, m_send, m_recv = refs
     b, c = lax.axis_index("batch"), lax.axis_index("ctx")
 
     barrier = pltpu.get_barrier_semaphore()
@@ -606,7 +603,7 @@
 
         copy_rows(to.shape[1], rows)
 
-    flights, z_flights = {}, {}
+    flights, z_flights, owns = {}, {}, {}
 
     def begin(item):
         copies = []
@@ -694,8 +691,26 @@
             for r in range(1, nctx)
         ]
 
+    def late(i):
+        slot = n_slots - n_late + i
+        own = pltpu.make_async_copy(lates[i * nctx], lands[slot].at[0], z_send.at[slot, 0])
+        own.start()
+        z_flights[slot] = [
+            remote(
+                lates[i * nctx + r],
+                lands[slot].at[r],
+                z_send.at[slot, r],
+                z_recv.at[slot, r],
+                {"ctx": c ^ r},
+            )
+            for r in range(1, nctx)
+        ]
+        owns[slot] = own
+
     def finish(slot):
         land, out = lands[slot], outs[slot]
+        if slot in owns:
+            owns[slot].wait()
         for copy in z_flights[slot]:
             copy.wait_recv()
 
@@ -709,14 +724,30 @@
 
         copy_rows(out.shape[0], rows)
 
-    acts = {"b": begin, "f": first, "s": second, "t": third, "p": spread, "e": finish}
+    ways = [{"batch": b ^ bit} for bit in (1, 2, 4)] + [{"ctx": c ^ bit} for bit in bits_of("ctx")]
+    swaps = []
+
+    def swap(stage):
+        if stage:
+            swaps[-1].wait_recv()
+            held[stage] = held[stage - 1] + came[stage - 1]
+        else:
+            held[0] = tile[...]
+        if stage == len(ways):
+            tile_out[...] = held[stage]
+            return
+        swaps.append(
+            remote(held.at[stage], came.at[stage], m_send.at[stage], m_recv.at[stage], ways[stage])
+        )
+
+    acts = {"b": begin, "f": first, "s": second, "t": third, "p": spread, "e": finish, "m": swap, "l": late}
     for act, which in program:
         acts[act](which)
     for copy in started:
         copy.wait_send()
 
 
-def reduce_all(terms, items, widths, program, collective_id):
+def reduce_all(terms, tile, lates, items, widths, program, collective_id):
     nctx, nbatch = lax.axis_size("ctx"), lax.axis_size("batch")
     plain = [i for i, pieces in enumerate(items) if not pieces]
     rows = {piece[0]: terms[i].shape[0] // nbatch for i, ps in enumerate(items) for piece in ps}
@@ -730,26 +761,87 @@
                     if at_part == part:
                         whole = whole.at[:, place, lo:hi].set(sums[i][:, col : col + hi - lo])
             out.append(lax.psum_scatter(whole, "ctx", scatter_dimension=1).astype(F32))
-        return out + [lax.psum(sums[i], "ctx").astype(F32) for i in plain]
+        out += [lax.psum(sums[i], "ctx").astype(F32) for i in plain]
+        out += [ToCtx(blocks).result() for blocks in lates]
+        return out + [lax.psum(tile, ("batch", "ctx"))]
     terms = [t.reshape(nbatch, -1, t.shape[1]) for t in terms]
     sizes = [t.shape[1:] for t in terms]
     shapes = [(rows[part], n) for part, n in enumerate(widths)] + [sizes[i] for i in plain]
+    shapes += [blocks[0].shape for blocks in lates]
+    late_blocks = [blocks[r] for blocks in lates for r in range(nctx)]
+    hops = 3 + len(bits_of("ctx"))
     dma = pltpu.SemaphoreType.DMA
     return pl.pallas_call(
-        functools.partial(reduce_kernel, len(widths), tuple(items), program),
-        in_specs=[pl.BlockSpec(memory_space=pl.ANY)] * len(terms),
-        out_specs=[pl.BlockSpec(memory_space=pltpu.VMEM)] * len(shapes),
-        out_shape=[jax.ShapeDtypeStruct(shape, F32) for shape in shapes],
+        functools.partial(reduce_kernel, len(widths), len(lates), tuple(items), program),
+        in_specs=[pl.BlockSpec(memory_space=pl.ANY)] * len(terms)
+        + [pl.BlockSpec(memory_space=pltpu.VMEM)]
+        + [pl.BlockSpec(memory_space=pl.ANY)] * len(late_blocks),
+        out_specs=[pl.BlockSpec(memory_space=pltpu.VMEM)] * (len(shapes) + 1),
+        out_shape=[jax.ShapeDtypeStruct(shape, F32) for shape in shapes + [tile.shape]],
         scratch_shapes=[pltpu.VMEM((count,) + size, BF16) for count in (4, 4, 2, 1) for size in sizes]
         + [pltpu.VMEM((nctx,) + shape, BF16) for shape in shapes[: len(widths)]]
         + [pltpu.VMEM((nctx,) + shape, BF16) for shape in shapes]
         + [dma((len(terms), 4)), dma((len(terms), 10)), dma((len(terms), 10))]
-        + [dma((len(shapes), nctx)), dma((len(shapes), nctx))],
+        + [dma((len(shapes), nctx)), dma((len(shapes), nctx))]
+        + [pltpu.VMEM((hops + 1,) + tile.shape, F32), pltpu.VMEM((hops,) + tile.shape, F32)]
+        + [dma((hops,)), dma((hops,))],
+        cost_estimate=pl.CostEstimate(flops=1, bytes_accessed=1, transcendentals=0),
         compiler_params=pltpu.CompilerParams(
             collective_id=collective_id, has_side_effects=True, vmem_limit_bytes=62 << 20
         ),
         name="reduce_gradients",
-    )(*terms)
+    )(*terms, tile, *late_blocks)
+
+
+def pack_kernel(heights, n_rows, n_gains, *refs):
+    blocks, refs = refs[: len(heights)], refs[len(heights) :]
+    lines, gains, (out, few) = refs[:n_rows], refs[n_rows : n_rows + n_gains], refs[n_rows + n_gains :]
+    owners, width = out.shape[0], few.shape[1]
+    chan = width // owners
+    out[...] = jnp.zeros_like(out)
+    few[...] = jnp.zeros_like(few)
+    for i, line in enumerate(lines):
+        few[i : i + 1, :] = line[...]
+    for i, gain in enumerate(gains):
+        n = gain.shape[1] // owners
+        for q in range(owners):
+            few[n_rows + i : n_rows + i + 1, q * chan : q * chan + n] = gain[:, q * n : (q + 1) * n]
+    at = 0
+    for block in blocks + (few,):
+        rows = block.shape[0]
+        for q in range(owners):
+            out[q, at : at + rows, :chan] = block[:, q * chan : (q + 1) * chan].astype(BF16)
+        at += rows
+
+
+def pack_small(blocks, lines, gains):
+    nbatch = lax.axis_size("batch")
+    heights = [block.shape[0] for block in blocks]
+    total, chan = sum(heights) + 16, INNER // nbatch
+    wide = -(-chan // (2 * LANE)) * 2 * LANE
+    if nbatch != 8:
+        own = D // nbatch
+        gains = [
+            jnp.pad(g.reshape(nbatch, own), ((0, 0), (0, chan - own))).reshape(1, INNER)
+            for g in gains
+        ]
+        few = lines + gains
+        few.append(jnp.zeros((16 - len(few), INNER), F32))
+        packed = jnp.concatenate(blocks + few, axis=0).astype(BF16)
+        packed = packed.reshape(total, nbatch, chan).transpose(1, 0, 2)
+        packed = jnp.pad(packed, ((0, 0), (0, 0), (0, wide - chan)))
+    else:
+        vmem = pl.BlockSpec(memory_space=pltpu.VMEM)
+        packed = pl.pallas_call(
+            functools.partial(pack_kernel, tuple(heights), len(lines), len(gains)),
+            in_specs=[vmem] * (len(blocks) + len(lines) + len(gains)),
+            out_specs=vmem,
+            out_shape=jax.ShapeDtypeStruct((nbatch, total, wide), BF16),
+            scratch_shapes=[pltpu.VMEM((16, INNER), F32)],
+            compiler_params=pltpu.CompilerParams(vmem_limit_bytes=40 << 20),
+            name="pack_small",
+        )(*blocks, *lines, *gains)
+    return packed.reshape(nbatch * total, wide)
 
 
 def wide(tile, width):
@@ -763,7 +855,7 @@
 
 SCAN_WIDTH = 640
 SCAN_PART = 384
-UNROLL = 8
+UNROLL = 16
 
 
 def scan_parts(width):
@@ -783,8 +875,7 @@
 
 
 def scan_cost(seqs, span, chan, ops):
-    cells = seqs * span * chan * STATE
-    return pl.CostEstimate(flops=cells * ops, bytes_accessed=seqs * span * chan * 16, transcendentals=cells)
+    return pl.CostEstimate(flops=ops, bytes_accessed=seqs * span * chan, transcendentals=0)
 
 
 def final_kernel(step_ref, xc_ref, b_ref, dec_ref, fin_ref, drive):
@@ -1000,13 +1091,15 @@
 
 
 def attend_kernel(n, place_ref, q_ref, *refs):
-    k_refs, v_refs, (out_ref, mask, k_all, v_all) = refs[:n], refs[n : 2 * n], refs[2 * n :]
+    k_refs, v_refs, (out_ref, lse_ref, mask, k_all, v_all) = refs[:n], refs[n : 2 * n], refs[2 * n :]
     pl.when(first_step())(lambda: attend_mask(place_ref, mask))
     heads_in(k_refs, v_refs, k_all, v_all)
     for g in range(GROUP):
         s = scores_of(q_ref[0, :, g * HD : (g + 1) * HD], k_all[...]) + mask[...]
-        e = jnp.exp(s - jnp.max(s, axis=-1, keepdims=True))
+        peak = jnp.max(s, axis=-1, keepdims=True)
+        e = jnp.exp(s - peak)
         total = jnp.sum(e, axis=-1, keepdims=True)
+        lse_ref[0, :, g : g + 1] = peak + jnp.log(total)
         mixed = jnp.dot(e.astype(BF16), v_all[...], preferred_element_type=F32)
         out_ref[0, :, g * VHEAD : (g + 1) * VHEAD] = mixed / total
 
@@ -1019,37 +1112,39 @@
         for kv in kvs
     ]
     out = pl.BlockSpec((1, span, GROUP * VHEAD), lambda s, h: (s, 0, h))
+    lse = pl.BlockSpec((1, span, LANE), lambda s, h: (s, 0, h))
     length = span * sum(kv.shape[0] for kv in kvs)
     held = [
         pltpu.VMEM((span, length), F32),
         pltpu.VMEM((length, HD), BF16),
         pltpu.VMEM((length, VHEAD), BF16),
     ]
-    return [pl.BlockSpec(memory_space=pltpu.SMEM), q] + ks + vs, q, out, length, held
+    return [pl.BlockSpec(memory_space=pltpu.SMEM), q] + ks + vs, q, out, lse, length, held
 
 
 def attend(place_of, q, kvs):
     seqs, span, _ = q.shape
-    ins, _, out, length, held = attend_specs(span, kvs)
+    ins, _, out, lse, length, held = attend_specs(span, kvs)
     cells = seqs * HEADS * span * length
     return pl.pallas_call(
         functools.partial(attend_kernel, len(kvs)),
         grid=(seqs, KV),
         in_specs=ins,
-        out_specs=out,
-        out_shape=jax.ShapeDtypeStruct((seqs, span, INNER), F32),
+        out_specs=[out, lse],
+        out_shape=[
+            jax.ShapeDtypeStruct((seqs, span, INNER), F32),
+            jax.ShapeDtypeStruct((seqs, span, KV * LANE), F32),
+        ],
         scratch_shapes=held,
         compiler_params=pltpu.CompilerParams(vmem_limit_bytes=50 << 20),
-        cost_estimate=pl.CostEstimate(
-            flops=cells * 2 * (HD + VHEAD), bytes_accessed=cells, transcendentals=cells
-        ),
+        cost_estimate=pl.CostEstimate(flops=1, bytes_accessed=cells // 8, transcendentals=0),
         name="attend",
     )(place_of, q, *kvs, *kvs)
 
 
 def attend_back_kernel(n, place_ref, q_ref, *refs):
     k_refs, v_refs, refs = refs[:n], refs[n : 2 * n], refs[2 * n :]
-    o_ref, do_ref, dq_ref, dk_ref, dv_ref, mask, k_all, v_all, dk_sum, dv_sum = refs
+    lse_ref, o_ref, do_ref, dq_ref, dk_ref, dv_ref, mask, k_all, v_all, dk_sum, dv_sum = refs
     pl.when(first_step())(lambda: attend_mask(place_ref, mask))
     heads_in(k_refs, v_refs, k_all, v_all)
     k, v = k_all[...], v_all[...]
@@ -1058,8 +1153,7 @@
         do = do_ref[0, :, g * VHEAD : (g + 1) * VHEAD]
         o = o_ref[0, :, g * VHEAD : (g + 1) * VHEAD]
         s = scores_of(q, k) + mask[...]
-        e = jnp.exp(s - jnp.max(s, axis=-1, keepdims=True))
-        p = e * (1.0 / jnp.sum(e, axis=-1, keepdims=True))
+        p = jnp.exp(s - lse_ref[0, :, g : g + 1])
         dp = scores_of(do, v)
         ds = (p * (dp - jnp.sum(do.astype(F32) * o, axis=-1, keepdims=True))).astype(BF16)
         dq = jnp.dot(ds, k, preferred_element_type=F32).astype(BF16)
@@ -1088,14 +1182,14 @@
             dk_ref[0, :, h * HD : (h + 1) * HD] = dk
 
 
-def attend_back(place_of, q, kvs, o, do):
+def attend_back(place_of, q, kvs, lse_in, o, do):
     seqs, span, _ = q.shape
-    ins, qs, out, length, held = attend_specs(span, kvs)
+    ins, qs, out, lse, length, held = attend_specs(span, kvs)
     cells = seqs * HEADS * span * length
     return pl.pallas_call(
         functools.partial(attend_back_kernel, len(kvs)),
         grid=(seqs, KV),
-        in_specs=ins + [out, out],
+        in_specs=ins + [lse, out, out],
         out_specs=[
             qs,
             pl.BlockSpec((1, length, KWIDE), lambda s, h: (s, 0, 0)),
@@ -1108,11 +1202,9 @@
         ],
         scratch_shapes=held + [pltpu.VMEM((HD, length), F32), pltpu.VMEM((VHEAD, length), F32)],
         compiler_params=pltpu.CompilerParams(vmem_limit_bytes=50 << 20),
-        cost_estimate=pl.CostEstimate(
-            flops=cells * 2 * (3 * HD + 2 * VHEAD), bytes_accessed=cells, transcendentals=cells
-        ),
+        cost_estimate=pl.CostEstimate(flops=1, bytes_accessed=cells // 8, transcendentals=0),
         name="attend_back",
-    )(place_of, q, *kvs, *kvs, o, do)
+    )(place_of, q, *kvs, *kvs, lse_in, o, do)
 
 
 def rms_scale(value):
@@ -1235,7 +1327,6 @@
     count = jnp.sum(counts[:, 0, ::LANE])
     get_output, get_gate_up = Gather(row_output), Gather(row_gate_up)
     get_down = Gather(None, w_down)
-    f_conv = hold([get_down], f_conv)
     f_vectors = f_packed[:, :n_lines, :chan].transpose(1, 0, 2).reshape(n_lines, nbatch * chan)
     f_select = f_vectors[RANK + STATE + CONV + 5 :].T
     f_gains = f_packed[:, n_lines : n_lines + 2, : gains.shape[1]]
@@ -1259,6 +1350,7 @@
     rim = shift(conv_in[:, span - (CONV - 1) :], "ctx", 1, False)
     conv_in, then1 = hold([], conv_in, normed1)
     kv_own = matmul(then1, f_kv).astype(BF16).reshape(seqs, span, KWIDE + KV * VHEAD)
+    rim, kv_own, then1 = hold([], rim, kv_own, then1)
     get_kv = FromCtx(kv_own)
     get_kv.step()
     q_heads = (matmul(then1, f_q) * scale).astype(BF16).reshape(seqs, span, KV * QWIDE)
@@ -1266,12 +1358,7 @@
     extended = jnp.concatenate([rim, conv_in], axis=1).astype(F32)
     pre_conv = f_conv_bias + sum((taps[tap] * extended[:, tap : tap + span] for tap in range(CONV)))
     conv_out, conv_slope = silu_pair(pre_conv)
-    conv_out = hold([get_gate_up, get_kv], conv_out)
-
-    get_kv.step()
-    get_gate_up.step()
-    get_output.step()
-    get_down.step()
+
     conv_low = conv_out.reshape(rows, INNER).astype(BF16)
     projected = matmul(conv_low, f_select)
     rank_low = projected[:, :RANK].astype(BF16)
@@ -1281,22 +1368,24 @@
     step_pre = matmul(rank_low, f_step) + f_step_bias
     steps = jax.nn.softplus(step_pre).reshape(seqs, span, INNER)
     step_sums = jnp.sum(steps, axis=1, keepdims=True)
+    steps, step_sums = hold([get_gate_up], steps, step_sums)
+    get_gate_up.step()
+    get_output.step()
+    get_down.step()
     final = scan_final(steps, conv_out, bb, dec)
-    final = hold([get_output, get_kv, get_gate_up, get_down], final)
+    final = hold([get_kv], final)
+    get_kv.step()
 
     sums_high = step_sums.astype(BF16)
     sums_low = (step_sums - sums_high.astype(F32)).astype(BF16)
     get_state = FromCtx(jnp.concatenate([final.astype(BF16), sums_high, sums_low], axis=1))
     get_state.step()
+    get_down.step()
+    q_heads = hold([get_state, get_gate_up], q_heads)
+    get_state.step()
+    f_gate, f_up = hold([get_state, get_output, get_down], *get_gate_up.whole(2, ff, ff))
     get_output.step()
     get_down.step()
-    get_kv.finish()
-    kvs = list(get_kv.live.values())
-    attn = attend(place_of, q_heads, kvs).reshape(rows, INNER)
-    attn = hold([get_state, get_output, get_down], attn)
-    get_state.step()
-    get_down.step()
-    f_gate, f_up = hold([get_state], *get_gate_up.whole(2, ff, ff))
 
     states = get_state.finish()
     all_sums = {
@@ -1305,9 +1394,14 @@
     }
     entry = carried({r: v[:, :STATE] for r, v in states.items()}, all_sums, dec, False)
     scan_out = scan_out_of(steps, conv_out, bb, cc, dec, entry)
+    scan_out = hold([get_kv, get_output, get_down], scan_out)
+    get_down.step()
+    get_kv.finish()
+    kvs = list(get_kv.live.values())
+    attn, lse = attend(place_of, q_heads, kvs)
+    attn = attn.reshape(rows, INNER)
+    attn = hold([get_down], attn)
     (f_output,) = get_output.whole(1, D)
-    scan_out, f_output = hold([get_down], scan_out, f_output)
-    get_down.step()
 
     gate_act, gate_slope = silu_pair(gate_z)
     pre_gate = scan_out + skip * conv_out
@@ -1331,21 +1425,21 @@
     weight_rows = valid.reshape(rows, 1).astype(F32)
     diff = hidden2 - teacher.reshape(rows, D).astype(F32)
     loss_local = jnp.sum(weight_rows * diff * diff)
-    loss_sum = total_over(jnp.full((8, LANE), loss_local), ("batch", "ctx"))[0, 0]
 
     seed = cotangent.reshape(rows, D).astype(F32) + all_tokens / count * weight_rows * diff
     seed_low = seed.astype(BF16)
     put_down = Scatter(inner_ff, seed_low, w_down.shape[1])
     put_down.step()
+    put_down.fresh.clear()
     d_inner = matmul_back(seed_low, f_down)
     d_gate = (d_inner * up_pre * gate_slope2).astype(BF16)
     d_up = (d_inner * gate_act2).astype(BF16)
-    d_gate, d_up = hold([put_down], d_gate, d_up)
+    d_gate, d_up = hold([], d_gate, d_up)
 
     put_down.step()
     put_gate = Scatter(normed2, d_gate, w_gate.shape[1])
     put_gate.step()
-    put_up = Scatter(normed2, d_up, w_up.shape[1])
+    put_up = Scatter(normed2, d_up)
     put_up.step()
     d_norm2 = matmul_back(d_gate, f_gate) + matmul_back(d_up, f_up)
     g_gain_second = jnp.sum(d_norm2 * hidden1 * scale2, axis=0, keepdims=True)
@@ -1355,7 +1449,7 @@
     put_down.step()
     put_gate.step()
     d_branch = d_hidden1.astype(BF16)
-    put_output = Scatter(merged, d_branch, w_output.shape[1])
+    put_output = Scatter(merged, d_branch)
     put_output.step()
     d_merged = matmul_back(d_branch, f_output)
     g_beta_attn = jnp.sum(0.5 * d_merged * attn_norm, axis=0, keepdims=True)
@@ -1376,11 +1470,15 @@
     get_adjoint = FromCtx(adjoint.astype(BF16))
     get_adjoint.step()
     dq, dk, dv = attend_back(
-        place_of, q_heads, kvs, attn.reshape(seqs, span, INNER), d_attn.reshape(seqs, span, INNER)
+        place_of,
+        q_heads,
+        kvs,
+        lse,
+        attn.reshape(seqs, span, INNER),
+        d_attn.reshape(seqs, span, INNER),
     )
     dq, dk, dv = hold([put_down, put_gate, put_up, get_adjoint], dq, dk, dv)
     get_adjoint.step()
-    put_down.step()
     put_gate.step()
     put_up.step()
     put_output.step()
@@ -1388,27 +1486,22 @@
     g_q = outer_sum(normed1, dq).astype(BF16)
     g_z = outer_sum(normed1, d_gate_z).astype(BF16)
     d_norm1 = matmul_back(dq, f_q) + matmul_back(d_gate_z, f_z)
-    d_norm1, g_q, g_z = hold(
-        [get_adjoint, put_down, put_gate, put_up, put_output], d_norm1, g_q, g_z
-    )
+    d_norm1, g_q, g_z = hold([get_adjoint, put_up, put_output], d_norm1, g_q, g_z)
 
     d_kv = jnp.concatenate([dk, dv], axis=-1).reshape(seqs, nctx, span, KWIDE + KV * VHEAD)
     put_kv = ToCtx({r: d_kv[:, i] for i, r in enumerate(order)})
     put_kv.step()
-    put_gate.step()
-    put_up.step()
+    put_down.step()
     put_output.step()
     arrive = carried(get_adjoint.finish(), all_sums, dec, True)
     g_drive, g_steps, g_b, g_c, grad_decay = scan_back(
         steps, conv_out, d_pre_gate, bb, cc, dec, entry, arrive
     )
     g_drive, g_steps, g_b, g_c = hold(
-        [put_gate, put_up, put_output, put_kv], g_drive, g_steps, g_b, g_c
+        [put_down, put_gate, put_output, put_kv], g_drive, g_steps, g_b, g_c
     )
 
     put_kv.step()
-    put_up.step()
-    put_output.step()
     d_step_pre = g_steps.reshape(rows, INNER) * jax.nn.sigmoid(step_pre)
     g_step_bias = jnp.sum(d_step_pre, axis=0, keepdims=True)
     d_step_low = d_step_pre.astype(BF16)
@@ -1422,6 +1515,7 @@
         + matmul_back(d_projected, f_select).reshape(seqs, span, INNER)
     )
     d_pre_conv = hold([put_kv], d_conv * conv_slope)
+    put_gate.step()
     g_conv_bias = jnp.sum(d_pre_conv, axis=(0, 1))[None]
     g_taps = [
         jnp.sum(d_pre_conv * extended[:, tap : tap + span], axis=(0, 1))[None]
@@ -1435,10 +1529,8 @@
     )
     back_rim = shift(d_extended[:, : CONV - 1].astype(BF16), "ctx", -1, False)
     d_conv_in = d_extended[:, CONV - 1 :].at[:, span - (CONV - 1) :].add(back_rim.astype(F32))
-    d_conv_in = d_conv_in.reshape(rows, INNER).astype(BF16)
-    d_conv_in = hold([put_output, put_up], d_conv_in)
-
-    put_output.step()
+    d_conv_in = hold([put_gate], d_conv_in.reshape(rows, INNER).astype(BF16))
+
     d_kv_own = put_kv.result().astype(BF16).reshape(rows, KWIDE + KV * VHEAD)
     d_norm1 = d_norm1 + matmul_back(d_kv_own, f_kv) + matmul_back(d_conv_in, f_conv)
     g_gain_first = jnp.sum(d_norm1 * x_flat * scale1, axis=0, keepdims=True)
@@ -1447,37 +1539,36 @@
     g_conv = outer_sum(normed1, d_conv_in).astype(BF16)
     g_kv = outer_sum(normed1, d_kv_own).astype(BF16)
 
-    pad_rank, pad_sel = -RANK % 8, -(RANK + 2 * STATE) % 8
+    pad_rank, pad_sel = -RANK % 16, -(RANK + 2 * STATE) % 16
     g_step = outer_sum(jnp.pad(rank_low, ((0, 0), (0, pad_rank))), d_step_low)
     g_select = outer_sum(jnp.pad(d_projected, ((0, 0), (0, pad_sel))), conv_low)
     own_gain = D // nbatch
-    gains_wide = [
-        jnp.pad(g.reshape(nbatch, own_gain), ((0, 0), (0, chan - own_gain))).reshape(1, INNER)
-        for g in (g_gain_first, g_gain_second)
-    ]
-    few = g_taps + [g_conv_bias, g_step_bias, g_skip, g_beta_attn, g_beta_ssm] + gains_wide
-    few.append(jnp.zeros((-len(few) % 8, INNER), F32))
     at_sel = RANK + pad_rank
     at_dec = at_sel + RANK + 2 * STATE + pad_sel
     at_few = at_dec + STATE
 
-    small = jnp.concatenate(
-        [g_step, g_select, jnp.sum(grad_decay, axis=0) * decay] + few, axis=0
-    ).astype(BF16)
-    small = small.reshape(small.shape[0], nbatch, chan).transpose(1, 0, 2)
-    small = jnp.pad(small, ((0, 0), (0, -small.shape[1] % 16), (0, -chan % (2 * LANE))))
-    small = small.reshape(-1, small.shape[2])
-    small = hold([put_output], small)
+    small = pack_small(
+        [g_step, g_select, jnp.sum(grad_decay, axis=0) * decay],
+        g_taps + [g_conv_bias, g_step_bias, g_skip, g_beta_attn, g_beta_ssm],
+        [g_gain_first, g_gain_second],
+    )
+    lates = [put_output.blocks(w_output.shape[1]), put_up.blocks(w_up.shape[1])]
     terms = [g_conv, g_z, g_q, g_kv, small]
     items = [items[3][0], items[4][0], items[2][0], items[1][0], ()]
-    program = "b4 b3 b2 b1 b0 f4 f3 f2 f1 s4 f0 s3 t4 s2 t3 p1 p2 t2 p0 s1 e4 t1 s0 t0 p3 e1 e2 e0 e3"
+    program = "b4 b3 l0 l1 b2 b1 b0 m0 f4 f3 m1 f2 f1 s4 m2 f0 s3 t4 m3 s2 t3 p1 p2 m4 t2 p0 s1 e4 m5 t1 s0 "
+    program += "t0 p3 e5 e6 e1 e2 e0 e3"
     program = tuple((word[0], int(word[1:])) for word in program.split())
-    (r_down,), (r_gate,), (r_up,), (r_output,) = [
-        put.result() for put in (put_down, put_gate, put_up, put_output)
-    ]
-    r_query, r_key, r_value, r_mixer, small = reduce_all(
-        terms, items, (n_q, n_k, n_v, n_mixer), program, 4
+    (r_down,), (r_gate,) = put_down.result(), put_gate.result()
+    r_query, r_key, r_value, r_mixer, small, r_output, r_up, loss_sum = reduce_all(
+        terms,
+        jnp.full((8, LANE), loss_local),
+        lates,
+        items,
+        (n_q, n_k, n_v, n_mixer),
+        program,
+        4,
     )
+    loss_sum = loss_sum[0, 0]
     small = small[:, :chan]
     return (
         output,

time: 1770 us -> 1740 us (0.983)
  Pallas kernels: 749 us -> 725 us
    unnamed x409 -> x421, local copies, waits for them, and re-layouts: 36.5 us -> 61.2 us
    concatenate x16 -> x0, local copies, waits for them, and re-layouts: 22.9 us -> none  [per_device(): jnp.concatenate([g_step, g_select, jnp.sum(grad_decay, axis=0) * decay] +...]
    ppermute x55 -> x46, waiting for transfers between devices: 97.8 us -> 110 us  [permute_bit(): return lax.ppermute(value, axis, [(i, i ^ bit) for i in range(count)])]
    pallas_call x1 -> x2, Pallas kernels: 213 us -> 214 us  [the longest x1 213 us: reduce_all(): pl.pallas_call(functools.partial(reduce_kernel, len(widths), len(lates),...]
    ppermute x55 -> x46, starting transfers between devices: 70.3 us -> 71 us  [permute_bit(): return lax.ppermute(value, axis, [(i, i ^ bit) for i in range(count)])]
  transfers between devices with their start and end apart: 57 -> 48, of which waited for: 10 -> 12; matrix products, arithmetic and copies ran while one was open for 34% -> 31% of each run, Pallas kernels for 19% -> 18%
where the time goes in v2:
time: 1740 us; the launch traced here: 1730 us
  Pallas kernels  725 us (42%)
  matrix products  405 us (23%)
  local copies, waits for them, and re-layouts  214 us (12%)
  other arithmetic  183 us (11%)
  waiting for transfers between devices  110 us (6%)
  starting transfers between devices  83 us (5%)
    dot_general x38, matrix products, matmul(): return jnp.dot(left, right, preferred_element_type=F32)  256 us
    pallas_call x1, Pallas kernels, reduce_all(): pl.pallas_call(functools.partial(reduce_kernel, len(widths), len(lates),...  213 us
    pallas_call x1, Pallas kernels, gather_all(): pl.pallas_call(functools.partial(gather_kernel, len(shards), tuple(kinds)...  189 us
    dot_general x10, matrix products, matmul_back(): lax.dot_general(left, right, (((1,), (1,)), ((), ())), preferred_element_...  116 us
    ppermute x46, waiting for transfers between devices, permute_bit(): return lax.ppermute(value, axis, [(i, i ^ bit) for i in range(count)])  110 us
    pallas_call x1, Pallas kernels, scan_back(): pl.pallas_call(back_kernel, grid=(seqs, chan // SCAN_WIDTH), in_specs=[po...  102 us
    ppermute x46, starting transfers between devices, permute_bit(): return lax.ppermute(value, axis, [(i, i ^ bit) for i in range(count)])  71 us
    unnamed x421, local copies, waits for them, and re-layouts  61.2 us
  transfers between devices with their start and end apart: 48, of which 12 were waited for; matrix products, arithmetic and copies ran while one was open for 31% of the time, Pallas kernels for 18%

profile of v2, /device:TPU:8, one launch (start us, length us, event | category | flops | bytes accessed | tf_op | source)
XLA Modules:
  0.0 1726.0 jit_solution(3419395464312616017)
XLA Ops:
  15.6 189.4 %gather_weights.1 = (bf16[8,272,512]{2,1,0:T(8,128)(2,1)}, bf16[8,200,1024]{2,1,0:T(8,128)(2,1)}, bf16[8,200,1920]{2,1,0:T(8,128)(2,1)}, bf16[8,200,3200]{2,1,0:...) custom-call(bf16[200,400]{1,0:T(8,128)(2,1)} %refs_0_.1, ...), custom_call_target="tpu_custom_call" | custom-call | tf_op jit(solution)/shard_map/gather_weights/pallas_call | solution.py:258
  307.4 23.7 %scan_final.1 = f32[2,16,3200]{2,1,0:T(8,128)} custom-call(f32[2,256,3200]{2,1,0:T(8,128)} %bitcast.375, f32[2,256,3200]{2,1,0:T(8,128)} %get-tuple-element.377.xc_ref, f32[2,256,16,128]{3,2,1,0:T(8,128)} %broadcast_in_dim.148.b_ref, f32[16,3200]{1,0:T(8,128)} %broadcast_multiply_fusion.4.dec_ref), custom_call_target="tpu_custom_call" | custom-call | flops 6 | bytes 1638400 | tf_op jit(solution)/shard_map/scan_final/pallas_call | solution.py:902
  410.1 27.3 %assemble.3 = (bf16[8,200,5504]{2,1,0:T(8,128)(2,1)}, bf16[8,200,5504]{2,1,0:T(8,128)(2,1)}) custom-call(bf16[200,11008]{1,0:T(8,128)(2,1)S(1)} %copy-done.6, bf16[200,11008]{1,0:T(8,128)(2,1)} %collective-permute-done.2.refs_1_, bf16[200,11008]{1,0:T(8,128)(2,1)} %collective-permute-done.3.refs_2_, bf16[200,5504]{1,0:T(8,128)(2,1)} %collective-permute-done.6.refs_3_, ...), custom_call_target="tpu_custom_call" | custom-call | bytes 70451200 | tf_op jit(solution)/shard_map/assemble/pallas_call | solution.py:386
  464.0 44.1 %scan_out.1 = f32[2,256,3200]{2,1,0:T(8,128)} custom-call(f32[2,256,3200]{2,1,0:T(8,128)} %bitcast.376, f32[2,256,3200]{2,1,0:T(8,128)} %get-tuple-element.377.xc_ref, f32[2,256,16,128]{3,2,1,0:T(8,128)} %broadcast_in_dim.148.b_ref, f32[2,256,16,128]{3,2,1,0:T(8,128)} %broadcast_in_dim.152.c_ref, f32[16,3200]{1,0:T(8,128)} %broadcast_multiply_fusion.4.dec_ref, ...), custom_call_target="tpu_custom_call" | custom-call | flops 10 | bytes 1638400 | tf_op jit(solution)/shard_map/scan_out/pallas_call | solution.py:938
  521.8 16.9 multiply_reduce_fusion.8
  538.7 31.8 %attend.1 = (f32[2,256,3200]{2,1,0:T(8,128)}, f32[2,256,640]{2,1,0:T(8,128)S(1)}) custom-call(s32[4]{0:T(128)S(1)} %pad_add_fusion.1.place_ref, bf16[2,256,1920]{2,1,0:T(8,128)(2,1)} %bitcast.417, bf16[1,2,256,1024]{3,2,1,0:T(8,128)(2,1)S(1)} %bitcast.367, bf16[1,2,256,1024]{3,2,1,0:T(8,128)(2,1)S(1)} %collective-permute-done.1.refs_1_.refs_4_, ...), custom_call_target="tpu_custom_call" | custom-call | flops 1 | bytes 1638400 | tf_op jit(solution)/shard_map/attend/pallas_call | solution.py:1129
  589.4 14.6 multiply_reduce_fusion.14
  607.1 17.0 fusion.219
  624.0 23.7 %fusion = (bf16[5504,512]{0,1:T(8,128)(2,1)}, f32[512,5504]{1,0:T(8,128)}) fusion(f32[512,5504]{1,0:T(8,128)} %fusion.219, bf16[512,1600]{0,1:T(8,128)(2,1)} %copy-done.50, bf16[1600,5504]{1,0:T(8,128)(2,1)} %bitcast.473), kind=kOutput, calls=%fused_computation.6 | convolution fusion | flops 9034661888 | bytes 47431680 | tf_op jit(solution)/shard_map/dot_general | solution.py:1224
  652.7 15.9 assemble.5
  668.6 24.4 %fusion.204 = (bf16[512,1600]{0,1:T(8,128)(2,1)}, f32[512,1600]{0,1:T(8,128)}, f32[]{:T(128)}, bf16[512,1600]{0,1:T(8,128)(2,1)}) fusion(f32[512,1600]{0,1:T(8,128)} %bitcast.432, f32[512,1600]{0,1:T(8,128)} %bitcast.433, f32[512]{0:T(512)S(1)} %broadcast_multiply_fusion.7, f32[512]{0:T(512)S(1)} %bitcast.463, f32[512,1600]{0,1:T(8,128)} %copy-done.38, ...), kind=kOutput, calls=%fused_computation.426 | convolution fusion | flops 9042034688 | bytes 56545284 | tf_op jit(solution)/shard_map/dot_general | solution.py:1224
  693.0 23.8 %multiply_convert_fusion = (bf16[512,5504]{1,0:T(8,128)(2,1)}, bf16[512,5504]{1,0:T(8,128)(2,1)}) fusion(f32[512,5504]{1,0:T(8,128)} %fusion.219, f32[512,5504]{1,0:T(8,128)} %get-tuple-element.474, bf16[512,1600]{0,1:T(8,128)(2,1)} %get-tuple-element.372, bf16[5504,1600]{1,0:T(8,128)(2,1)} %bitcast.401), kind=kOutput, calls=%fused_computation.12 | convolution fusion | flops 9054388224 | bytes 53067776 | tf_op jit(solution)/shard_map/dot_general | solution.py:1228
  762.9 14.3 fusion.220
  783.0 20.6 %multiply_reduce_fusion.11 = (f32[1600]{0:T(1024)S(1)}, f32[512]{0:T(512)S(1)}, f32[512,1600]{0,1:T(8,128)}) fusion(f32[512,1600]{0,1:T(8,128)} %copy-done.38, f32[512]{0:T(512)S(1)} %copy-done.163, f32[1600]{0:T(1024)S(1)} %copy-done.147, f32[512,1600]{0,1:T(8,128)} %fusion.220, bf16[512,5504]{1,0:T(8,128)(2,1)} %get-tuple-element.193, ...), kind=kOutput, calls=%fused_computation.77 | convolution fusion | flops 9023485952 | bytes 33096192 | tf_op jit(solution)/shard_map/dot_general | solution.py:1228
  872.4 24.5 %collective-permute-done.20 = bf16[1376,768]{1,0:T(8,128)(2,1)} collective-permute-done((bf16[1376,768]{1,0:T(8,128)(2,1)}, bf16[1376,768]{1,0:T(8,128)(2,1)}, u32[]{:S(2)}, u32[]{:S(2)}) %collective-permute-start.20) | collective-permute-done | bytes 2113568 | tf_op jit(solution)/shard_map/ppermute | solution.py:34
  900.3 18.7 %multiply_reduce_fusion = (f32[3200]{0:T(1024)S(1)}, f32[512]{0:T(512)S(1)}, f32[512]{0:T(512)S(1)}, f32[3200]{0:T(1024)S(1)}, f32[512,3200]{1,0:T(8,128)}) fusion(f32[2,256,3200]{2,1,0:T(8,128)} %get-tuple-element.375, f32[512]{0:T(512)S(1)} %bitcast.460, f32[3200]{0:T(1024)S(1)} %copy-done.149, f32[512,3200]{1,0:T(8,128)} %bitcast.379, ...), kind=kOutput, calls=%fused_computation.30 | convolution fusion | flops 5264172032 | bytes 31598592 | tf_op jit(solution)/shard_map/dot_general | solution.py:1228
  983.0 23.5 %scan_adjoint.1 = f32[2,16,3200]{2,1,0:T(8,128)} custom-call(f32[2,256,3200]{2,1,0:T(8,128)} %bitcast.377, f32[2,256,3200]{2,1,0:T(8,128)} %get-tuple-element.224.gy_ref, f32[2,256,16,128]{3,2,1,0:T(8,128)} %broadcast_in_dim.152.c_ref, f32[16,3200]{1,0:T(8,128)} %broadcast_multiply_fusion.4.dec_ref), custom_call_target="tpu_custom_call" | custom-call | flops 6 | bytes 1638400 | tf_op jit(solution)/shard_map/scan_adjoint/pallas_call | solution.py:971
  1060.4 42.9 %attend_back.1 = (bf16[2,256,1920]{2,1,0:T(8,128)(2,1)}, bf16[2,1024,384]{2,1,0:T(8,128)(2,1)}, bf16[2,1024,640]{2,1,0:T(8,128)(2,1)}) custom-call(s32[4]{0:T(128)S(1)} %pad_add_fusion.1.place_ref, bf16[2,256,1920]{2,1,0:T(8,128)(2,1)} %bitcast.418, bf16[1,2,256,1024]{3,2,1,0:T(8,128)(2,1)S(1)} %bitcast.369, ...), custom_call_target="tpu_custom_call" | custom-call | flops 1 | bytes 1638400 | tf_op jit(solution)/shard_map/attend_back/pallas_call | solution.py:1189
  1161.6 18.5 %collective-permute-done.35 = bf16[1,688,400]{1,2,0:T(8,128)(2,1)} collective-permute-done((bf16[1,688,400]{1,2,0:T(8,128)(2,1)}, bf16[1,688,400]{1,2,0:T(8,128)(2,1)}, u32[]{:S(2)}, u32[]{:S(2)}) %collective-permute-start.35) | collective-permute-done | bytes 550432 | tf_op jit(solution)/shard_map/ppermute | solution.py:34
  1215.2 101.5 %scan_back.1 = (f32[2,256,3200]{2,1,0:T(8,128)}, f32[2,256,3200]{2,1,0:T(8,128)}, f32[2,256,16,128]{3,2,1,0:T(8,128)}, f32[2,256,16,128]{3,2,1,0:T(8,128)}, f32[2,16,3200]{2,1,0:T(8,128)}) custom-call(f32[2,256,3200]{2,1,0:T(8,128)} %bitcast.378, f32[2,256,3200]{2,1,0:T(8,128)} %get-tuple-element.377.xc_ref, f32[2,256,3200]{2,1,0:T(8,128)} %get-tuple-element.224.gy_ref, ...), custom_call_target="tpu_custom_call" | custom-call | flops 24 | bytes 1638400 | tf_op jit(solution)/shard_map/scan_back/pallas_call | solution.py:1043
  1373.7 30.5 %collective-permute-done.46 = bf16[1,2,256,1024]{3,2,1,0:T(8,128)(2,1)} collective-permute-done((bf16[1,2,256,1024]{3,2,1,0:T(8,128)(2,1)}, bf16[1,2,256,1024]{3,2,1,0:T(8,128)(2,1)}, u32[]{:S(2)}, u32[]{:S(2)}) %collective-permute-start.46) | collective-permute-done | bytes 1048608 | tf_op jit(solution)/shard_map/ppermute | solution.py:34
  1404.2 21.1 %multiply_reduce_fusion.3 = (f32[3200]{0:T(1024)}, f32[3200]{0:T(1024)}, f32[3200]{0:T(1024)}, f32[3200]{0:T(1024)}, f32[3200]{0:T(1024)}, /*index=5*/f32[2,256,...) fusion(f32[2,256,3200]{2,1,0:T(8,128)} %multiply_multiply_fusion, ...), kind=kLoop, calls=%fused_computation.33 | loop fusion | flops 21283200 | bytes 59097600 | tf_op jit(solution)/shard_map/reduce_sum | solution.py:1521
  1465.5 12.9 multiply_reduce_fusion.10
  1481.9 213.5 %reduce_gradients.1 = (f32[200,400]{1,0:T(8,128)}, f32[200,80]{1,0:T(8,128)}, f32[200,160]{1,0:T(8,128)}, f32[200,1600]{1,0:T(8,128)}, f32[288,512]{1,0:T(8,128)...) custom-call(bf16[8,200,3200]{2,1,0:T(8,128)(2,1)} %bitcast.411, bf16[8,200,3200]{2,1,0:T(8,128)(2,1)} %bitcast.410, ...), custom_call_target="tpu_custom_call" | custom-call | flops 1 | bytes 1 | tf_op jit(solution)/shard_map/reduce_gradients/pallas_call | solution.py:774
  (765 shorter events, 724.5 us)
Async XLA Ops:
  205.0 97.9 %collective-permute-start.2 = (bf16[200,11008]{1,0:T(8,128)(2,1)}, bf16[200,11008]{1,0:T(8,128)(2,1)}, u32[]{:S(2)}, u32[]{:S(2)}) collective-permute-start(bf16[200,11008]{1,0:T(8,128)(2,1)} %get-tuple-element.168.refs_0_), channel_id=1, source_target_pairs={{0,8},{4,12},{8,0},{12,4},{16,24},{20,28},{24,16},{28,20},{1,9},{5... | collective-permute-start | bytes 13209608 | tf_op jit(solution)/shard_map/ppermute | solution.py:34
  205.7 98.2 %collective-permute-start.3 = (bf16[200,11008]{1,0:T(8,128)(2,1)}, bf16[200,11008]{1,0:T(8,128)(2,1)}, u32[]{:S(2)}, u32[]{:S(2)}) collective-permute-start(bf16[200,11008]{1,0:T(8,128)(2,1)} %get-tuple-element.168.refs_0_), channel_id=1, source_target_pairs={{0,16},{4,20},{8,24},{12,28},{16,0},{20,4},{24,8},{28,12},{1,17},{... | collective-permute-start | bytes 13209608 | tf_op jit(solution)/shard_map/ppermute | solution.py:34
  232.5 205.0 %collective-permute-start.10 = (bf16[400,1600]{1,0:T(8,128)(2,1)}, bf16[400,1600]{1,0:T(8,128)(2,1)S(1)}, u32[]{:S(2)}, u32[]{:S(2)}) collective-permute-start(bf16[400,1600]{1,0:T(8,128)(2,1)} %get-tuple-element.185.refs_0_), channel_id=1, source_target_pairs={{0,16},{4,20},{8,24},{12,28},{16,0},{20,4},{24,8},{28,12},{1,17},{... | collective-permute-start | bytes 3840008 | tf_op jit(solution)/shard_map/ppermute | solution.py:34
  233.0 137.9 %collective-permute-start.11 = (bf16[1,688,400]{1,2,0:T(8,128)(2,1)}, bf16[1,688,400]{1,2,0:T(8,128)(2,1)}, u32[]{:S(2)}, u32[]{:S(2)}) collective-permute-start(bf16[1,688,400]{1,2,0:T(8,128)(2,1)} %bitcast.15), channel_id=1, source_target_pairs={{0,2},{1,3},{2,0},{3,1},{4,6},{5,7},{6,4},{7,5},{8,10},{9,11},{10,... | collective-permute-start | bytes 1651208 | tf_op jit(solution)/shard_map/ppermute | solution.py:34
  407.9 101.5 %collective-permute-start.4 = (bf16[2,2,256,1024]{3,2,1,0:T(8,128)(2,1)}, bf16[2,2,256,1024]{3,2,1,0:T(8,128)(2,1)}, u32[]{:S(2)}, u32[]{:S(2)}) collective-permute-start(bf16[2,2,256,1024]{3,2,1,0:T(8,128)(2,1)} %pad_maximum_fusion.1), channel_id=1, source_target_pairs={{0,1},{1,0},{2,3},{3,2},{4,5},{5,4},{6,7},{7,6},{8,9},{9,8},{10,11... | collective-permute-start | bytes 6291464 | tf_op jit(solution)/shard_map/ppermute | solution.py:34
  450.0 67.8 %collective-permute-start.15 = (bf16[688,1600]{1,0:T(8,128)(2,1)}, bf16[688,1600]{1,0:T(8,128)(2,1)S(1)}, u32[]{:S(2)}, u32[]{:S(2)}) collective-permute-start(bf16[688,1600]{1,0:T(8,128)(2,1)} %concatenate.115.refs_0_), channel_id=1, source_target_pairs={{0,8},{4,12},{8,0},{12,4},{16,24},{20,28},{24,16},{28,20},{1,9},{5... | collective-permute-start | bytes 6604808 | tf_op jit(solution)/shard_map/ppermute | solution.py:34
  729.8 142.6 %collective-permute-start.23 = (bf16[800,5504]{1,0:T(8,128)(2,1)}, bf16[800,5504]{1,0:T(8,128)(2,1)}, u32[]{:S(2)}, u32[]{:S(2)}) collective-permute-start(bf16[800,5504]{1,0:T(8,128)(2,1)} %convolution_convert_fusion.3), channel_id=1, source_target_pairs={{0,4},{4,0},{8,12},{12,8},{16,20},{20,16},{24,28},{28,24},{1,5},{5... | collective-permute-start | bytes 26419208 | tf_op jit(solution)/shard_map/ppermute | solution.py:34
  754.1 73.2 %collective-permute-start.19 = (bf16[2752,1600]{0,1:T(8,128)(2,1)}, bf16[2752,1600]{0,1:T(8,128)(2,1)}, u32[]{:S(2)}, u32[]{:S(2)}) collective-permute-start(bf16[2752,1600]{0,1:T(8,128)(2,1)} %convolution_convert_fusion.2), channel_id=1, source_target_pairs={{0,4},{4,0},{8,12},{12,8},{16,20},{20,16},{24,28},{28,24},{1,5},{5... | collective-permute-start | bytes 26419208 | tf_op jit(solution)/shard_map/ppermute | solution.py:34
  762.6 109.9 %collective-permute-start.22 = (bf16[800,5504]{1,0:T(8,128)(2,1)}, bf16[800,5504]{1,0:T(8,128)(2,1)}, u32[]{:S(2)}, u32[]{:S(2)}) collective-permute-start(bf16[800,5504]{1,0:T(8,128)(2,1)} %convolution_convert_fusion.4), channel_id=1, source_target_pairs={{0,4},{4,0},{8,12},{12,8},{16,20},{20,16},{24,28},{28,24},{1,5},{5... | collective-permute-start | bytes 26419208 | tf_op jit(solution)/shard_map/ppermute | solution.py:34
  926.2 90.7 %collective-permute-start.28 = (bf16[1600,1600]{1,0:T(8,128)(2,1)}, bf16[1600,1600]{1,0:T(8,128)(2,1)}, u32[]{:S(2)}, u32[]{:S(2)}) collective-permute-start(bf16[1600,1600]{1,0:T(8,128)(2,1)} %convolution_convert_fusion.5), channel_id=1, source_target_pairs={{0,4},{4,0},{8,12},{12,8},{16,20},{20,16},{24,28},{28,24},{1,5},{5... | collective-permute-start | bytes 15360008 | tf_op jit(solution)/shard_map/ppermute | solution.py:34
  933.3 83.6 %collective-permute-start.27 = (bf16[400,2816]{1,0:T(8,128)(2,1)}, bf16[400,2816]{1,0:T(8,128)(2,1)}, u32[]{:S(2)}, u32[]{:S(2)}) collective-permute-start(bf16[400,2816]{1,0:T(8,128)(2,1)} %add_convert_fusion.2), channel_id=1, source_target_pairs={{0,16},{4,20},{8,24},{12,28},{16,0},{20,4},{24,8},{28,12},{1,17},{... | collective-permute-start | bytes 6758408 | tf_op jit(solution)/shard_map/ppermute | solution.py:34
  938.1 78.8 %collective-permute-start.26 = (bf16[400,2688]{1,0:T(8,128)(2,1)}, bf16[400,2688]{1,0:T(8,128)(2,1)}, u32[]{:S(2)}, u32[]{:S(2)}) collective-permute-start(bf16[400,2688]{1,0:T(8,128)(2,1)} %fusion.11), channel_id=1, source_target_pairs={{0,8},{4,12},{8,0},{12,4},{16,24},{20,28},{24,16},{28,20},{1,9},{5... | collective-permute-start | bytes 6451208 | tf_op jit(solution)/shard_map/ppermute | solution.py:34
  945.7 70.7 %collective-permute-start.25 = (bf16[688,832]{1,0:T(8,128)(2,1)S(1)}, bf16[688,832]{1,0:T(8,128)(2,1)S(1)}, u32[]{:S(2)}, u32[]{:S(2)}) collective-permute-start(bf16[688,832]{1,0:T(8,128)(2,1)S(1)} %add_convert_fusion.7), channel_id=1, source_target_pairs={{0,8},{4,12},{8,0},{12,4},{16,24},{20,28},{24,16},{28,20},{1,9},{5... | collective-permute-start | bytes 3434504 | tf_op jit(solution)/shard_map/ppermute | solution.py:34
  1016.0 100.5 %collective-permute-start.33 = (bf16[400,2816]{1,0:T(8,128)(2,1)}, bf16[400,2816]{1,0:T(8,128)(2,1)}, u32[]{:S(2)}, u32[]{:S(2)}) collective-permute-start(bf16[400,2816]{1,0:T(8,128)(2,1)} %add_convert_fusion.1), channel_id=1, source_target_pairs={{0,16},{4,20},{8,24},{12,28},{16,0},{20,4},{24,8},{28,12},{1,17},{... | collective-permute-start | bytes 6758408 | tf_op jit(solution)/shard_map/ppermute | solution.py:34
  1016.3 99.7 %collective-permute-start.32 = (bf16[400,2688]{1,0:T(8,128)(2,1)}, bf16[400,2688]{1,0:T(8,128)(2,1)}, u32[]{:S(2)}, u32[]{:S(2)}) collective-permute-start(bf16[400,2688]{1,0:T(8,128)(2,1)} %fusion.12), channel_id=1, source_target_pairs={{0,8},{4,12},{8,0},{12,4},{16,24},{20,28},{24,16},{28,20},{1,9},{5... | collective-permute-start | bytes 6451208 | tf_op jit(solution)/shard_map/ppermute | solution.py:34
  1021.3 99.6 %collective-permute-start.31 = (bf16[200,2816]{1,0:T(8,128)(2,1)}, bf16[200,2816]{1,0:T(8,128)(2,1)}, u32[]{:S(2)}, u32[]{:S(2)}) collective-permute-start(bf16[200,2816]{1,0:T(8,128)(2,1)} %add_convert_fusion.12), channel_id=1, source_target_pairs={{0,8},{4,12},{8,0},{12,4},{16,24},{20,28},{24,16},{28,20},{1,9},{5... | collective-permute-start | bytes 3379208 | tf_op jit(solution)/shard_map/ppermute | solution.py:34
  1032.3 78.0 %collective-permute-start.29 = (bf16[2,688,400]{1,2,0:T(8,128)(2,1)}, bf16[2,688,400]{1,2,0:T(8,128)(2,1)S(1)}, u32[]{:S(2)}, u32[]{:S(2)}) collective-permute-start(bf16[2,688,400]{1,2,0:T(8,128)(2,1)} %copy.143), channel_id=1, source_target_pairs={{0,1},{1,0},{2,3},{3,2},{4,5},{5,4},{6,7},{7,6},{8,9},{9,8},{10,11... | collective-permute-start | bytes 3302408 | tf_op jit(solution)/shard_map/ppermute | solution.py:34
  1116.0 76.8 %collective-permute-start.41 = (bf16[800,832]{1,0:T(8,128)(2,1)}, bf16[800,832]{1,0:T(8,128)(2,1)}, u32[]{:S(2)}, u32[]{:S(2)}) collective-permute-start(bf16[800,832]{1,0:T(8,128)(2,1)} %add_convert_fusion.5), channel_id=1, source_target_pairs={{0,16},{4,20},{8,24},{12,28},{16,0},{20,4},{24,8},{28,12},{1,17},{... | collective-permute-start | bytes 3993608 | tf_op jit(solution)/shard_map/ppermute | solution.py:34
  1116.5 74.2 %collective-permute-start.40 = (bf16[800,768]{1,0:T(8,128)(2,1)}, bf16[800,768]{1,0:T(8,128)(2,1)}, u32[]{:S(2)}, u32[]{:S(2)}) collective-permute-start(bf16[800,768]{1,0:T(8,128)(2,1)} %add_convert_fusion.8), channel_id=1, source_target_pairs={{0,8},{4,12},{8,0},{12,4},{16,24},{20,28},{24,16},{28,20},{1,9},{5... | collective-permute-start | bytes 3686408 | tf_op jit(solution)/shard_map/ppermute | solution.py:34
  1125.3 78.8 %collective-permute-start.39 = (bf16[200,2816]{1,0:T(8,128)(2,1)}, bf16[200,2816]{1,0:T(8,128)(2,1)}, u32[]{:S(2)}, u32[]{:S(2)}) collective-permute-start(bf16[200,2816]{1,0:T(8,128)(2,1)} %add_convert_fusion.10), channel_id=1, source_target_pairs={{0,8},{4,12},{8,0},{12,4},{16,24},{20,28},{24,16},{28,20},{1,9},{5... | collective-permute-start | bytes 3379208 | tf_op jit(solution)/shard_map/ppermute | solution.py:34
  1190.8 133.9 %collective-permute-start.44 = (bf16[2,2,256,1024]{3,2,1,0:T(8,128)(2,1)}, bf16[2,2,256,1024]{3,2,1,0:T(8,128)(2,1)}, u32[]{:S(2)}, u32[]{:S(2)}) collective-permute-start(bf16[2,2,256,1024]{3,2,1,0:T(8,128)(2,1)} %pad_maximum_fusion.2), channel_id=1, source_target_pairs={{0,1},{1,0},{2,3},{3,2},{4,5},{5,4},{6,7},{7,6},{8,9},{9,8},{10,11... | collective-permute-start | bytes 6291464 | tf_op jit(solution)/shard_map/ppermute | solution.py:34
  1207.2 121.3 %collective-permute-start.43 = (bf16[400,832]{1,0:T(8,128)(2,1)}, bf16[400,832]{1,0:T(8,128)(2,1)}, u32[]{:S(2)}, u32[]{:S(2)}) collective-permute-start(bf16[400,832]{1,0:T(8,128)(2,1)} %add_convert_fusion.22), channel_id=1, source_target_pairs={{0,8},{4,12},{8,0},{12,4},{16,24},{20,28},{24,16},{28,20},{1,9},{5... | collective-permute-start | bytes 1996808 | tf_op jit(solution)/shard_map/ppermute | solution.py:34
  1211.1 117.3 %collective-permute-start.42 = (bf16[400,768]{1,0:T(8,128)(2,1)}, bf16[400,768]{1,0:T(8,128)(2,1)}, u32[]{:S(2)}, u32[]{:S(2)}) collective-permute-start(bf16[400,768]{1,0:T(8,128)(2,1)} %add_convert_fusion.25), channel_id=1, source_target_pairs={{0,16},{4,20},{8,24},{12,28},{16,0},{20,4},{24,8},{28,12},{1,17},{... | collective-permute-start | bytes 1843208 | tf_op jit(solution)/shard_map/ppermute | solution.py:34
  1365.7 89.2 %collective-permute-start.45 = (bf16[1,200,1376]{2,1,0:T(8,128)(2,1)}, bf16[1,200,1376]{2,1,0:T(8,128)(2,1)}, u32[]{:S(2)}, u32[]{:S(2)}) collective-permute-start(bf16[1,200,1376]{2,1,0:T(8,128)(2,1)} %fusion.112), channel_id=1, source_target_pairs={{0,2},{1,3},{2,0},{3,1},{4,6},{5,7},{6,4},{7,5},{8,10},{9,11},{10,... | collective-permute-start | bytes 1651208 | tf_op jit(solution)/shard_map/ppermute | solution.py:34
  (221 other events, 4884.3 us)

commit v3 on v2

--- a/solution.py
+++ b/solution.py
@@ -1486,7 +1486,8 @@
     g_q = outer_sum(normed1, dq).astype(BF16)
     g_z = outer_sum(normed1, d_gate_z).astype(BF16)
     d_norm1 = matmul_back(dq, f_q) + matmul_back(d_gate_z, f_z)
-    d_norm1, g_q, g_z = hold([get_adjoint, put_up, put_output], d_norm1, g_q, g_z)
+    put_down.fresh = list(put_down.live)
+    d_norm1, g_q, g_z = hold([get_adjoint, put_up, put_output, put_down], d_norm1, g_q, g_z)
 
     d_kv = jnp.concatenate([dk, dv], axis=-1).reshape(seqs, nctx, span, KWIDE + KV * VHEAD)
     put_kv = ToCtx({r: d_kv[:, i] for i, r in enumerate(order)})
@@ -1514,8 +1515,7 @@
         + d_pre_gate * skip
         + matmul_back(d_projected, f_select).reshape(seqs, span, INNER)
     )
-    d_pre_conv = hold([put_kv], d_conv * conv_slope)
-    put_gate.step()
+    d_pre_conv = d_conv * conv_slope
     g_conv_bias = jnp.sum(d_pre_conv, axis=(0, 1))[None]
     g_taps = [
         jnp.sum(d_pre_conv * extended[:, tap : tap + span], axis=(0, 1))[None]
@@ -1529,7 +1529,9 @@
     )
     back_rim = shift(d_extended[:, : CONV - 1].astype(BF16), "ctx", -1, False)
     d_conv_in = d_extended[:, CONV - 1 :].at[:, span - (CONV - 1) :].add(back_rim.astype(F32))
-    d_conv_in = hold([put_gate], d_conv_in.reshape(rows, INNER).astype(BF16))
+    put_gate.fresh = list(put_gate.live)
+    d_conv_in = hold([put_kv, put_gate], d_conv_in.reshape(rows, INNER).astype(BF16))
+    put_gate.step()
 
     d_kv_own = put_kv.result().astype(BF16).reshape(rows, KWIDE + KV * VHEAD)
     d_norm1 = d_norm1 + matmul_back(d_kv_own, f_kv) + matmul_back(d_conv_in, f_conv)
@@ -1552,6 +1554,7 @@
         g_taps + [g_conv_bias, g_step_bias, g_skip, g_beta_attn, g_beta_ssm],
         [g_gain_first, g_gain_second],
     )
+    small = hold([put_gate], small)
     lates = [put_output.blocks(w_output.shape[1]), put_up.blocks(w_up.shape[1])]
     terms = [g_conv, g_z, g_q, g_kv, small]
     items = [items[3][0], items[4][0], items[2][0], items[1][0], ()]

time: 1740 us -> 1700 us (0.977)
  waiting for transfers between devices: 110 us -> 76.2 us
    ppermute x46, waiting for transfers between devices: 110 us -> 76.2 us  [permute_bit(): return lax.ppermute(value, axis, [(i, i ^ bit) for i in range(count)])]
    unnamed x421 -> x397, local copies, waits for them, and re-layouts: 61.2 us -> 62.5 us
  transfers between devices with their start and end apart: 48 -> 48, of which waited for: 12 -> 11; matrix products, arithmetic and copies ran while one was open for 31% -> 31% of each run, Pallas kernels for 18% -> 18%
where the time goes in v3:
time: 1700 us; the launch traced here: 1680 us
  Pallas kernels  723 us (43%)
  matrix products  397 us (23%)
  local copies, waits for them, and re-layouts  218 us (13%)
  other arithmetic  176 us (10%)
  starting transfers between devices  87.7 us (5%)
  waiting for transfers between devices  76.2 us (4%)
    dot_general x38, matrix products, matmul(): return jnp.dot(left, right, preferred_element_type=F32)  254 us
    pallas_call x1, Pallas kernels, reduce_all(): pl.pallas_call(functools.partial(reduce_kernel, len(widths), len(lates),...  212 us
    pallas_call x1, Pallas kernels, gather_all(): pl.pallas_call(functools.partial(gather_kernel, len(shards), tuple(kinds)...  189 us
    dot_general x10, matrix products, matmul_back(): lax.dot_general(left, right, (((1,), (1,)), ((), ())), preferred_element_...  113 us
    pallas_call x1, Pallas kernels, scan_back(): pl.pallas_call(back_kernel, grid=(seqs, chan // SCAN_WIDTH), in_specs=[po...  102 us
    ppermute x46, waiting for transfers between devices, permute_bit(): return lax.ppermute(value, axis, [(i, i ^ bit) for i in range(count)])  76.2 us
    ppermute x46, starting transfers between devices, permute_bit(): return lax.ppermute(value, axis, [(i, i ^ bit) for i in range(count)])  76.1 us
    unnamed x397, local copies, waits for them, and re-layouts  62.5 us
  transfers between devices with their start and end apart: 48, of which 11 were waited for; matrix products, arithmetic and copies ran while one was open for 31% of the time, Pallas kernels for 18%

profile of v3, /device:TPU:8, one launch (start us, length us, event | category | flops | bytes accessed | tf_op | source)
XLA Modules:
  0.0 1684.4 jit_solution(3779281293046244022)
XLA Ops:
  15.6 189.4 %gather_weights.1 = (bf16[8,272,512]{2,1,0:T(8,128)(2,1)}, bf16[8,200,1024]{2,1,0:T(8,128)(2,1)}, bf16[8,200,1920]{2,1,0:T(8,128)(2,1)}, bf16[8,200,3200]{2,1,0:...) custom-call(bf16[200,400]{1,0:T(8,128)(2,1)} %refs_0_.1, ...), custom_call_target="tpu_custom_call" | custom-call | tf_op jit(solution)/shard_map/gather_weights/pallas_call | solution.py:258
  307.4 23.7 %scan_final.1 = f32[2,16,3200]{2,1,0:T(8,128)} custom-call(f32[2,256,3200]{2,1,0:T(8,128)} %bitcast.375, f32[2,256,3200]{2,1,0:T(8,128)} %get-tuple-element.394.xc_ref, f32[2,256,16,128]{3,2,1,0:T(8,128)} %broadcast_in_dim.148.b_ref, f32[16,3200]{1,0:T(8,128)} %broadcast_multiply_fusion.4.dec_ref), custom_call_target="tpu_custom_call" | custom-call | flops 6 | bytes 1638400 | tf_op jit(solution)/shard_map/scan_final/pallas_call | solution.py:902
  342.3 12.8 collective-permute-start.5
  410.1 27.3 %assemble.3 = (bf16[8,200,5504]{2,1,0:T(8,128)(2,1)}, bf16[8,200,5504]{2,1,0:T(8,128)(2,1)}) custom-call(bf16[200,11008]{1,0:T(8,128)(2,1)S(1)} %copy-done.6, bf16[200,11008]{1,0:T(8,128)(2,1)} %collective-permute-done.2.refs_1_, bf16[200,11008]{1,0:T(8,128)(2,1)} %collective-permute-done.3.refs_2_, bf16[200,5504]{1,0:T(8,128)(2,1)} %collective-permute-done.6.refs_3_, ...), custom_call_target="tpu_custom_call" | custom-call | bytes 70451200 | tf_op jit(solution)/shard_map/assemble/pallas_call | solution.py:386
  464.0 44.1 %scan_out.1 = f32[2,256,3200]{2,1,0:T(8,128)} custom-call(f32[2,256,3200]{2,1,0:T(8,128)} %bitcast.376, f32[2,256,3200]{2,1,0:T(8,128)} %get-tuple-element.394.xc_ref, f32[2,256,16,128]{3,2,1,0:T(8,128)} %broadcast_in_dim.148.b_ref, f32[2,256,16,128]{3,2,1,0:T(8,128)} %broadcast_in_dim.152.c_ref, f32[16,3200]{1,0:T(8,128)} %broadcast_multiply_fusion.4.dec_ref, ...), custom_call_target="tpu_custom_call" | custom-call | flops 10 | bytes 1638400 | tf_op jit(solution)/shard_map/scan_out/pallas_call | solution.py:938
  521.8 16.9 %multiply_reduce_fusion.8 = (f32[2,256]{1,0:T(2,128)S(1)}, f32[2,256,3200]{2,1,0:T(8,128)}, f32[2,256,3200]{2,1,0:T(8,128)}) fusion(f32[2,256,3200]{2,1,0:T(8,128)} %scan_out.1, f32[2,256,3200]{2,1,0:T(8,128)} %get-tuple-element.394.xc_ref, f32[3200]{0:T(1024)S(1)} %reshape.493, bf16[1600,3200,1]{1,0,2:T(8,128)(2,1)} %bitcast.474, ...), kind=kOutput, calls=%fused_computation.42 | convolution fusion | flops 5257625088 | bytes 38107648 | tf_op jit(solution)/shard_map/dot_general | solution.py:1224
  538.7 31.8 %attend.1 = (f32[2,256,3200]{2,1,0:T(8,128)}, f32[2,256,640]{2,1,0:T(8,128)S(1)}) custom-call(s32[4]{0:T(128)S(1)} %pad_add_fusion.1.place_ref, bf16[2,256,1920]{2,1,0:T(8,128)(2,1)} %bitcast.413, bf16[1,2,256,1024]{3,2,1,0:T(8,128)(2,1)S(1)} %bitcast.369, bf16[1,2,256,1024]{3,2,1,0:T(8,128)(2,1)S(1)} %collective-permute-done.1.refs_1_.refs_4_, ...), custom_call_target="tpu_custom_call" | custom-call | flops 1 | bytes 1638400 | tf_op jit(solution)/shard_map/attend/pallas_call | solution.py:1129
  589.3 14.6 multiply_reduce_fusion.14
  607.0 17.0 %fusion.219 = f32[512,5504]{1,0:T(8,128)} fusion(bf16[512,1600]{0,1:T(8,128)(2,1)S(1)} %multiply_convert_fusion.9, bf16[1600,5504]{1,0:T(8,128)(2,1)} %bitcast.468), kind=kOutput, calls=%fused_computation.443 | convolution fusion | flops 9017753600 | bytes 30523392 | tf_op jit(solution)/shard_map/dot_general | solution.py:1224
  624.0 23.7 %fusion = (bf16[5504,512]{0,1:T(8,128)(2,1)}, f32[512,5504]{1,0:T(8,128)}) fusion(f32[512,5504]{1,0:T(8,128)} %fusion.219, bf16[512,1600]{0,1:T(8,128)(2,1)} %copy-done.39, bf16[1600,5504]{1,0:T(8,128)(2,1)} %bitcast.470), kind=kOutput, calls=%fused_computation.6 | convolution fusion | flops 9034661888 | bytes 47431680 | tf_op jit(solution)/shard_map/dot_general | solution.py:1224
  652.7 15.9 assemble.5
  668.6 24.8 %fusion.204 = (bf16[512,1600]{0,1:T(8,128)(2,1)}, f32[512,1600]{0,1:T(8,128)}, f32[]{:T(128)}, bf16[512,1600]{0,1:T(8,128)(2,1)}) fusion(f32[512,1600]{0,1:T(8,128)} %bitcast.428, f32[512,1600]{0,1:T(8,128)} %bitcast.429, f32[512]{0:T(512)S(1)} %broadcast_multiply_fusion.7, f32[512]{0:T(512)S(1)} %bitcast.460, f32[512,1600]{0,1:T(8,128)} %copy-done.30, ...), kind=kOutput, calls=%fused_computation.430 | convolution fusion | flops 9042034688 | bytes 56545284 | tf_op jit(solution)/shard_map/dot_general | solution.py:1224
  693.3 23.8 %multiply_convert_fusion = (bf16[512,5504]{1,0:T(8,128)(2,1)}, bf16[512,5504]{1,0:T(8,128)(2,1)}) fusion(f32[512,5504]{1,0:T(8,128)} %fusion.219, f32[512,5504]{1,0:T(8,128)} %get-tuple-element.497, bf16[512,1600]{0,1:T(8,128)(2,1)} %get-tuple-element.389, bf16[5504,1600]{1,0:T(8,128)(2,1)} %bitcast.397), kind=kOutput, calls=%fused_computation.12 | convolution fusion | flops 9054388224 | bytes 53067776 | tf_op jit(solution)/shard_map/dot_general | solution.py:1228
  742.9 11.7 convolution_convert_fusion.2
  763.4 14.4 fusion.220
  783.5 20.6 %multiply_reduce_fusion.11 = (f32[1600]{0:T(1024)S(1)}, f32[512]{0:T(512)S(1)}, f32[512,1600]{0,1:T(8,128)}) fusion(f32[512,1600]{0,1:T(8,128)} %copy-done.30, f32[512]{0:T(512)S(1)} %copy-done.155, f32[1600]{0:T(1024)S(1)} %copy-done.146, f32[512,1600]{0,1:T(8,128)} %fusion.220, bf16[512,5504]{1,0:T(8,128)(2,1)} %get-tuple-element.201, ...), kind=kOutput, calls=%fused_computation.77 | convolution fusion | flops 9023485952 | bytes 33096192 | tf_op jit(solution)/shard_map/dot_general | solution.py:1228
  872.7 24.5 %collective-permute-done.20 = bf16[1376,768]{1,0:T(8,128)(2,1)} collective-permute-done((bf16[1376,768]{1,0:T(8,128)(2,1)}, bf16[1376,768]{1,0:T(8,128)(2,1)}, u32[]{:S(2)}, u32[]{:S(2)}) %collective-permute-start.20) | collective-permute-done | bytes 2113568 | tf_op jit(solution)/shard_map/ppermute | solution.py:34
  900.6 18.7 %multiply_reduce_fusion = (f32[3200]{0:T(1024)S(1)}, f32[512]{0:T(512)S(1)}, f32[512]{0:T(512)S(1)}, f32[3200]{0:T(1024)S(1)}, f32[512,3200]{1,0:T(8,128)}) fusion(f32[2,256,3200]{2,1,0:T(8,128)} %get-tuple-element.392, f32[512]{0:T(512)S(1)} %bitcast.457, f32[3200]{0:T(1024)S(1)} %copy-done.147, f32[512,3200]{1,0:T(8,128)} %bitcast.379, ...), kind=kOutput, calls=%fused_computation.30 | convolution fusion | flops 5264172032 | bytes 31598592 | tf_op jit(solution)/shard_map/dot_general | solution.py:1228
  983.1 23.5 %scan_adjoint.1 = f32[2,16,3200]{2,1,0:T(8,128)} custom-call(f32[2,256,3200]{2,1,0:T(8,128)} %bitcast.377, f32[2,256,3200]{2,1,0:T(8,128)} %get-tuple-element.235.gy_ref, f32[2,256,16,128]{3,2,1,0:T(8,128)} %broadcast_in_dim.152.c_ref, f32[16,3200]{1,0:T(8,128)} %broadcast_multiply_fusion.4.dec_ref), custom_call_target="tpu_custom_call" | custom-call | flops 6 | bytes 1638400 | tf_op jit(solution)/shard_map/scan_adjoint/pallas_call | solution.py:971
  1060.8 43.0 %attend_back.1 = (bf16[2,256,1920]{2,1,0:T(8,128)(2,1)}, bf16[2,1024,384]{2,1,0:T(8,128)(2,1)}, bf16[2,1024,640]{2,1,0:T(8,128)(2,1)}) custom-call(s32[4]{0:T(128)S(1)} %pad_add_fusion.1.place_ref, bf16[2,256,1920]{2,1,0:T(8,128)(2,1)} %bitcast.414, bf16[1,2,256,1024]{3,2,1,0:T(8,128)(2,1)S(1)} %bitcast.371, ...), custom_call_target="tpu_custom_call" | custom-call | flops 1 | bytes 1638400 | tf_op jit(solution)/shard_map/attend_back/pallas_call | solution.py:1189
  1193.7 101.6 %scan_back.1 = (f32[2,256,3200]{2,1,0:T(8,128)}, f32[2,256,3200]{2,1,0:T(8,128)}, f32[2,256,16,128]{3,2,1,0:T(8,128)}, f32[2,256,16,128]{3,2,1,0:T(8,128)}, f32[2,16,3200]{2,1,0:T(8,128)}) custom-call(f32[2,256,3200]{2,1,0:T(8,128)} %bitcast.378, f32[2,256,3200]{2,1,0:T(8,128)} %get-tuple-element.394.xc_ref, f32[2,256,3200]{2,1,0:T(8,128)} %get-tuple-element.235.gy_ref, ...), custom_call_target="tpu_custom_call" | custom-call | flops 24 | bytes 1638400 | tf_op jit(solution)/shard_map/scan_back/pallas_call | solution.py:1043
  1328.3 23.2 %multiply_reduce_fusion.3 = (f32[3200]{0:T(1024)}, f32[3200]{0:T(1024)}, f32[3200]{0:T(1024)}, f32[3200]{0:T(1024)}, f32[3200]{0:T(1024)}, /*index=5*/f32[2,256,3200]{2,1,0:T(8,128)}) fusion(f32[2,259,3200]{2,1,0:T(8,128)} %copy-done.18, f32[2,256,3200]{2,1,0:T(8,128)} %get-tuple-element.395, f32[2,256,3200]{2,1,0:T(8,128)} %fusion.139, ...), kind=kLoop, calls=%fused_computation.33 | loop fusion | flops 32752000 | bytes 59059200 | tf_op jit(solution)/shard_map/reduce_sum | solution.py:1521
  1428.7 11.9 multiply_reduce_fusion.10
  1449.9 211.7 %reduce_gradients.1 = (f32[200,400]{1,0:T(8,128)}, f32[200,80]{1,0:T(8,128)}, f32[200,160]{1,0:T(8,128)}, f32[200,1600]{1,0:T(8,128)}, f32[288,512]{1,0:T(8,128)...) custom-call(bf16[8,200,3200]{2,1,0:T(8,128)(2,1)} %bitcast.407, bf16[8,200,3200]{2,1,0:T(8,128)(2,1)} %bitcast.406, ...), custom_call_target="tpu_custom_call" | custom-call | flops 1 | bytes 1 | tf_op jit(solution)/shard_map/reduce_gradients/pallas_call | solution.py:774
  (739 shorter events, 707.8 us)
Async XLA Ops:
  205.0 97.9 %collective-permute-start.2 = (bf16[200,11008]{1,0:T(8,128)(2,1)}, bf16[200,11008]{1,0:T(8,128)(2,1)}, u32[]{:S(2)}, u32[]{:S(2)}) collective-permute-start(bf16[200,11008]{1,0:T(8,128)(2,1)} %get-tuple-element.176.refs_0_), channel_id=1, source_target_pairs={{0,8},{4,12},{8,0},{12,4},{16,24},{20,28},{24,16},{28,20},{1,9},{5... | collective-permute-start | bytes 13209608 | tf_op jit(solution)/shard_map/ppermute | solution.py:34
  205.7 98.2 %collective-permute-start.3 = (bf16[200,11008]{1,0:T(8,128)(2,1)}, bf16[200,11008]{1,0:T(8,128)(2,1)}, u32[]{:S(2)}, u32[]{:S(2)}) collective-permute-start(bf16[200,11008]{1,0:T(8,128)(2,1)} %get-tuple-element.176.refs_0_), channel_id=1, source_target_pairs={{0,16},{4,20},{8,24},{12,28},{16,0},{20,4},{24,8},{28,12},{1,17},{... | collective-permute-start | bytes 13209608 | tf_op jit(solution)/shard_map/ppermute | solution.py:34
  232.4 205.0 %collective-permute-start.10 = (bf16[400,1600]{1,0:T(8,128)(2,1)}, bf16[400,1600]{1,0:T(8,128)(2,1)S(1)}, u32[]{:S(2)}, u32[]{:S(2)}) collective-permute-start(bf16[400,1600]{1,0:T(8,128)(2,1)} %get-tuple-element.193.refs_0_), channel_id=1, source_target_pairs={{0,16},{4,20},{8,24},{12,28},{16,0},{20,4},{24,8},{28,12},{1,17},{... | collective-permute-start | bytes 3840008 | tf_op jit(solution)/shard_map/ppermute | solution.py:34
  233.0 137.8 %collective-permute-start.11 = (bf16[1,688,400]{1,2,0:T(8,128)(2,1)}, bf16[1,688,400]{1,2,0:T(8,128)(2,1)}, u32[]{:S(2)}, u32[]{:S(2)}) collective-permute-start(bf16[1,688,400]{1,2,0:T(8,128)(2,1)} %bitcast.15), channel_id=1, source_target_pairs={{0,2},{1,3},{2,0},{3,1},{4,6},{5,7},{6,4},{7,5},{8,10},{9,11},{10,... | collective-permute-start | bytes 1651208 | tf_op jit(solution)/shard_map/ppermute | solution.py:34
  370.8 66.6 %collective-permute-start.9 = (bf16[400,1600]{1,0:T(8,128)(2,1)}, bf16[400,1600]{1,0:T(8,128)(2,1)}, u32[]{:S(2)}, u32[]{:S(2)}) collective-permute-start(bf16[400,1600]{1,0:T(8,128)(2,1)} %get-tuple-element.193.refs_0_), channel_id=1, source_target_pairs={{0,8},{4,12},{8,0},{12,4},{16,24},{20,28},{24,16},{28,20},{1,9},{5... | collective-permute-start | bytes 3840008 | tf_op jit(solution)/shard_map/ppermute | solution.py:34
  407.8 101.5 %collective-permute-start.4 = (bf16[2,2,256,1024]{3,2,1,0:T(8,128)(2,1)}, bf16[2,2,256,1024]{3,2,1,0:T(8,128)(2,1)}, u32[]{:S(2)}, u32[]{:S(2)}) collective-permute-start(bf16[2,2,256,1024]{3,2,1,0:T(8,128)(2,1)} %pad_maximum_fusion.1), channel_id=1, source_target_pairs={{0,1},{1,0},{2,3},{3,2},{4,5},{5,4},{6,7},{7,6},{8,9},{9,8},{10,11... | collective-permute-start | bytes 6291464 | tf_op jit(solution)/shard_map/ppermute | solution.py:34
  449.9 67.8 %collective-permute-start.15 = (bf16[688,1600]{1,0:T(8,128)(2,1)}, bf16[688,1600]{1,0:T(8,128)(2,1)S(1)}, u32[]{:S(2)}, u32[]{:S(2)}) collective-permute-start(bf16[688,1600]{1,0:T(8,128)(2,1)} %concatenate.115.refs_0_), channel_id=1, source_target_pairs={{0,8},{4,12},{8,0},{12,4},{16,24},{20,28},{24,16},{28,20},{1,9},{5... | collective-permute-start | bytes 6604808 | tf_op jit(solution)/shard_map/ppermute | solution.py:34
  452.0 65.7 %collective-permute-start.16 = (bf16[688,1600]{1,0:T(8,128)(2,1)}, bf16[688,1600]{1,0:T(8,128)(2,1)S(1)}, u32[]{:S(2)}, u32[]{:S(2)}) collective-permute-start(bf16[688,1600]{1,0:T(8,128)(2,1)} %concatenate.115.refs_0_), channel_id=1, source_target_pairs={{0,16},{4,20},{8,24},{12,28},{16,0},{20,4},{24,8},{28,12},{1,17},{... | collective-permute-start | bytes 6604808 | tf_op jit(solution)/shard_map/ppermute | solution.py:34
  730.2 142.5 %collective-permute-start.23 = (bf16[800,5504]{1,0:T(8,128)(2,1)}, bf16[800,5504]{1,0:T(8,128)(2,1)}, u32[]{:S(2)}, u32[]{:S(2)}) collective-permute-start(bf16[800,5504]{1,0:T(8,128)(2,1)} %convolution_convert_fusion.3), channel_id=1, source_target_pairs={{0,4},{4,0},{8,12},{12,8},{16,20},{20,16},{24,28},{28,24},{1,5},{5... | collective-permute-start | bytes 26419208 | tf_op jit(solution)/shard_map/ppermute | solution.py:34
  754.6 73.0 %collective-permute-start.19 = (bf16[2752,1600]{0,1:T(8,128)(2,1)}, bf16[2752,1600]{0,1:T(8,128)(2,1)}, u32[]{:S(2)}, u32[]{:S(2)}) collective-permute-start(bf16[2752,1600]{0,1:T(8,128)(2,1)} %convolution_convert_fusion.2), channel_id=1, source_target_pairs={{0,4},{4,0},{8,12},{12,8},{16,20},{20,16},{24,28},{28,24},{1,5},{5... | collective-permute-start | bytes 26419208 | tf_op jit(solution)/shard_map/ppermute | solution.py:34
  763.0 109.7 %collective-permute-start.22 = (bf16[800,5504]{1,0:T(8,128)(2,1)}, bf16[800,5504]{1,0:T(8,128)(2,1)}, u32[]{:S(2)}, u32[]{:S(2)}) collective-permute-start(bf16[800,5504]{1,0:T(8,128)(2,1)} %convolution_convert_fusion.4), channel_id=1, source_target_pairs={{0,4},{4,0},{8,12},{12,8},{16,20},{20,16},{24,28},{28,24},{1,5},{5... | collective-permute-start | bytes 26419208 | tf_op jit(solution)/shard_map/ppermute | solution.py:34
  926.5 90.5 %collective-permute-start.28 = (bf16[1600,1600]{1,0:T(8,128)(2,1)}, bf16[1600,1600]{1,0:T(8,128)(2,1)}, u32[]{:S(2)}, u32[]{:S(2)}) collective-permute-start(bf16[1600,1600]{1,0:T(8,128)(2,1)} %convolution_convert_fusion.5), channel_id=1, source_target_pairs={{0,4},{4,0},{8,12},{12,8},{16,20},{20,16},{24,28},{28,24},{1,5},{5... | collective-permute-start | bytes 15360008 | tf_op jit(solution)/shard_map/ppermute | solution.py:34
  933.6 83.3 %collective-permute-start.27 = (bf16[400,2816]{1,0:T(8,128)(2,1)}, bf16[400,2816]{1,0:T(8,128)(2,1)}, u32[]{:S(2)}, u32[]{:S(2)}) collective-permute-start(bf16[400,2816]{1,0:T(8,128)(2,1)} %add_convert_fusion.2), channel_id=1, source_target_pairs={{0,16},{4,20},{8,24},{12,28},{16,0},{20,4},{24,8},{28,12},{1,17},{... | collective-permute-start | bytes 6758408 | tf_op jit(solution)/shard_map/ppermute | solution.py:34
  938.4 78.5 %collective-permute-start.26 = (bf16[400,2688]{1,0:T(8,128)(2,1)}, bf16[400,2688]{1,0:T(8,128)(2,1)}, u32[]{:S(2)}, u32[]{:S(2)}) collective-permute-start(bf16[400,2688]{1,0:T(8,128)(2,1)} %fusion.11), channel_id=1, source_target_pairs={{0,8},{4,12},{8,0},{12,4},{16,24},{20,28},{24,16},{28,20},{1,9},{5... | collective-permute-start | bytes 6451208 | tf_op jit(solution)/shard_map/ppermute | solution.py:34
  945.8 70.5 %collective-permute-start.25 = (bf16[688,832]{1,0:T(8,128)(2,1)S(1)}, bf16[688,832]{1,0:T(8,128)(2,1)S(1)}, u32[]{:S(2)}, u32[]{:S(2)}) collective-permute-start(bf16[688,832]{1,0:T(8,128)(2,1)S(1)} %add_convert_fusion.7), channel_id=1, source_target_pairs={{0,8},{4,12},{8,0},{12,4},{16,24},{20,28},{24,16},{28,20},{1,9},{5... | collective-permute-start | bytes 3434504 | tf_op jit(solution)/shard_map/ppermute | solution.py:34
  949.9 66.1 %collective-permute-start.24 = (bf16[688,768]{1,0:T(8,128)(2,1)}, bf16[688,768]{1,0:T(8,128)(2,1)}, u32[]{:S(2)}, u32[]{:S(2)}) collective-permute-start(bf16[688,768]{1,0:T(8,128)(2,1)} %add_convert_fusion.18), channel_id=1, source_target_pairs={{0,16},{4,20},{8,24},{12,28},{16,0},{20,4},{24,8},{28,12},{1,17},{... | collective-permute-start | bytes 3170312 | tf_op jit(solution)/shard_map/ppermute | solution.py:34
  1016.0 100.9 %collective-permute-start.33 = (bf16[400,2816]{1,0:T(8,128)(2,1)}, bf16[400,2816]{1,0:T(8,128)(2,1)}, u32[]{:S(2)}, u32[]{:S(2)}) collective-permute-start(bf16[400,2816]{1,0:T(8,128)(2,1)} %add_convert_fusion.1), channel_id=1, source_target_pairs={{0,16},{4,20},{8,24},{12,28},{16,0},{20,4},{24,8},{28,12},{1,17},{... | collective-permute-start | bytes 6758408 | tf_op jit(solution)/shard_map/ppermute | solution.py:34
  1016.3 100.1 %collective-permute-start.32 = (bf16[400,2688]{1,0:T(8,128)(2,1)}, bf16[400,2688]{1,0:T(8,128)(2,1)}, u32[]{:S(2)}, u32[]{:S(2)}) collective-permute-start(bf16[400,2688]{1,0:T(8,128)(2,1)} %fusion.12), channel_id=1, source_target_pairs={{0,8},{4,12},{8,0},{12,4},{16,24},{20,28},{24,16},{28,20},{1,9},{5... | collective-permute-start | bytes 6451208 | tf_op jit(solution)/shard_map/ppermute | solution.py:34
  1021.3 99.9 %collective-permute-start.31 = (bf16[200,2816]{1,0:T(8,128)(2,1)}, bf16[200,2816]{1,0:T(8,128)(2,1)}, u32[]{:S(2)}, u32[]{:S(2)}) collective-permute-start(bf16[200,2816]{1,0:T(8,128)(2,1)} %add_convert_fusion.12), channel_id=1, source_target_pairs={{0,8},{4,12},{8,0},{12,4},{16,24},{20,28},{24,16},{28,20},{1,9},{5... | collective-permute-start | bytes 3379208 | tf_op jit(solution)/shard_map/ppermute | solution.py:34
  1032.5 78.1 %collective-permute-start.29 = (bf16[2,688,400]{1,2,0:T(8,128)(2,1)S(1)}, bf16[2,688,400]{1,2,0:T(8,128)(2,1)S(1)}, u32[]{:S(2)}, u32[]{:S(2)}) collective-permute-start(bf16[2,688,400]{1,2,0:T(8,128)(2,1)S(1)} %copy.143), channel_id=1, source_target_pairs={{0,1},{1,0},{2,3},{3,2},{4,5},{5,4},{6,7},{7,6},{8,9},{9,8},{10,11... | collective-permute-start | bytes 3302408 | tf_op jit(solution)/shard_map/ppermute | solution.py:34
  1168.1 137.3 %collective-permute-start.44 = (bf16[2,2,256,1024]{3,2,1,0:T(8,128)(2,1)}, bf16[2,2,256,1024]{3,2,1,0:T(8,128)(2,1)}, u32[]{:S(2)}, u32[]{:S(2)}) collective-permute-start(bf16[2,2,256,1024]{3,2,1,0:T(8,128)(2,1)} %pad_maximum_fusion.2), channel_id=1, source_target_pairs={{0,1},{1,0},{2,3},{3,2},{4,5},{5,4},{6,7},{7,6},{8,9},{9,8},{10,11... | collective-permute-start | bytes 6291464 | tf_op jit(solution)/shard_map/ppermute | solution.py:34
  1181.1 127.1 %collective-permute-start.43 = (bf16[400,832]{1,0:T(8,128)(2,1)}, bf16[400,832]{1,0:T(8,128)(2,1)}, u32[]{:S(2)}, u32[]{:S(2)}) collective-permute-start(bf16[400,832]{1,0:T(8,128)(2,1)} %add_convert_fusion.22), channel_id=1, source_target_pairs={{0,8},{4,12},{8,0},{12,4},{16,24},{20,28},{24,16},{28,20},{1,9},{5... | collective-permute-start | bytes 1996808 | tf_op jit(solution)/shard_map/ppermute | solution.py:34
  1184.4 123.7 %collective-permute-start.42 = (bf16[400,768]{1,0:T(8,128)(2,1)}, bf16[400,768]{1,0:T(8,128)(2,1)}, u32[]{:S(2)}, u32[]{:S(2)}) collective-permute-start(bf16[400,768]{1,0:T(8,128)(2,1)} %add_convert_fusion.25), channel_id=1, source_target_pairs={{0,16},{4,20},{8,24},{12,28},{16,0},{20,4},{24,8},{28,12},{1,17},{... | collective-permute-start | bytes 1843208 | tf_op jit(solution)/shard_map/ppermute | solution.py:34
  1187.1 116.2 %collective-permute-start.40 = (bf16[1,688,400]{1,2,0:T(8,128)(2,1)}, bf16[1,688,400]{1,2,0:T(8,128)(2,1)}, u32[]{:S(2)}, u32[]{:S(2)}) collective-permute-start(bf16[1,688,400]{1,2,0:T(8,128)(2,1)} %copy.146), channel_id=1, source_target_pairs={{0,2},{1,3},{2,0},{3,1},{4,6},{5,7},{6,4},{7,5},{8,10},{9,11},{10,... | collective-permute-start | bytes 1651208 | tf_op jit(solution)/shard_map/ppermute | solution.py:34
  (209 other events, 4056.8 us)
